TPU v7x, 32 devices: a whole 2x2x4 slice. The times are simulated.
32 devices in a mesh: rep: 8 (over z, y), shard: 4 (over x, core).
Axes of the slice: x: 2, y: 2, z: 4, core: 2. Of those that a mesh axis runs over, the one named last changes fastest.
Arguments:
- inputs: bfloat16 [65536, 768], P(('rep', 'shard')), may hold values from -6 to 6
- earlier: bfloat16 [4, 65536, 768], P(None, ('rep', 'shard')), may hold values from -6 to 6
- segments: int32 [64, 1024], P(('rep', 'shard')), may hold values from 0 to 31, never falling along the last dimension, each value on 1 to 512 neighbouring positions
- cotangent: bfloat16 [65536, 768], P(('rep', 'shard')), may hold values from -6 to 6
- mix_weights: float32 [5], replicated, may hold values from 0.2 to 1
- ln1_gain: bfloat16 [768], P('shard'), may hold values from 0.25 to 1.75
- ln1_bias: bfloat16 [768], P('shard'), may hold values from -1.75 to 1.75
- qkv_weight: bfloat16 [768, 2304], P('shard'), may hold values from -0.21875 to 0.21875
- qkv_bias: bfloat16 [2304], P('shard'), may hold values from -1.75 to 1.75
- out_weight: bfloat16 [768, 768], P('shard'), may hold values from -0.875 to 0.875
- out_bias: bfloat16 [768], P('shard'), may hold values from -1.75 to 1.75
- ln2_gain: bfloat16 [768], P('shard'), may hold values from 0.25 to 1.75
- ln2_bias: bfloat16 [768], P('shard'), may hold values from -1.75 to 1.75
- up_weight: bfloat16 [768, 3072], P('shard'), may hold values from -0.21875 to 0.21875
- up_bias: bfloat16 [3072], P('shard'), may hold values from -1.75 to 1.75
- down_weight: bfloat16 [3072, 768], P('shard'), may hold values from -0.109375 to 0.109375
- down_bias: bfloat16 [768], P('shard'), may hold values from -1.75 to 1.75
Outputs:
- output: bfloat16 [65536, 768], P(('rep', 'shard'))
- input_grad: float32 [65536, 768], P(('rep', 'shard'))
- earlier_grad: float32 [4, 65536, 768], P(None, ('rep', 'shard'))
- mix_grad: float32 [5], replicated
- grad_ln1_gain: float32 [768], P('shard')
- grad_ln1_bias: float32 [768], P('shard')
- grad_qkv_weight: float32 [768, 2304], P('shard')
- grad_qkv_bias: float32 [2304], P('shard')
- grad_out_weight: float32 [768, 768], P('shard')
- grad_out_bias: float32 [768], P('shard')
- grad_ln2_gain: float32 [768], P('shard')
- grad_ln2_bias: float32 [768], P('shard')
- grad_up_weight: float32 [768, 3072], P('shard')
- grad_up_bias: float32 [3072], P('shard')
- grad_down_weight: float32 [3072, 768], P('shard')
- grad_down_bias: float32 [768], P('shard')
Inputs may be any that keep to these rules, and one draw needn't show every extreme that they name: `segments`: document numbers never fall along a sequence; each of the 32 documents of a sequence holds 1 to 512 tokens, and one of them exactly 512.
All inputs are finite; a program needn't handle non-finite values.
Results may differ from a plain program's by a relative error of at most 0.0092.
Values may be sent and summed in bfloat16 or wider, within the bound.
No kernel may reach another device: no remote copies, remote signals or barrier semaphores. Data moves between devices by JAX's collectives and lax.ppermute only.
A program may use at most 384 MiB of HBM per device.

v0:
```python
import math

import jax
import jax.numpy as jnp
from jax import lax
from jax.sharding import PartitionSpec as P

HEADS = 12
HEAD = 64


epsilon = 1e-05


def rope_tables(length, half_size):
    inv_freq = jnp.exp(jnp.arange(half_size, dtype=jnp.float32) * (-math.log(10000.0) / half_size))
    angles = jnp.arange(length, dtype=jnp.float32)[:, None] * inv_freq[None, :]
    return (jnp.cos(angles), jnp.sin(angles))


def rotate(tensor, cosine_table, sine_table):
    half_size = tensor.shape[-1] // 2
    first_half = tensor[..., :half_size]
    second_half = tensor[..., half_size:]
    cos_part = cosine_table[:, None, :]
    sin_part = sine_table[:, None, :]
    return jnp.concatenate(
        [
            first_half * cos_part - second_half * sin_part,
            second_half * cos_part + first_half * sin_part,
        ],
        axis=-1,
    )


def layer_norm(values, gain, bias):
    row_mean = jnp.mean(values, axis=-1, keepdims=True)
    centred = values - row_mean
    row_var = jnp.mean(centred * centred, axis=-1, keepdims=True)
    return centred * lax.rsqrt(row_var + epsilon) * gain + bias


def outer_sum(left, right):
    return lax.dot_general(
        left, right, (((0,), (0,)), ((), ())), preferred_element_type=jnp.float32
    )


def back_prod(grad_low, weight):
    return lax.dot_general(
        grad_low, weight, (((1,), (1,)), ((), ())), preferred_element_type=jnp.float32
    )


def gelu_tanh(values):
    return jax.nn.gelu(values, approximate=True)


def run_micro(params, block_in, state_rows, doc_ids, cot_rows, mix_alpha):
    (
        gain_one,
        bias_one,
        w_qkv,
        b_qkv,
        w_out,
        b_out,
        gain_two,
        bias_two,
        w_up,
        b_up,
        w_down,
        b_down,
    ) = params
    length, model_width = block_in.shape
    head_count = HEADS
    head_size = HEAD
    score_scale = head_size ** (-0.5)
    cosine_table, sine_table = rope_tables(length, head_size // 2)
    positions = jnp.arange(length)
    allowed = (positions[:, None] >= positions[None, :]) & (doc_ids[:, None] == doc_ids[None, :])
    residual = block_in.astype(jnp.float32)
    normed_one, norm_pull_one = jax.vjp(
        layer_norm, residual, gain_one.astype(jnp.float32), bias_one.astype(jnp.float32)
    )
    act_one = normed_one.astype(jnp.bfloat16)
    qkv_rows = jnp.dot(act_one, w_qkv, preferred_element_type=jnp.float32) + b_qkv.astype(
        jnp.float32
    )
    qkv_rows = qkv_rows.reshape(length, 3, head_count, head_size)
    rotated, rope_pull = jax.vjp(
        lambda query_in, key_in: (
            rotate(query_in, cosine_table, sine_table),
            rotate(key_in, cosine_table, sine_table),
        ),
        qkv_rows[:, 0],
        qkv_rows[:, 1],
    )
    queries = rotated[0].astype(jnp.bfloat16)
    key_rows = rotated[1].astype(jnp.bfloat16)
    value_rows = qkv_rows[:, 2].astype(jnp.bfloat16)

    def masked_scores():
        raw_scores = jnp.einsum(
            "qhd,khd->hqk", queries, key_rows, preferred_element_type=jnp.float32
        )
        return jnp.where(allowed[None], raw_scores * score_scale, -1e30)

    scores = masked_scores()
    row_max = jnp.max(scores, axis=-1, keepdims=True)
    exponent = jnp.exp(scores - row_max)
    row_total = jnp.sum(exponent, axis=-1, keepdims=True)
    log_total = row_max + jnp.log(row_total)
    probs_low = (exponent / row_total).astype(jnp.bfloat16)
    attended = (
        jnp.einsum("hqk,khd->qhd", probs_low, value_rows, preferred_element_type=jnp.float32)
        .reshape(length, model_width)
        .astype(jnp.bfloat16)
    )
    hidden_one = (
        residual
        + jnp.dot(attended, w_out, preferred_element_type=jnp.float32)
        + b_out.astype(jnp.float32)
    )
    normed_two, norm_pull_two = jax.vjp(
        layer_norm, hidden_one, gain_two.astype(jnp.float32), bias_two.astype(jnp.float32)
    )
    act_two = normed_two.astype(jnp.bfloat16)
    pre_act = jnp.dot(act_two, w_up, preferred_element_type=jnp.float32) + b_up.astype(jnp.float32)
    activated, gelu_pull = jax.vjp(gelu_tanh, pre_act)
    act_three = activated.astype(jnp.bfloat16)
    block_out = (
        hidden_one
        + jnp.dot(act_three, w_down, preferred_element_type=jnp.float32)
        + b_down.astype(jnp.float32)
    )
    states = state_rows.astype(jnp.float32)
    mixed_rows = (
        mix_alpha[0] * states[0]
        + mix_alpha[1] * states[1]
        + mix_alpha[2] * states[2]
        + mix_alpha[3] * states[3]
        + mix_alpha[4] * block_out
    )
    output = mixed_rows.astype(jnp.bfloat16)
    cot_full = cot_rows.astype(jnp.float32)
    earlier_part = mix_alpha[:4, None, None] * cot_full[None]
    alpha_part = jnp.concatenate(
        [jnp.sum(states * cot_full[None], axis=(1, 2)), jnp.sum(block_out * cot_full)[None]]
    )
    grad_out = mix_alpha[4] * cot_full
    grad_b_down = jnp.sum(grad_out, axis=0)
    grad_out_low = grad_out.astype(jnp.bfloat16)
    grad_w_down = outer_sum(act_three, grad_out_low)
    grad_act = back_prod(grad_out_low, w_down)
    (grad_pre,) = gelu_pull(grad_act)
    grad_b_up = jnp.sum(grad_pre, axis=0)
    grad_pre_low = grad_pre.astype(jnp.bfloat16)
    grad_w_up = outer_sum(act_two, grad_pre_low)
    grad_norm_two = back_prod(grad_pre_low, w_up)
    hidden_part, grad_gain_two, grad_bias_two = norm_pull_two(grad_norm_two)
    grad_hidden = grad_out + hidden_part
    grad_b_out = jnp.sum(grad_hidden, axis=0)
    grad_hidden_low = grad_hidden.astype(jnp.bfloat16)
    grad_w_out = outer_sum(attended, grad_hidden_low)
    grad_att = (
        back_prod(grad_hidden_low, w_out)
        .astype(jnp.bfloat16)
        .reshape(length, head_count, head_size)
    )
    attn_probs = jnp.exp(masked_scores() - log_total)
    again_low = attn_probs.astype(jnp.bfloat16)
    grad_probs = jnp.einsum(
        "qhd,khd->hqk", grad_att, value_rows, preferred_element_type=jnp.float32
    )
    row_delta = jnp.sum(attn_probs * grad_probs, axis=-1, keepdims=True)
    grad_scores = (attn_probs * (grad_probs - row_delta) * score_scale).astype(jnp.bfloat16)
    grad_query = jnp.einsum(
        "hqk,khd->qhd", grad_scores, key_rows, preferred_element_type=jnp.float32
    )
    grad_key = jnp.einsum("hqk,qhd->khd", grad_scores, queries, preferred_element_type=jnp.float32)
    grad_value = jnp.einsum("hqk,qhd->khd", again_low, grad_att, preferred_element_type=jnp.float32)
    grad_query_raw, grad_key_raw = rope_pull((grad_query, grad_key))
    grad_qkv = jnp.stack([grad_query_raw, grad_key_raw, grad_value], axis=1).reshape(
        length, 3 * model_width
    )
    grad_b_qkv = jnp.sum(grad_qkv, axis=0)
    grad_qkv_low = grad_qkv.astype(jnp.bfloat16)
    grad_w_qkv = outer_sum(act_one, grad_qkv_low)
    grad_norm_one = back_prod(grad_qkv_low, w_qkv)
    input_part, grad_gain_one, grad_bias_one = norm_pull_one(grad_norm_one)
    grad_input = grad_hidden + input_part
    grads = (
        grad_gain_one,
        grad_bias_one,
        grad_w_qkv,
        grad_b_qkv,
        grad_w_out,
        grad_b_out,
        grad_gain_two,
        grad_bias_two,
        grad_w_up,
        grad_b_up,
        grad_w_down,
        grad_b_down,
    )
    return (output, grad_input, earlier_part, alpha_part, grads)


def shards(
    inputs,
    earlier,
    segments,
    cotangent,
    mix_weights,
    ln1_gain,
    ln1_bias,
    qkv_weight,
    qkv_bias,
    out_weight,
    out_bias,
    ln2_gain,
    ln2_bias,
    up_weight,
    up_bias,
    down_weight,
    down_bias,
):
    micro_count, length = segments.shape
    outputs_list = []
    input_list = []
    earlier_list = []
    alpha_total = jnp.zeros((5,), jnp.float32)
    shard_total = None
    for index in range(micro_count):
        full_params = (
            lax.all_gather(ln1_gain, "shard", axis=0, tiled=True),
            lax.all_gather(ln1_bias, "shard", axis=0, tiled=True),
            lax.all_gather(qkv_weight, "shard", axis=0, tiled=True),
            lax.all_gather(qkv_bias, "shard", axis=0, tiled=True),
            lax.all_gather(out_weight, "shard", axis=0, tiled=True),
            lax.all_gather(out_bias, "shard", axis=0, tiled=True),
            lax.all_gather(ln2_gain, "shard", axis=0, tiled=True),
            lax.all_gather(ln2_bias, "shard", axis=0, tiled=True),
            lax.all_gather(up_weight, "shard", axis=0, tiled=True),
            lax.all_gather(up_bias, "shard", axis=0, tiled=True),
            lax.all_gather(down_weight, "shard", axis=0, tiled=True),
            lax.all_gather(down_bias, "shard", axis=0, tiled=True),
        )
        row_slice = slice(index * length, (index + 1) * length)
        output, grad_input, earlier_part, alpha_part, grads = run_micro(
            full_params,
            inputs[row_slice],
            earlier[:, row_slice],
            segments[index],
            cotangent[row_slice],
            mix_weights,
        )
        outputs_list.append(output)
        input_list.append(grad_input)
        earlier_list.append(earlier_part)
        alpha_total = alpha_total + alpha_part
        reduced = (
            lax.psum_scatter(grads[0], "shard", scatter_dimension=0, tiled=True),
            lax.psum_scatter(grads[1], "shard", scatter_dimension=0, tiled=True),
            lax.psum_scatter(grads[2], "shard", scatter_dimension=0, tiled=True),
            lax.psum_scatter(grads[3], "shard", scatter_dimension=0, tiled=True),
            lax.psum_scatter(grads[4], "shard", scatter_dimension=0, tiled=True),
            lax.psum_scatter(grads[5], "shard", scatter_dimension=0, tiled=True),
            lax.psum_scatter(grads[6], "shard", scatter_dimension=0, tiled=True),
            lax.psum_scatter(grads[7], "shard", scatter_dimension=0, tiled=True),
            lax.psum_scatter(grads[8], "shard", scatter_dimension=0, tiled=True),
            lax.psum_scatter(grads[9], "shard", scatter_dimension=0, tiled=True),
            lax.psum_scatter(grads[10], "shard", scatter_dimension=0, tiled=True),
            lax.psum_scatter(grads[11], "shard", scatter_dimension=0, tiled=True),
        )
        shard_total = (
            reduced
            if shard_total is None
            else tuple((running + added for running, added in zip(shard_total, reduced)))
        )
    summed = lax.psum(
        (
            shard_total[0],
            shard_total[1],
            shard_total[2],
            shard_total[3],
            shard_total[4],
            shard_total[5],
            shard_total[6],
            shard_total[7],
            shard_total[8],
            shard_total[9],
            shard_total[10],
            shard_total[11],
        ),
        "rep",
    )
    mix_grad = lax.psum(alpha_total, ("rep", "shard"))
    output_all = jnp.concatenate(outputs_list, axis=0)
    input_all = jnp.concatenate(input_list, axis=0)
    earlier_all = jnp.concatenate(earlier_list, axis=1)
    return (
        output_all,
        input_all,
        earlier_all,
        mix_grad,
        summed[0],
        summed[1],
        summed[2],
        summed[3],
        summed[4],
        summed[5],
        summed[6],
        summed[7],
        summed[8],
        summed[9],
        summed[10],
        summed[11],
    )


def solution(mesh):
    return jax.shard_map(
        shards,
        mesh=mesh,
        in_specs=(
            P(("rep", "shard"), None),
            P(None, ("rep", "shard"), None),
            P(("rep", "shard"), None),
            P(("rep", "shard"), None),
            P(),
            P("shard"),
            P("shard"),
            P("shard", None),
            P("shard"),
            P("shard", None),
            P("shard"),
            P("shard"),
            P("shard"),
            P("shard", None),
            P("shard"),
            P("shard", None),
            P("shard"),
        ),
        out_specs=(
            P(("rep", "shard"), None),
            P(("rep", "shard"), None),
            P(None, ("rep", "shard"), None),
            P(),
            P("shard"),
            P("shard"),
            P("shard", None),
            P("shard"),
            P("shard", None),
            P("shard"),
            P("shard"),
            P("shard"),
            P("shard", None),
            P("shard"),
            P("shard", None),
            P("shard"),
        ),
        check_vma=False,
    )
```

profile of v0, /device:TPU:0, one launch (start us, length us, event | category | flops | bytes accessed | tf_op | source)
XLA Modules:
  0.0 1182.0 jit_solution(195760556087470829)
XLA Ops:
  14.3 14.0 %all-reduce.26 = (bf16[2304]{0:T(1024)(128)(2,1)S(1)}, bf16[768]{0:T(1024)(128)(2,1)S(1)}, bf16[768]{0:T(1024)(128)(2,1)S(1)}, bf16[768]{0:T(1024)(128)(2,1)S(1)...) all-reduce(bf16[2304]{0:T(1024)(128)(2,1)S(1)} %dynamic-update-slic, ...), channel_id=1, replica_groups=mesh['rep'=8,'shard'=4] {'shard'}, use_global_device_ids=true, to_apply=%add.10 | all-reduce | flops 6912 | bytes 27648
  33.0 5.2 all-gather
  40.4 3.2 all-gather.6.cloned.1.call-done
  43.6 8.8 convolution_add_fusion
  52.4 9.6 copy.59
  62.0 3.4 slice_bitcast_fusion.1
  66.7 20.3 %fusion.7 = (f32[12,1024]{1,0:T(8,128)S(1)}, f32[12,1024,1024]{1,2,0:T(8,128)}) fusion(pred[1024,1024]{0,1:T(8,128)(4,1)S(1)} %copy-done.40, bf16[1024,12,32]{0,2,1:T(8,128)(2,1)S(1)} %get-tuple-element.110, bf16[1024,12,32]{0,2,1:T(8,128)(2,1)S(1)} %get-tuple-element.111, bf16[1024,12,32]{0,2,1:T(8,128)(2,1)S(1)} %get-tuple-element.95, ...), kind=kOutput, calls=%fused_computation.19 | convolution fusion | flops 1654640640 | bytes 54575104 | tf_op jit(solution)/shard_map/qhd,khd->hqk/dot_general | solution.py:103
  87.0 21.1 %fusion.5 = f32[12,1024]{1,0:T(8,128)S(1)} fusion(f32[12,1024,1024]{1,2,0:T(8,128)} %get-tuple-element.124, f32[12,1024]{1,0:T(8,128)S(1)} %get-tuple-element.123, pred[1024,1024]{0,1:T(8,128)(4,1)S(1)} %copy-done.40), kind=kLoop, calls=%fused_computation.17 | loop fusion | flops 50319360 | bytes 51478528 | tf_op jit(solution)/shard_map/reduce_sum | solution.py:111
  108.1 23.3 %fusion.145 = bf16[12,64,1024]{2,1,0:T(8,128)(2,1)} fusion(f32[12,1024,1024]{1,2,0:T(8,128)} %get-tuple-element.124, f32[12,1024]{1,0:T(8,128)S(1)} %fusion.5, f32[12,1024]{1,0:T(8,128)S(1)} %get-tuple-element.123, pred[1024,1024]{0,1:T(8,128)(4,1)S(1)} %copy-done.40, f32[1024,3,12,64]{0,3,2,1:T(8,128)} %bitcast.118), kind=kOutput, calls=%fused_computation.188 | convolution fusion | flops 1674313728 | bytes 54624256 | tf_op jit(solution)/shard_map/hqk,khd->qhd/dot_general | solution.py:115
  131.4 6.9 convolution_add_fusion.1
  138.3 9.6 copy.57
  147.9 3.6 fusion.223
  153.7 3.3 slice_bitcast_fusion.3
  157.0 10.5 fusion.215
  167.6 18.3 %fusion.226 = (f32[3072]{0:T(1024)}, bf16[1024,3072]{1,0:T(8,128)(2,1)S(1)}) fusion(f32[1024,3072]{1,0:T(8,128)} %fusion.215, f32[3072]{0:T(1024)S(1)} %bitcast.135, bf16[3072,768]{1,0:T(8,128)(2,1)} %all-gather.12.cloned.1.call-done, f32[]{:T(128)} %bitcast.5, bf16[2048,768]{1,0:T(8,128)(2,1)} %param.20), kind=kOutput, calls=%fused_computation.297 | convolution fusion | flops 4903400448 | bytes 25190912 | tf_op jit(solution)/shard_map/dot_general | solution.py:50
  185.9 6.1 multiply_reduce_fusion.4
  196.4 21.5 %fusion.161 = f32[12,1024,1024]{1,2,0:T(8,128)} fusion(bf16[1024,12,64]{0,2,1:T(8,128)(2,1)S(1)} %bitcast.130, f32[1024,3,12,64]{0,3,2,1:T(8,128)} %bitcast.119), kind=kOutput, calls=%fused_computation.227 | convolution fusion | flops 1610612736 | bytes 53477376 | tf_op jit(solution)/shard_map/qhd,khd->hqk/dot_general | solution.py:172
  218.0 65.3 %fusion.133 = f32[1024,12,64]{0,2,1:T(8,128)} fusion(f32[12,1024,1024]{1,2,0:T(8,128)} %fusion.161, f32[12,1024,1024]{1,2,0:T(8,128)} %get-tuple-element.124, f32[12,1024]{1,0:T(8,128)S(1)} %log_add_fusion, pred[1024,1024]{0,1:T(8,128)(4,1)S(1)} %copy-done.41, bf16[1024,12,32]{0,2,1:T(8,128)(2,1)} %copy-done.59, bf16[1024,12,32]{0,2,1:T(8,128)(2,1)} %copy-done.60), kind=kOutput, calls=%fused_computation.182 | convolution fusion | flops 1752183808 | bytes 106479616 | tf_op jit(solution)/shard_map/hqk,khd->qhd/dot_general | solution.py:177
  283.2 66.0 %fusion.136 = f32[1024,12,64]{0,2,1:T(8,128)} fusion(f32[12,1024,1024]{1,2,0:T(8,128)} %fusion.161, f32[12,1024,1024]{1,2,0:T(8,128)} %get-tuple-element.124, f32[12,1024]{1,0:T(8,128)S(1)} %log_add_fusion, pred[1024,1024]{0,1:T(8,128)(4,1)S(1)} %copy-done.41, bf16[1024,12,32]{0,2,1:T(8,128)(2,1)} %copy-done.58, bf16[1024,12,32]{0,2,1:T(8,128)(2,1)S(1)} %copy-done.57), kind=kOutput, calls=%fused_computation.183 | convolution fusion | flops 1752183808 | bytes 106479616 | tf_op jit(solution)/shard_map/hqk,qhd->khd/dot_general | solution.py:180
  349.3 22.4 %fusion.130 = f32[1024,1,12,64]{0,3,2,1:T(8,128)} fusion(bf16[1024,12,64]{0,2,1:T(8,128)(2,1)S(1)} %bitcast.131, f32[12,1024,1024]{1,2,0:T(8,128)} %get-tuple-element.124, f32[12,1024]{1,0:T(8,128)S(1)} %log_add_fusion, pred[1024,1024]{0,1:T(8,128)(4,1)S(1)} %copy-done.41), kind=kOutput, calls=%fused_computation.181 | convolution fusion | flops 1660944384 | bytes 56147968 | tf_op jit(solution)/shard_map/hqk,qhd->khd/dot_general | solution.py:181
  371.7 5.6 multiply_add_fusion.3
  377.4 18.8 %fusion.6 = (f32[12,1024]{1,0:T(8,128)S(1)}, f32[12,1024,1024]{1,2,0:T(8,128)}) fusion(pred[1024,1024]{0,1:T(8,128)(4,1)S(1)} %copy-done.38, bf16[1024,12,32]{0,2,1:T(8,128)(2,1)S(1)} %get-tuple-element.102, bf16[1024,12,32]{0,2,1:T(8,128)(2,1)S(1)} %get-tuple-element.103, bf16[1024,12,32]{0,2,1:T(8,128)(2,1)S(1)} %get-tuple-element.106, ...), kind=kOutput, calls=%fused_computation.18 | convolution fusion | flops 1654640640 | bytes 54575104 | tf_op jit(solution)/shard_map/qhd,khd->hqk/dot_general | solution.py:103
  396.2 21.0 %fusion.4 = f32[12,1024]{1,0:T(8,128)S(1)} fusion(f32[12,1024,1024]{1,2,0:T(8,128)} %get-tuple-element.131, f32[12,1024]{1,0:T(8,128)S(1)} %get-tuple-element.130, pred[1024,1024]{0,1:T(8,128)(4,1)S(1)} %copy-done.38), kind=kLoop, calls=%fused_computation.16 | loop fusion | flops 50319360 | bytes 51478528 | tf_op jit(solution)/shard_map/reduce_sum | solution.py:111
  417.2 21.4 %fusion.146 = bf16[12,64,1024]{2,1,0:T(8,128)(2,1)S(1)} fusion(f32[12,1024,1024]{1,2,0:T(8,128)} %get-tuple-element.131, f32[12,1024]{1,0:T(8,128)S(1)} %fusion.4, f32[12,1024]{1,0:T(8,128)S(1)} %get-tuple-element.130, pred[1024,1024]{0,1:T(8,128)(4,1)S(1)} %copy-done.38, f32[1024,3,12,64]{0,3,2,1:T(8,128)} %bitcast.114), kind=kOutput, calls=%fused_computation.189 | convolution fusion | flops 1674313728 | bytes 54624256 | tf_op jit(solution)/shard_map/hqk,khd->qhd/dot_general | solution.py:115
  442.2 8.3 fusion.214
  450.5 15.9 %fusion.225 = (f32[3072]{0:T(1024)}, bf16[1024,3072]{1,0:T(8,128)(2,1)S(1)}) fusion(f32[1024,3072]{1,0:T(8,128)} %fusion.214, f32[3072]{0:T(1024)S(1)} %bitcast.136, bf16[3072,768]{1,0:T(8,128)(2,1)} %all-gather.12.cloned.1.call-done, f32[]{:T(128)} %bitcast.5, bf16[2048,768]{1,0:T(8,128)(2,1)S(1)} %copy-done.21), kind=kOutput, calls=%fused_computation.296 | convolution fusion | flops 4903400448 | bytes 25190404 | tf_op jit(solution)/shard_map/dot_general | solution.py:50
  466.4 10.8 multiply_reduce_fusion.5
  478.9 3.3 convolution_convert_fusion.1
  482.2 21.2 %fusion.164 = f32[12,1024,1024]{1,2,0:T(8,128)} fusion(bf16[1024,12,64]{0,2,1:T(8,128)(2,1)} %bitcast.128, f32[1024,3,12,64]{0,3,2,1:T(8,128)} %bitcast.115), kind=kOutput, calls=%fused_computation.228 | convolution fusion | flops 1610612736 | bytes 53477376 | tf_op jit(solution)/shard_map/qhd,khd->hqk/dot_general | solution.py:172
  503.5 65.9 %fusion.139 = f32[1024,12,64]{0,2,1:T(8,128)} fusion(f32[12,1024,1024]{1,2,0:T(8,128)} %fusion.164, f32[12,1024,1024]{1,2,0:T(8,128)} %get-tuple-element.131, f32[12,1024]{1,0:T(8,128)S(1)} %log_add_fusion.1, pred[1024,1024]{0,1:T(8,128)(4,1)} %fusion.91, bf16[1024,12,32]{0,2,1:T(8,128)(2,1)} %copy-done.54, bf16[1024,12,32]{0,2,1:T(8,128)(2,1)} %copy-done.55), kind=kOutput, calls=%fused_computation.184 | convolution fusion | flops 1752183808 | bytes 106479616 | tf_op jit(solution)/shard_map/hqk,khd->qhd/dot_general | solution.py:177
  569.3 67.1 %fusion.142 = f32[1024,12,64]{0,2,1:T(8,128)} fusion(f32[12,1024,1024]{1,2,0:T(8,128)} %fusion.164, f32[12,1024,1024]{1,2,0:T(8,128)} %get-tuple-element.131, f32[12,1024]{1,0:T(8,128)S(1)} %log_add_fusion.1, pred[1024,1024]{0,1:T(8,128)(4,1)} %fusion.91, bf16[1024,12,32]{0,2,1:T(8,128)(2,1)} %copy-done.52, bf16[1024,12,32]{0,2,1:T(8,128)(2,1)} %copy-done.53), kind=kOutput, calls=%fused_computation.185 | convolution fusion | flops 1752183808 | bytes 106479616 | tf_op jit(solution)/shard_map/hqk,qhd->khd/dot_general | solution.py:180
  636.5 5.0 fusion.154
  641.5 3.7 convolution_add_fusion.5
  649.3 2.4 copy-done.42
  657.3 3.2 fusion.79
  660.5 21.4 %fusion.127 = f32[1024,1,12,64]{0,3,2,1:T(8,128)} fusion(bf16[1024,12,64]{0,2,1:T(8,128)(2,1)} %bitcast.129, f32[12,1024,1024]{1,2,0:T(8,128)} %get-tuple-element.131, f32[12,1024]{1,0:T(8,128)S(1)} %log_add_fusion.1, pred[1024,1024]{0,1:T(8,128)(4,1)S(1)} %copy-done.39), kind=kOutput, calls=%fused_computation.180 | convolution fusion | flops 1660944384 | bytes 56147968 | tf_op jit(solution)/shard_map/hqk,qhd->khd/dot_general | solution.py:181
  682.0 2.6 fusion.81
  684.8 6.7 fusion.207
  691.5 8.7 convolution_add_fusion.2
  701.0 9.7 fusion.123
  710.6 11.8 convolution_add_fusion.4
  723.1 14.2 %fusion.149 = f32[3072,768]{1,0:T(8,128)S(1)} fusion(f32[]{:T(128)} %bitcast.5, bf16[2048,768]{1,0:T(8,128)(2,1)} %param.20, f32[1024,3072]{1,0:T(8,128)} %fusion.214, f32[3072]{0:T(1024)S(1)} %bitcast.137), kind=kOutput, calls=%fused_computation.213 | convolution fusion | flops 4865654784 | bytes 23605760 | tf_op jit(solution)/shard_map/dot_general | solution.py:44
  737.3 14.0 %convolution_add_fusion.3 = f32[3072,768]{1,0:T(8,128)} fusion(f32[3072,768]{1,0:T(8,128)S(1)} %fusion.149, f32[]{:T(128)} %bitcast.5, bf16[2048,768]{1,0:T(8,128)(2,1)S(1)} %copy-done.22, f32[1024,3072]{1,0:T(8,128)} %fusion.215, f32[3072]{0:T(1024)S(1)} %bitcast.138), kind=kOutput, calls=%fused_computation.83 | convolution fusion | flops 4868014080 | bytes 33042436 | tf_op jit(solution)/shard_map/dot_general | solution.py:44
  753.3 5.1 slice_convert_fusion.5
  758.4 15.2 %multiply_reduce_fusion.2 = (f32[4]{0:T(128)S(1)}, f32[4]{0:T(128)S(1)}, f32[4,1024,768]{2,1,0:T(8,128)S(1)}, f32[4,1024,768]{2,1,0:T(8,128)}) fusion(f32[1024,768]{1,0:T(8,128)} %get-tuple-element.101, bf16[4,2048,768]{2,1,0:T(8,128)(2,1)} %param.18, f32[1024,768]{1,0:T(8,128)} %get-tuple-element.100, f32[4]{0:T(128)S(1)} %bitcast.134), kind=kLoop, calls=%fused_computation.65 | loop fusion | flops 25165816 | bytes 44040240 | tf_op jit(solution)/shard_map/reduce_sum | solution.py:148
  773.6 17.1 %pad_maximum_fusion = f32[4,2048,768]{2,1,0:T(8,128)} fusion(f32[4,1024,768]{2,1,0:T(8,128)} %get-tuple-element.99, f32[4,1024,768]{2,1,0:T(8,128)S(1)} %get-tuple-element.98), kind=kLoop, calls=%fused_computation.26 | loop fusion | flops 6291456 | bytes 50331648 | tf_op jit(solution)/shard_map/concatenate | solution.py:301
  790.8 11.1 slice_convert_fusion.1
  801.9 5.9 fusion.227
  807.9 6.2 fusion.103
  814.2 20.4 %fusion.111 = (bf16[1024,768]{1,0:T(8,128)(2,1)}, f32[1024,768]{1,0:T(8,128)}) fusion(f32[4,1024,768]{2,1,0:T(8,128)} %get-tuple-element.76, f32[]{:T(128)} %bitcast.5, f32[]{:T(128)} %bitcast.3, f32[]{:T(128)} %bitcast.2, f32[]{:T(128)} %bitcast.1, f32[]{:T(128)} %bitcast, f32[768]{0:T(1024)S(1)} %convert_element_type.175, ...), kind=kOutput, calls=%fused_computation.129 | convolution fusion | flops 4872732672 | bytes 37764116 | tf_op jit(solution)/shard_map/dot_general | solution.py:133
  834.7 10.8 reduce-scatter.9.cloned.1.call-done
  845.4 81.1 %reduce-scatter.11.cloned.1.call-done = f32[768,768]{1,0:T(8,128)} async-done(((f32[3072,768]{1,0:T(8,128)}), f32[768,768]{1,0:T(8,128)}) %reduce-scatter.11.cloned.1.call-update) | async-done | bytes 2359312 | tf_op jit(solution)/shard_map/reduce_scatter | solution.py:273
  926.5 5.3 fusion.101
  931.9 21.1 %fusion.117 = (bf16[1024,768]{1,0:T(8,128)(2,1)}, f32[1024,768]{1,0:T(8,128)}) fusion(f32[4,1024,768]{2,1,0:T(8,128)} %get-tuple-element.75, f32[]{:T(128)} %bitcast.5, f32[]{:T(128)} %bitcast.3, f32[]{:T(128)} %bitcast.2, f32[]{:T(128)} %bitcast.1, f32[]{:T(128)} %bitcast, f32[768]{0:T(1024)S(1)} %convert_element_type.175, f32[1024,768]{1,0:T(8,128)S(1)} %copy-done.5, ...), kind=kOutput, calls=%fused_computation.142 | convolution fusion | flops 4872732672 | bytes 37764116 | tf_op jit(solution)/shard_map/dot_general | solution.py:133
  953.1 9.8 multiply_reduce_fusion.12
  964.9 43.7 %psum.91 = f32[5]{0:T(128)} all-reduce(f32[5]{0:T(128)S(1)} %maximum_add_fusion), channel_id=1, replica_groups=mesh['rep'=8,'shard'=4] {'rep','shard'}, use_global_device_ids=true, to_apply=%region_26.27 | all-reduce | flops 5 | bytes 40 | tf_op jit(solution)/shard_map/psum | solution.py:298
  1008.6 4.4 fusion.80
  1016.1 11.6 all-reduce.25
  1028.3 37.6 %all-reduce.23 = (f32[192]{0:T(256)}, f32[192]{0:T(256)}, f32[576]{0:T(1024)}, f32[192]{0:T(256)}, f32[192]{0:T(256)}, /*index=5*/f32[192]{0:T(256)}, f32[768]{0:T(1024)}, f32[192]{0:T(256)}) all-reduce(f32[192]{0:T(256)S(1)} %dynamic-slice.8, f32[192]{0:T(256)S(1)} %dynamic-slice.10, ...), channel_id=1, replica_groups=mesh['rep'=8,'shard'=4] {'rep'}, use_global_device_ids=true, to_apply=%region_31.32 | all-reduce | flops 2496 | bytes 19968 | tf_op jit(solution)/shard_map/psum | solution.py:281
  1065.9 3.9 pad_maximum_fusion.4
  1070.8 4.5 add_add_fusion.4
  1075.4 3.1 pad_maximum_fusion.3
  1078.5 89.9 %all-reduce.29.cloned.1.call-done = (f32[192,2304]{1,0:T(8,128)}, f32[192,768]{1,0:T(8,128)}, f32[192,3072]{1,0:T(8,128)}, f32[768,768]{1,0:T(8,128)}) async-done(((f32[192,2304]{1,0:T(8,128)}, f32[192,768]{1,0:T(8,128)}, f32[192,3072]{1,0:T(8,128)}, f32[768,768]{1,0:T(8,128)}), (f32[192,2304]{1,0:T(8,128)}, f32[192,768]{1,0:T(8,128)}, f32[192,3072]{1,0:T(8,128)}, ...) | async-done | bytes 7077904 | tf_op jit(solution)/shard_map/psum | solution.py:281
  1168.4 2.9 copy.86
  (385 shorter events, 46.8 us)
Async XLA Ops:
  7.3 21.1 %copy-start.102 = (s32[2,1024]{1,0:T(2,128)S(1)}, s32[2,1024]{1,0:T(2,128)}, u32[]{:S(2)}) copy-start(s32[2,1024]{1,0:T(2,128)} %param.19) | copy-start | bytes 24580
  7.3 22.6 %copy-start = (bf16[2048,768]{1,0:T(8,128)(2,1)S(1)}, bf16[2048,768]{1,0:T(8,128)(2,1)}, u32[]{:S(2)}) copy-start(bf16[2048,768]{1,0:T(8,128)(2,1)} %param.17) | copy-start | bytes 9437188
  7.3 36.3 %all-gather.6.cloned.1.call-start = ((), (), s32[]{:S(2)}) async-start(), calls=%async_computation.4 | async-start | bytes 4423680 | tf_op jit(solution)/shard_map/all_gather | solution.py:238
  8.0 139.8 %all-gather.8.cloned.1.call-start = ((), (), s32[]{:S(2)}) async-start(), calls=%async_computation.5 | async-start | bytes 1474560 | tf_op jit(solution)/shard_map/all_gather | solution.py:240
  8.8 148.3 %all-gather.10.cloned.1.call-start = ((), (), s32[]{:S(2)}) async-start(), calls=%async_computation.6 | async-start | bytes 5898240 | tf_op jit(solution)/shard_map/all_gather | solution.py:244
  9.5 158.0 %all-gather.12.cloned.1.call-start = ((), (), s32[]{:S(2)}) async-start(), calls=%async_computation.7 | async-start | bytes 5898240 | tf_op jit(solution)/shard_map/all_gather | solution.py:246
  10.1 824.5 %reduce-scatter.7.cloned.1.call-start = ((), (), s32[]{:S(2)}) async-start(), calls=%async_computation.9 | async-start | bytes 2949120 | tf_op jit(solution)/shard_map/reduce_scatter | solution.py:267
  28.3 119.6 %copy-start.109 = (f32[768]{0:T(1024)}, f32[768]{0:T(1024)S(1)}, u32[]{:S(2)}) copy-start(f32[768]{0:T(1024)S(1)} %convert_element_type.169) | copy-start | bytes 9220
  30.4 101.0 %copy-start.80 = (f32[1024]{0:T(1024)}, f32[1024]{0:T(1024)S(1)}, u32[]{:S(2)}) copy-start(f32[1024]{0:T(1024)S(1)} %broadcast_multiply_fusion.5) | copy-start | bytes 12292
  30.4 22.0 %copy-start.76 = (f32[1024]{0:T(1024)}, f32[1024]{0:T(1024)S(1)}, u32[]{:S(2)}) copy-start(f32[1024]{0:T(1024)S(1)} %broadcast_multiply_fusion.3) | copy-start | bytes 12292
  31.8 20.6 %copy-start.82 = (f32[1024]{0:T(1024)}, f32[1024]{0:T(1024)S(1)}, u32[]{:S(2)}) copy-start(f32[1024]{0:T(1024)S(1)} %fusion.171) | copy-start | bytes 12292
  32.4 99.0 %copy-start.107 = (f32[768]{0:T(1024)}, f32[768]{0:T(1024)S(1)}, u32[]{:S(2)}) copy-start(f32[768]{0:T(1024)S(1)} %convert_element_type.161) | copy-start | bytes 9220
  32.4 99.0 %copy-start.78 = (f32[768]{0:T(1024)}, f32[768]{0:T(1024)S(1)}, u32[]{:S(2)}) copy-start(f32[768]{0:T(1024)S(1)} %convert_element_type.160) | copy-start | bytes 9220
  32.9 32.5 %copy-start.46 = (f32[1024,32]{0,1:T(8,128)}, f32[1024,32]{0,1:T(8,128)S(1)}, u32[]{:S(2)}) copy-start(f32[1024,32]{0,1:T(8,128)S(1)} %get-tuple-element.121) | copy-start | bytes 393220
  33.0 32.5 %copy-start.49 = (f32[1024,32]{0,1:T(8,128)}, f32[1024,32]{0,1:T(8,128)S(1)}, u32[]{:S(2)}) copy-start(f32[1024,32]{0,1:T(8,128)S(1)} %get-tuple-element.122) | copy-start | bytes 393220
  33.0 124.1 %copy-start.65 = (f32[768]{0:T(1024)}, f32[768]{0:T(1024)S(1)}, u32[]{:S(2)}) copy-start(f32[768]{0:T(1024)S(1)} %convert_element_type.171) | copy-start | bytes 9220
  33.0 159.0 %copy-start.61 = (f32[768]{0:T(1024)}, f32[768]{0:T(1024)S(1)}, u32[]{:S(2)}) copy-start(f32[768]{0:T(1024)S(1)} %convert_element_type.170) | copy-start | bytes 9220
  40.4 90.9 %copy-start.88 = (f32[1024]{0:T(1024)}, f32[1024]{0:T(1024)S(1)}, u32[]{:S(2)}) copy-start(f32[1024]{0:T(1024)S(1)} %fusion.169) | copy-start | bytes 12292
  66.6 20.4 %copy-start.56 = (bf16[1024,12,32]{0,2,1:T(8,128)(2,1)}, bf16[1024,12,32]{0,2,1:T(8,128)(2,1)S(1)}, u32[]{:S(2)}) copy-start(bf16[1024,12,32]{0,2,1:T(8,128)(2,1)S(1)} %get-tuple-element.94) | copy-start | bytes 2359300
  66.6 20.4 %copy-start.58 = (bf16[1024,12,32]{0,2,1:T(8,128)(2,1)}, bf16[1024,12,32]{0,2,1:T(8,128)(2,1)S(1)}, u32[]{:S(2)}) copy-start(bf16[1024,12,32]{0,2,1:T(8,128)(2,1)S(1)} %get-tuple-element.95) | copy-start | bytes 2359300
  66.6 20.3 %copy-start.59 = (bf16[1024,12,32]{0,2,1:T(8,128)(2,1)}, bf16[1024,12,32]{0,2,1:T(8,128)(2,1)S(1)}, u32[]{:S(2)}) copy-start(bf16[1024,12,32]{0,2,1:T(8,128)(2,1)S(1)} %get-tuple-element.110) | copy-start | bytes 2359300
  66.6 20.3 %copy-start.60 = (bf16[1024,12,32]{0,2,1:T(8,128)(2,1)}, bf16[1024,12,32]{0,2,1:T(8,128)(2,1)S(1)}, u32[]{:S(2)}) copy-start(bf16[1024,12,32]{0,2,1:T(8,128)(2,1)S(1)} %get-tuple-element.111) | copy-start | bytes 2359300
  108.1 23.3 %copy-start.116 = (bf16[768,2304]{1,0:T(8,128)(2,1)S(1)}, bf16[768,2304]{1,0:T(8,128)(2,1)}, u32[]{:S(2)}) copy-start(bf16[768,2304]{1,0:T(8,128)(2,1)} %all-gather.6.cloned.1.call-done) | copy-start | bytes 10616836
  151.5 40.5 %copy-start.68 = (f32[1024]{0:T(1024)}, f32[1024]{0:T(1024)S(1)}, u32[]{:S(2)}) copy-start(f32[1024]{0:T(1024)S(1)} %broadcast_multiply_fusion.2) | copy-start | bytes 12292
  153.7 38.4 %copy-start.72 = (f32[1024]{0:T(1024)}, f32[1024]{0:T(1024)S(1)}, u32[]{:S(2)}) copy-start(f32[1024]{0:T(1024)S(1)} %fusion.172) | copy-start | bytes 12292
  157.0 10.5 copy-start.97
  167.6 18.3 %copy-start.115 = (bf16[768,3072]{1,0:T(8,128)(2,1)S(1)}, bf16[768,3072]{1,0:T(8,128)(2,1)}, u32[]{:S(2)}) copy-start(bf16[768,3072]{1,0:T(8,128)(2,1)} %all-gather.10.cloned.1.call-done) | copy-start | bytes 14155780
  196.4 21.5 %copy-start.41 = (pred[1024,1024]{0,1:T(8,128)(4,1)S(1)}, pred[1024,1024]{0,1:T(8,128)(4,1)}, u32[]{:S(2)}) copy-start(pred[1024,1024]{0,1:T(8,128)(4,1)} %fusion.90) | copy-start | bytes 3145732
  218.0 65.3 %copy-start.57 = (bf16[1024,12,32]{0,2,1:T(8,128)(2,1)S(1)}, bf16[1024,12,32]{0,2,1:T(8,128)(2,1)}, u32[]{:S(2)}) copy-start(bf16[1024,12,32]{0,2,1:T(8,128)(2,1)} %copy-done.56) | copy-start | bytes 2359300
  349.3 22.4 %copy-start.30 = (f32[1024,12,64]{0,2,1:T(8,128)S(1)}, f32[1024,12,64]{0,2,1:T(8,128)}, u32[]{:S(2)}) copy-start(f32[1024,12,64]{0,2,1:T(8,128)} %get-tuple-element.77) | copy-start | bytes 9437188
  349.3 22.4 %copy-start.31 = (f32[1024,12,64]{0,2,1:T(8,128)S(1)}, f32[1024,12,64]{0,2,1:T(8,128)}, u32[]{:S(2)}) copy-start(f32[1024,12,64]{0,2,1:T(8,128)} %get-tuple-element.78) | copy-start | bytes 9437188
  349.3 22.4 %copy-start.47 = (f32[1024,32]{0,1:T(8,128)S(1)}, f32[1024,32]{0,1:T(8,128)}, u32[]{:S(2)}) copy-start(f32[1024,32]{0,1:T(8,128)} %copy-done.46) | copy-start | bytes 393220
  349.3 22.4 %copy-start.50 = (f32[1024,32]{0,1:T(8,128)S(1)}, f32[1024,32]{0,1:T(8,128)}, u32[]{:S(2)}) copy-start(f32[1024,32]{0,1:T(8,128)} %copy-done.49) | copy-start | bytes 393220
  377.3 18.9 %copy-start.52 = (bf16[1024,12,32]{0,2,1:T(8,128)(2,1)}, bf16[1024,12,32]{0,2,1:T(8,128)(2,1)S(1)}, u32[]{:S(2)}) copy-start(bf16[1024,12,32]{0,2,1:T(8,128)(2,1)S(1)} %get-tuple-element.106) | copy-start | bytes 2359300
  377.3 18.9 %copy-start.53 = (bf16[1024,12,32]{0,2,1:T(8,128)(2,1)}, bf16[1024,12,32]{0,2,1:T(8,128)(2,1)S(1)}, u32[]{:S(2)}) copy-start(bf16[1024,12,32]{0,2,1:T(8,128)(2,1)S(1)} %get-tuple-element.107) | copy-start | bytes 2359300
  377.4 18.9 %copy-start.54 = (bf16[1024,12,32]{0,2,1:T(8,128)(2,1)}, bf16[1024,12,32]{0,2,1:T(8,128)(2,1)S(1)}, u32[]{:S(2)}) copy-start(bf16[1024,12,32]{0,2,1:T(8,128)(2,1)S(1)} %get-tuple-element.102) | copy-start | bytes 2359300
  377.4 18.9 %copy-start.55 = (bf16[1024,12,32]{0,2,1:T(8,128)(2,1)}, bf16[1024,12,32]{0,2,1:T(8,128)(2,1)S(1)}, u32[]{:S(2)}) copy-start(bf16[1024,12,32]{0,2,1:T(8,128)(2,1)S(1)} %get-tuple-element.103) | copy-start | bytes 2359300
  417.2 21.5 %copy-start.1 = (bf16[2048,768]{1,0:T(8,128)(2,1)S(1)}, bf16[2048,768]{1,0:T(8,128)(2,1)}, u32[]{:S(2)}) copy-start(bf16[2048,768]{1,0:T(8,128)(2,1)} %param.17) | copy-start | bytes 9437188
  417.2 21.5 %copy-start.110 = (f32[768]{0:T(1024)S(1)}, f32[768]{0:T(1024)}, u32[]{:S(2)}) copy-start(f32[768]{0:T(1024)} %copy-done.109) | copy-start | bytes 9220
  417.2 21.5 %copy-start.120 = (bf16[768,768]{1,0:T(8,128)(2,1)S(1)}, bf16[768,768]{1,0:T(8,128)(2,1)}, u32[]{:S(2)}) copy-start(bf16[768,768]{1,0:T(8,128)(2,1)} %all-gather.8.cloned.1.call-done) | copy-start | bytes 3538948
  440.5 36.8 %copy-start.4 = (f32[1024,768]{1,0:T(8,128)}, f32[1024,768]{1,0:T(8,128)S(1)}, u32[]{:S(2)}) copy-start(f32[1024,768]{1,0:T(8,128)S(1)} %get-tuple-element.133) | copy-start | bytes 9437188
  440.5 36.7 %copy-start.70 = (f32[1024]{0:T(1024)}, f32[1024]{0:T(1024)S(1)}, u32[]{:S(2)}) copy-start(f32[1024]{0:T(1024)S(1)} %broadcast_multiply_fusion.4) | copy-start | bytes 12292
  442.2 35.1 %copy-start.74 = (f32[1024]{0:T(1024)}, f32[1024]{0:T(1024)S(1)}, u32[]{:S(2)}) copy-start(f32[1024]{0:T(1024)S(1)} %fusion.170) | copy-start | bytes 12292
  466.4 10.8 copy-start.32
  478.9 157.5 %copy-start.95 = (f32[1024]{0:T(1024)}, f32[1024]{0:T(1024)S(1)}, u32[]{:S(2)}) copy-start(f32[1024]{0:T(1024)S(1)} %negate_multiply_fusion.3) | copy-start | bytes 12292
  645.2 189.5 %reduce-scatter.5.cloned.1.call-start = ((), (), s32[]{:S(2)}) async-start(), calls=%async_computation.8 | async-start | bytes 8847360 | tf_op jit(solution)/shard_map/reduce_scatter | solution.py:265
  654.2 27.7 %copy-start.10 = (f32[1024,1,12,64]{0,3,2,1:T(8,128)}, f32[1024,1,12,64]{0,3,2,1:T(8,128)S(1)}, u32[]{:S(2)}) copy-start(f32[1024,1,12,64]{0,3,2,1:T(8,128)S(1)} %add_bitcast_fusion.2) | copy-start | bytes 9437188
  657.3 24.6 %copy-start.11 = (f32[1024,1,12,64]{0,3,2,1:T(8,128)}, f32[1024,1,12,64]{0,3,2,1:T(8,128)S(1)}, u32[]{:S(2)}) copy-start(f32[1024,1,12,64]{0,3,2,1:T(8,128)S(1)} %add_bitcast_fusion.3) | copy-start | bytes 9437188
  700.3 10.3 copy-start.69
  700.3 10.3 copy-start.73
  700.3 145.1 %reduce-scatter.9.cloned.1.call-start = ((), (), s32[]{:S(2)}) async-start(), calls=%async_computation.10 | async-start | bytes 11796480 | tf_op jit(solution)/shard_map/reduce_scatter | solution.py:271
  722.4 204.0 %reduce-scatter.11.cloned.1.call-start = ((), (), s32[]{:S(2)}) async-start(), calls=%async_computation.11 | async-start | bytes 11796480 | tf_op jit(solution)/shard_map/reduce_scatter | solution.py:273
  723.1 14.2 %copy-start.22 = (bf16[2048,768]{1,0:T(8,128)(2,1)S(1)}, bf16[2048,768]{1,0:T(8,128)(2,1)}, u32[]{:S(2)}) copy-start(bf16[2048,768]{1,0:T(8,128)(2,1)} %param.20) | copy-start | bytes 9437188
  751.4 417.0 %all-reduce.29.cloned.1.call-start = ((), (), s32[]{:S(2)}) async-start(), calls=%async_computation.12 | async-start | bytes 14155776 | tf_op jit(solution)/shard_map/psum | solution.py:281
  758.4 32.3 %slice-start = ((s8[12582912]{0:T(1024)(128)(4,1)}), s8[4194304]{0:T(1024)(128)(4,1)S(1)}, s32[]{:S(2)}) async-start(s8[12582912]{0:T(1024)(128)(4,1)} %bitcast.112), calls=%async_computation.13 | async-start | bytes 8388608
  758.4 32.3 %slice-start.1 = ((s8[12582912]{0:T(1024)(128)(4,1)}), s8[4194304]{0:T(1024)(128)(4,1)S(1)}, s32[]{:S(2)}) async-start(s8[12582912]{0:T(1024)(128)(4,1)} %bitcast.112), calls=%async_computation.14 | async-start | bytes 8388608
  773.6 17.1 %slice-start.2 = ((s8[12582912]{0:T(1024)(128)(4,1)}), s8[4194304]{0:T(1024)(128)(4,1)S(1)}, s32[]{:S(2)}) async-start(s8[12582912]{0:T(1024)(128)(4,1)} %bitcast.112), calls=%async_computation.15 | async-start | bytes 8388608
  773.6 34.2 %slice-start.3 = ((s8[4718592]{0:T(1024)(128)(4,1)}), s8[524288]{0:T(1024)(128)(4,1)S(1)}, s32[]{:S(2)}) async-start(s8[4718592]{0:T(1024)(128)(4,1)} %bitcast.121), calls=%async_computation.16 | async-start | bytes 1048576
  790.8 11.2 copy-start.117
  790.8 17.1 %slice-start.4 = ((s8[4718592]{0:T(1024)(128)(4,1)}), s8[4194304]{0:T(1024)(128)(4,1)S(1)}, s32[]{:S(2)}) async-start(s8[4718592]{0:T(1024)(128)(4,1)} %bitcast.121), calls=%async_computation.17 | async-start | bytes 8388608
  931.9 21.2 %copy-start.14 = (f32[1024,768]{1,0:T(8,128)S(1)}, f32[1024,768]{1,0:T(8,128)}, u32[]{:S(2)}) copy-start(f32[1024,768]{1,0:T(8,128)} %copy-done.12) | copy-start | bytes 9437188
  931.9 21.2 %copy-start.23 = (bf16[2048,768]{1,0:T(8,128)(2,1)S(1)}, bf16[2048,768]{1,0:T(8,128)(2,1)}, u32[]{:S(2)}) copy-start(bf16[2048,768]{1,0:T(8,128)(2,1)} %param.20) | copy-start | bytes 9437188
  931.9 21.2 %copy-start.92 = (f32[1024]{0:T(1024)S(1)}, f32[1024]{0:T(1024)}, u32[]{:S(2)}) copy-start(f32[1024]{0:T(1024)} %copy-done.90) | copy-start | bytes 12292
  931.9 21.2 %copy-start.96 = (f32[1024]{0:T(1024)S(1)}, f32[1024]{0:T(1024)}, u32[]{:S(2)}) copy-start(f32[1024]{0:T(1024)} %copy-done.95) | copy-start | bytes 12292
  (83 other events, 324.8 us)
Sparse Core Ops, SparseCore 0:
  9.7 33.8 all-gather.5
  45.2 17.4 all-gather.7
  64.2 37.4 all-gather.9
  103.1 37.4 all-gather.11
  645.3 33.3 reduce-scatter.6
  700.4 63.9 reduce-scatter.4
  767.0 78.4 reduce-scatter.8
  848.0 78.4 reduce-scatter.10
  930.9 237.4 all-reduce.28
where the time goes:
time: 1190 us; the launch traced here: 1180 us
  matrix products  658 us (55%)
  waiting for transfers between devices  188 us (16%)
  other arithmetic  151 us (13%)
  blocking collectives  112 us (9%)
  local copies, waits for them, and re-layouts  53.6 us (5%)
  between operations  19.3 us (2%)
    dot_general x2, matrix products, run_micro(): jnp.einsum('hqk,qhd->khd', grad_scores, queries, preferred_element_type=j...  133 us
    dot_general x2, matrix products, run_micro(): jnp.einsum('hqk,khd->qhd', grad_scores, key_rows, preferred_element_type=...  131 us
    psum x1, waiting for transfers between devices, shards(): lax.psum((shard_total[0], shard_total[1], shard_total[2], shard_total[3],...  89.9 us
    reduce_scatter x1, waiting for transfers between devices, shards(): lax.psum_scatter(grads[10], 'shard', scatter_dimension=0, tiled=True)  81.1 us
    dot_general x8, matrix products, outer_sum(): lax.dot_general(left, right, (((0,), (0,)), ((), ())), preferred_element_...  73.6 us
    dot_general x8, matrix products, back_prod(): lax.dot_general(grad_low, weight, (((1,), (1,)), ((), ())), preferred_ele...  68.7 us
    dot_general x2, matrix products, run_micro(): jnp.einsum('hqk,khd->qhd', probs_low, value_rows, preferred_element_type=...  44.7 us
    dot_general x2, matrix products, run_micro(): jnp.einsum('hqk,qhd->khd', again_low, grad_att, preferred_element_type=jn...  43.8 us
  transfers between devices with their start and end apart: 9, of which 4 were waited for; matrix products, arithmetic and copies ran while one was open for 31% of the time, Pallas kernels for 0%

commit v1 on v0

v1 whole, which is shorter than its diff:
```python
import math

import jax
import jax.numpy as jnp
from jax import lax
from jax.experimental import pallas as pl
from jax.experimental.pallas import tpu as pltpu
from jax.sharding import PartitionSpec as P

HEADS = 12
HEAD = 64
PAIR = 2 * HEAD
EPSILON = 1e-05
LOG2E = math.log2(math.e)
NEG = -1e30
GELU_A = math.sqrt(2.0 / math.pi)
GELU_B = GELU_A * 0.044715
BF = jnp.bfloat16
F32 = jnp.float32
MIB = 1 << 20
MLP_PARTS = 2


def dot_nn(a, b):
    return lax.dot_general(a, b, (((1,), (0,)), ((), ())), preferred_element_type=F32)


def dot_nt(a, b):
    return lax.dot_general(a, b, (((1,), (1,)), ((), ())), preferred_element_type=F32)


def dot_tn(a, b):
    return lax.dot_general(a, b, (((0,), (0,)), ((), ())), preferred_element_type=F32)


def dot_tt(a, b):
    return lax.dot_general(a, b, (((0,), (1,)), ((), ())), preferred_element_type=F32)


def params(vmem):
    return pltpu.CompilerParams(vmem_limit_bytes=vmem * MIB)


ANY = pl.BlockSpec(memory_space=pl.ANY)


def load_pieces(me, pieces, target, sems, start, cols=None):
    copies = []
    for j, piece in enumerate(pieces):
        rows = piece.shape[0]
        at = pl.multiple_of((me ^ j) * rows, rows)
        source = piece if cols is None else piece.at[:, cols]
        copies.append(pltpu.make_async_copy(source, target.at[pl.ds(at, rows), :], sems.at[j]))
    for copy in copies:
        if start:
            copy.start()
        else:
            copy.wait()


def load_some_pieces(me, pieces, target, sems, start, index, count):
    for j, piece in enumerate(pieces):
        rows = piece.shape[0]
        per = len(pieces) // count
        owner = me ^ j

        @pl.when(owner // per == index)
        def _(j=j, piece=piece, rows=rows, owner=owner):
            at = pl.multiple_of((owner - index * per) * rows, rows)
            copy = pltpu.make_async_copy(piece, target.at[pl.ds(at, rows), :], sems.at[j])
            if start:
                copy.start()
            else:
                copy.wait()


def whole(shape):
    zeros = (0,) * len(shape)
    return pl.BlockSpec(shape, lambda *_: zeros, pipeline_mode=pl.Buffered(1))


SMEM = pl.BlockSpec(memory_space=pltpu.SMEM)


def ring_shape(length, width):
    return pltpu.VMEM((width // 128, 2 * length, 128), F32)


def ring_put(ring, at, value):
    for j in range(ring.shape[0]):
        part = value[:, j * 128 : (j + 1) * 128]
        ring[j, at : at + value.shape[0]] = part
        twin = ring.shape[1] // 2 + at
        ring[j, twin : twin + value.shape[0]] = part


def ring_get(ring, start, rows):
    return jnp.concatenate([ring[j, pl.ds(start, rows), :] for j in range(ring.shape[0])], axis=1)


def norm_parts(v):
    mean = jnp.mean(v, axis=-1, keepdims=True)
    centred = v - mean
    var = jnp.mean(centred * centred, axis=-1, keepdims=True)
    r = lax.rsqrt(var + EPSILON)
    return centred * r, r


def qkv_kernel(
    me_ref, shift_ref, x_ref, cot_ref, gain_ref, bias_ref, wb_ref, cos_ref, sin_ref, *refs
):
    pieces, (xr_ref, cr_ref, act_ref, q_ref, k_ref, v_ref, ring, w_ref, sems) = refs[:-9], refs[-9:]
    length, width = x_ref.shape

    @pl.when(pl.program_id(0) == 0)
    def _():
        load_pieces(me_ref[0], pieces, w_ref, sems, True)

    shift = shift_ref[pl.program_id(0)]
    for source, target in ((cot_ref, cr_ref), (x_ref, xr_ref)):
        ring_put(ring, 0, source[...].astype(F32))
        target[...] = ring_get(ring, shift, length).astype(BF)
    n, _ = norm_parts(xr_ref[...].astype(F32))
    act_ref[...] = (n * gain_ref[...].astype(F32) + bias_ref[...].astype(F32)).astype(BF)
    half = HEAD // 2
    rows = 256

    @pl.when(pl.program_id(0) == 0)
    def _():
        load_pieces(me_ref[0], pieces, w_ref, sems, False)

    for part, out in enumerate((q_ref, k_ref, v_ref)):
        scale = LOG2E * HEAD**-0.5 if part == 0 else 1.0
        for base in range(0, width, rows):
            at = part * width + base
            cols = slice(at, at + rows)
            y = dot_tt(w_ref[:, cols], act_ref[...]) + wb_ref[cols, :]
            if part == 2:
                out[0, base : base + rows, :] = y.astype(BF)
                continue
            cos, sin = cos_ref[0], sin_ref[0]
            for h in range(0, rows, HEAD):
                u, w = y[h : h + half], y[h + half : h + HEAD]
                a, b = u * cos - w * sin, w * cos + u * sin
                if part == 0:
                    a, b = a * scale, b * scale
                out[0, base + h : base + h + half, :] = a.astype(BF)
                out[0, base + h + half : base + h + HEAD, :] = b.astype(BF)


def qkv_call(me, shift, x, cot, gain, bias, wb, cos, sin, pieces):
    tokens, width = x.shape
    nseq = shift.shape[0]
    length = tokens // nseq
    row = pl.BlockSpec((length, width), lambda s: (s, 0))
    col = pl.BlockSpec((1, width, length), lambda s: (s, 0, 0))
    tab = pl.BlockSpec((1, HEAD // 2, length), lambda s: (s, 0, 0))
    low = jax.ShapeDtypeStruct((tokens, width), BF)
    turned = jax.ShapeDtypeStruct((nseq, width, length), BF)
    return pl.pallas_call(
        qkv_kernel,
        grid=(nseq,),
        in_specs=[
            SMEM, SMEM, row, row, whole((1, width)), whole((1, width)), whole(wb.shape), tab, tab,
            *(ANY for _ in pieces),
        ],
        out_specs=[row, row, row, col, col, col],
        out_shape=[low, low, low, turned, turned, turned],
        scratch_shapes=[
            ring_shape(length, width),
            pltpu.VMEM((width, 3 * width), BF),
            pltpu.SemaphoreType.DMA((len(pieces),)),
        ],
        compiler_params=params(60),
        cost_estimate=pl.CostEstimate(
            flops=2 * tokens * width * 3 * width, bytes_accessed=20 * MIB, transcendentals=0
        ),
        name="qkv",
    )(me, shift, x, cot, gain, bias, wb, cos, sin, *pieces)


def fill_masks(segc_ref, segr_ref, mask, blk):
    kk = lax.broadcasted_iota(jnp.int32, (blk, blk), 0)
    qq = lax.broadcasted_iota(jnp.int32, (blk, blk), 1)
    causal = kk <= qq
    mask[0] = jnp.where(causal, 0.0, NEG)
    for i, (kb, qb) in enumerate(((0, 0), (0, 1), (1, 1))):
        same = segc_ref[0, pl.ds(kb * blk, blk), :] == segr_ref[0, :, pl.ds(qb * blk, blk)]
        keep = same if kb != qb else same & causal
        mask[1 + i] = jnp.where(keep, 0.0, NEG)


def scores_of(keys, query, mask, half, qb, blk):
    top = dot_nn(keys[: (qb + 1) * blk], query)
    if half == 0:
        diag = top[qb * blk :] + mask[0]
        return diag if qb == 0 else jnp.concatenate([top[:blk], diag], axis=0)
    if qb == 0:
        return top + mask[1]
    return jnp.concatenate([top[:blk] + mask[2], top[blk:] + mask[3]], axis=0)


def one_head(pair_rows, head):
    zero = jnp.zeros((HEAD, pair_rows.shape[1]), pair_rows.dtype)
    rows = pair_rows[head * HEAD : (head + 1) * HEAD]
    return jnp.concatenate([rows, zero] if head == 0 else [zero, rows], axis=0)


def attend_kernel(segc_ref, segr_ref, q_ref, k_ref, v_ref, o_ref, l_ref, mask):
    length = q_ref.shape[2]
    blk = length // 4

    @pl.when(pl.program_id(1) == 0)
    def _():
        fill_masks(segc_ref, segr_ref, mask, blk)

    for half in range(2):
        base = half * 2 * blk
        keys = k_ref[0, :, base : base + 2 * blk].T
        for head in range(2):
            hs = slice(head * HEAD, (head + 1) * HEAD)
            for qb in range(2):
                qs = slice(base + qb * blk, base + (qb + 1) * blk)
                s = scores_of(keys, one_head(q_ref[0, :, qs], head), mask, half, qb, blk)
                top = jnp.max(s, axis=0, keepdims=True)
                p = jnp.exp2(s - top)
                total = jnp.sum(p, axis=0, keepdims=True)
                o = dot_nn(v_ref[0, hs, base : base + (qb + 1) * blk], p.astype(BF))
                o_ref[0, hs, qs] = (o / total).astype(BF)
                l_ref[0, 0, head : head + 1, qs] = top + jnp.log2(total)


def attend_call(segc, segr, q, k, v):
    nseq, width, length = q.shape
    pairs = width // PAIR
    blk = length // 4
    blockspec = pl.BlockSpec((1, PAIR, length), lambda s, h: (s, h, 0))
    return pl.pallas_call(
        attend_kernel,
        grid=(nseq, pairs),
        in_specs=[
            pl.BlockSpec((1, 2 * blk, 1), lambda s, h: (s, 0, 0)),
            pl.BlockSpec((1, 1, 2 * blk), lambda s, h: (s, 0, 0)),
            blockspec, blockspec, blockspec,
        ],
        out_specs=[blockspec, pl.BlockSpec((1, 1, 2, length), lambda s, h: (s, h, 0, 0))],
        out_shape=[
            jax.ShapeDtypeStruct((nseq, width, length), BF),
            jax.ShapeDtypeStruct((nseq, pairs, 2, length), F32),
        ],
        scratch_shapes=[pltpu.VMEM((4, blk, blk), F32)],
        compiler_params=params(40),
        cost_estimate=pl.CostEstimate(
            flops=18 * nseq * 10**9, bytes_accessed=14 * MIB, transcendentals=0
        ),
        name="attend",
    )(segc, segr, q, k, v)


def attend_back_kernel(
    segc_ref, segr_ref, q_ref, k_ref, v_ref, o_ref, g_ref, l_ref, cos_ref, sin_ref,
    gq_ref, gk_ref, gv_ref, sum_ref, mask, turn,
):
    length = q_ref.shape[2]
    blk = length // 4
    hd = HEAD // 2

    @pl.when(pl.program_id(1) == 0)
    def _():
        fill_masks(segc_ref, segr_ref, mask, blk)

    for half in range(2):
        base = half * 2 * blk
        ks = slice(base, base + 2 * blk)
        keys = k_ref[0, :, ks].T
        values = v_ref[0, :, ks].T
        for head in range(2):
            hs = slice(head * HEAD, (head + 1) * HEAD)
            for qb in range(2):
                qs = slice(base + qb * blk, base + (qb + 1) * blk)
                span = slice(base, base + (qb + 1) * blk)
                g = g_ref[0, hs, qs]
                delta = jnp.sum(g.astype(F32) * o_ref[0, hs, qs].astype(F32), axis=0, keepdims=True)
                s = scores_of(keys, one_head(q_ref[0, :, qs], head), mask, half, qb, blk)
                p = jnp.exp2(s - l_ref[0, 0, head : head + 1, qs])
                gp = dot_nn(values[: (qb + 1) * blk], one_head(g_ref[0, :, qs], head))
                ds = (p * (gp - delta)).astype(BF)
                dv = dot_nt(g, p.astype(BF))
                dk = dot_nt(q_ref[0, hs, qs], ds)
                turn[0, hs, qs] = dot_nn(k_ref[0, hs, span], ds)
                if qb == 0:
                    held_k, held_v = dk, dv
                else:
                    turn[1, hs, base : base + blk] = dk[:, :blk] + held_k
                    turn[1, hs, base + blk : base + 2 * blk] = dk[:, blk:]
                    turn[2, hs, base : base + blk] = dv[:, :blk] + held_v
                    turn[2, hs, base + blk : base + 2 * blk] = dv[:, blk:]
    cos, sin = cos_ref[0], sin_ref[0]

    def lanes(v):
        total = v[:, :128]
        for at in range(128, length, 128):
            total = total + v[:, at : at + 128]
        return total

    for part, (out, scale) in enumerate(((gq_ref, HEAD**-0.5), (gk_ref, 1.0 / LOG2E), (gv_ref, 1.0))):
        for head in range(2):
            at = head * HEAD
            u = turn[part, at : at + hd]
            w = turn[part, at + hd : at + HEAD]
            if part < 2:
                u, w = (u * cos + w * sin) * scale, (w * cos - u * sin) * scale
            out[0, at : at + hd, :] = u.astype(BF)
            out[0, at + hd : at + HEAD, :] = w.astype(BF)
            sum_ref[0, part, at : at + hd] = lanes(u)
            sum_ref[0, part, at + hd : at + HEAD] = lanes(w)


def attend_back_call(segc, segr, q, k, v, o, g, lse, cos, sin):
    nseq, width, length = q.shape
    pairs = width // PAIR
    blk = length // 4
    blockspec = pl.BlockSpec((1, PAIR, length), lambda s, h: (s, h, 0))
    tab = pl.BlockSpec((1, HEAD // 2, length), lambda s, h: (s, 0, 0))
    turned = jax.ShapeDtypeStruct((nseq, width, length), BF)
    return pl.pallas_call(
        attend_back_kernel,
        grid=(nseq, pairs),
        in_specs=[
            pl.BlockSpec((1, 2 * blk, 1), lambda s, h: (s, 0, 0)),
            pl.BlockSpec((1, 1, 2 * blk), lambda s, h: (s, 0, 0)),
            blockspec, blockspec, blockspec, blockspec, blockspec,
            pl.BlockSpec((1, 1, 2, length), lambda s, h: (s, h, 0, 0)),
            tab, tab,
        ],
        out_specs=[
            blockspec, blockspec, blockspec,
            pl.BlockSpec((1, 3, PAIR, 128), lambda s, h: (s, 0, h, 0)),
        ],
        out_shape=[turned, turned, turned, jax.ShapeDtypeStruct((nseq, 3, width, 128), F32)],
        scratch_shapes=[pltpu.VMEM((4, blk, blk), F32), pltpu.VMEM((3, PAIR, length), F32)],
        compiler_params=params(48),
        cost_estimate=pl.CostEstimate(
            flops=30 * nseq * 10**9, bytes_accessed=30 * MIB, transcendentals=0
        ),
        name="attend_back",
    )(segc, segr, q, k, v, o, g, lse, cos, sin)


def mlp_kernel(index, count, names, members, *refs):
    ref = dict(zip(names, refs))
    first, last = index == 0, index == count - 1
    rows, width = ref["cot"].shape
    step = pl.program_id(0)
    span = ref["wu"].shape[1]

    def weights(start):
        me, sems = ref["me"][0], ref["sems"]
        if first or last:
            load_pieces(me, [ref["wo", j] for j in range(members)], ref["wo"], sems.at[0], start)
        cols = slice(index * span, (index + 1) * span)
        load_pieces(me, [ref["wu", j] for j in range(members)], ref["wu"], sems.at[1], start, cols)
        pieces = [ref["wd", j] for j in range(members)]
        load_some_pieces(me, pieces, ref["wd"], sems.at[2], start, index, count)

    @pl.when(step == 0)
    def _():
        weights(True)
        weights(False)

    final = pl.num_programs(0) - 1
    acc_u, acc_d, low = ref["acc_u"], ref["acc_d"], ref["low"]
    chunks, _, chunk = acc_u.shape
    alpha = ref["mix"][4]

    @pl.when(step == 0)
    def _():
        acc_u[...] = jnp.zeros_like(acc_u)
        acc_d[...] = jnp.zeros_like(acc_d)
        ref["dbu"][...] = jnp.zeros_like(ref["dbu"])

    cot = ref["cot"][...].astype(F32)
    g_out = cot * alpha
    low[...] = g_out.astype(BF)
    if first:
        hidden = ref["x"][...].astype(F32) + dot_tn(ref["a"][0], ref["wo"][...]) + ref["bo"][...].astype(F32)
        n, _ = norm_parts(hidden)
        ref["hid"][...] = hidden
        ref["act"][...] = (n * ref["gain"][...].astype(F32) + ref["bias"][...].astype(F32)).astype(BF)
        total_up = hidden + ref["bd"][...].astype(F32)
        total_back = None
    else:
        total_up, total_back = ref["up_in"][...], ref["back_in"][...]
    act2 = ref["act"]
    for f in range(chunks):
        cols = slice(f * chunk, (f + 1) * chunk)
        wu = ref["wu"][:, cols]
        wd = ref["wd"][cols, :]
        pre = dot_nn(act2[...], wu) + ref["bu"][:, cols].astype(F32)
        g_act = dot_nt(low[...], wd)
        square = pre * pre
        h = 0.5 + 0.5 * jnp.tanh(pre * (GELU_A + GELU_B * square))
        act = (pre * h).astype(BF)
        slope = h + (pre * (h * (1.0 - h))) * (2.0 * GELU_A + 6.0 * GELU_B * square)
        g_pre = g_act * slope
        ref["dbu"][:, cols] += jnp.sum(g_pre, axis=0, keepdims=True)
        g_low = g_pre.astype(BF)
        total_up = total_up + dot_nn(act, wd)
        more = dot_nt(g_low, wu)
        total_back = more if total_back is None else total_back + more
        acc_d[f] += dot_tn(act, low[...])
        acc_u[f] += dot_tn(act2[...], g_low)
    ref["up"][...] = total_up
    if not last:
        ref["back"][...] = total_back
    else:
        e = total_back
        gain = ref["gain"][...].astype(F32)
        n, r = norm_parts(ref["hid"][...])
        eg = e * gain
        part = r * (
            eg - jnp.mean(eg, axis=-1, keepdims=True) - n * jnp.mean(eg * n, axis=-1, keepdims=True)
        )
        g_hidden = g_out + part
        ref["gh"][...] = g_hidden
        g_low = g_hidden.astype(BF)

        @pl.when(step == 0)
        def _():
            ref["sum"][...] = jnp.zeros_like(ref["sum"])
            ref["acc_o"][...] = jnp.zeros_like(ref["acc_o"])

        for i, term in enumerate((e * n, e, g_hidden, g_out, total_up * cot)):
            ref["sum"][i : i + 1, :] += jnp.sum(term, axis=0, keepdims=True)
        ref["acc_o"][...] += dot_nn(ref["a"][0], g_low)
        ref["ga"][0] = dot_nt(ref["wo"][...], g_low).astype(BF)

    @pl.when(step == final)
    def _():
        for f in range(chunks):
            cols = slice(f * chunk, (f + 1) * chunk)
            for m in range(members):
                own = width // members
                at = f * own
                ref["dw"][m, at : at + own] = acc_u[f, m * own : (m + 1) * own].astype(BF)
            if not last:
                ref["dwd"][cols, :] = acc_d[f].astype(BF)
        if last:
            base, own = chunks * width // members, width // members
            deep = count * span // members
            for m in range(members):
                at = m * deep
                if at < index * span:
                    piece = ref["dwd_in"][at : at + deep]
                else:
                    at -= index * span
                    parts, here = [], at
                    while here < at + deep:
                        f, off = divmod(here, chunk)
                        size = min(chunk - off, at + deep - here)
                        parts.append(acc_d[f, off : off + size].astype(BF))
                        here += size
                    piece = parts[0] if len(parts) == 1 else jnp.concatenate(parts, axis=0)
                ref["dw"][m, base : base + deep] = piece
                rest = base + deep
                ref["dw"][m, rest : rest + own] = ref["acc_o"][m * own : (m + 1) * own].astype(BF)


def mlp_call(index, count, values, pieces):
    tokens, width = values["cot"].shape
    nseq, _, length = values["a"].shape
    members = len(pieces["wu"])
    ff = pieces["wu"][0].shape[1]
    span = ff // count
    rows = length // 2
    chunk = width
    first, last = index == 0, index == count - 1
    row = pl.BlockSpec((rows, width), lambda i: (i, 0))
    col = pl.BlockSpec((1, width, rows), lambda i: (i // 2, 0, i % 2))
    vec = whole((1, width))
    f32row = jax.ShapeDtypeStruct((tokens, width), F32)
    depth = span // chunk * (width // members)
    if last:
        depth += ff // members + width // members
    ins = {
        "me": SMEM,
        "mix": SMEM,
        "cot": row,
        "bu": pl.BlockSpec((1, span), lambda i: (0, index), pipeline_mode=pl.Buffered(1)),
    }
    outs = {
        "dw": (whole((members, depth, width)), jax.ShapeDtypeStruct((members, depth, width), BF)),
        "dbu": (whole((1, span)), jax.ShapeDtypeStruct((1, span), F32)),
        "up": (row, f32row),
    }
    scratch = {
        "acc_u": pltpu.VMEM((span // chunk, width, chunk), F32),
        "acc_d": pltpu.VMEM((span // chunk, chunk, width), F32),
        "low": pltpu.VMEM((rows, width), BF),
        "wu": pltpu.VMEM((width, span), BF),
        "wd": pltpu.VMEM((span, width), BF),
        "sems": pltpu.SemaphoreType.DMA((3, members)),
    }
    if first:
        ins |= {"x": row, "a": col, "bo": vec, "gain": vec, "bias": vec, "bd": vec}
        outs |= {"hid": (row, f32row), "act": (row, jax.ShapeDtypeStruct((tokens, width), BF))}
    else:
        ins |= {"act": row, "up_in": row, "back_in": row}
    if last:
        ins |= {"hid": row, "a": col, "gain": vec, "dwd_in": whole((index * span, width))}
        outs |= {
            "gh": (row, f32row),
            "ga": (col, jax.ShapeDtypeStruct(values["a"].shape, BF)),
            "sum": (whole((8, width)), jax.ShapeDtypeStruct((8, width), F32)),
        }
        scratch |= {"acc_o": pltpu.VMEM((width, width), F32)}
    else:
        outs |= {
            "back": (row, f32row),
            "dwd": (whole((span, width)), jax.ShapeDtypeStruct((span, width), BF)),
        }
    if first or last:
        scratch |= {"wo": pltpu.VMEM((width, width), BF)}
    parts = {
        (name, j): piece
        for name in (("wo", "wu", "wd") if first or last else ("wu", "wd"))
        for j, piece in enumerate(pieces[name])
    }
    names = [*ins, *parts, *outs, *scratch]
    result = pl.pallas_call(
        lambda *refs: mlp_kernel(index, count, names, members, *refs),
        grid=(tokens // rows,),
        in_specs=[*ins.values(), *(ANY for _ in parts)],
        out_specs=[spec for spec, _ in outs.values()],
        out_shape=[shape for _, shape in outs.values()],
        scratch_shapes=list(scratch.values()),
        compiler_params=params(60),
        cost_estimate=pl.CostEstimate(
            flops=6 * tokens * width * (2 * span + width // 2), bytes_accessed=40 * MIB, transcendentals=0
        ),
        name="mlp",
    )(*(values[name] for name in ins), *parts.values())
    return dict(zip(outs, result))


def qkv_grad_kernel(gq_ref, gk_ref, gv_ref, act_ref, dw_ref, acc):
    step = pl.program_id(0)
    last = pl.num_programs(0) - 1
    for part, g in enumerate((gq_ref, gk_ref, gv_ref)):
        term = dot_tt(act_ref[...], g[0])
        acc[part] = jnp.where(step == 0, term, acc[part] + term)

    @pl.when(step == last)
    def _():
        members = dw_ref.shape[0]
        own = acc.shape[1] // members
        for part in range(3):
            for m in range(members):
                dw_ref[m, part * own : (part + 1) * own] = acc[part, m * own : (m + 1) * own].astype(BF)


def qkv_grad_call(members, gq, gk, gv, act):
    tokens, width = act.shape
    nseq, _, length = gq.shape
    col = pl.BlockSpec((1, width, length), lambda s: (s, 0, 0))
    packed = (members, 3 * width // members, width)
    return pl.pallas_call(
        qkv_grad_kernel,
        grid=(nseq,),
        in_specs=[col, col, col, pl.BlockSpec((length, width), lambda s: (s, 0))],
        out_specs=whole(packed),
        out_shape=jax.ShapeDtypeStruct(packed, BF),
        scratch_shapes=[pltpu.VMEM((3, width, width), F32)],
        compiler_params=params(60),
        cost_estimate=pl.CostEstimate(
            flops=2 * tokens * width * 3 * width, bytes_accessed=16 * MIB, transcendentals=0
        ),
        name="qkv_grad",
    )(gq, gk, gv, act)


def first_back_kernel(
    me_ref, shift_ref, gq_ref, gk_ref, gv_ref, x_ref, gh_ref, gain_ref, *refs
):
    pieces, (gx_ref, sum_ref, ring, w_ref, sems) = refs[:-5], refs[-5:]
    length, width = x_ref.shape
    step = pl.program_id(0)
    shift = shift_ref[step]

    @pl.when(step == 0)
    def _():
        load_pieces(me_ref[0], pieces, w_ref, sems, True)
        sum_ref[...] = jnp.zeros_like(sum_ref)
        load_pieces(me_ref[0], pieces, w_ref, sems, False)

    rows = 256
    gain = gain_ref[...].astype(F32)
    sum_n = jnp.zeros((1, width), F32)
    sum_e = jnp.zeros((1, width), F32)
    for at in range(0, length, rows):
        rs = slice(at, at + rows)
        e = sum(
            dot_tt(g[0, :, rs], w_ref[:, i * width : (i + 1) * width])
            for i, g in enumerate((gq_ref, gk_ref, gv_ref))
        )
        n, r = norm_parts(x_ref[rs].astype(F32))
        eg = e * gain
        part = r * (
            eg - jnp.mean(eg, axis=-1, keepdims=True) - n * jnp.mean(eg * n, axis=-1, keepdims=True)
        )
        sum_n += jnp.sum(e * n, axis=0, keepdims=True)
        sum_e += jnp.sum(e, axis=0, keepdims=True)
        ring_put(ring, at, gh_ref[rs] + part)
    sum_ref[0:1] += sum_n
    sum_ref[1:2] += sum_e
    gx_ref[...] = ring_get(ring, length - shift, length)


def first_back_call(me, shift, gq, gk, gv, x, gh, gain, pieces):
    tokens, width = x.shape
    nseq, _, length = gq.shape
    row = pl.BlockSpec((length, width), lambda s: (s, 0))
    col = pl.BlockSpec((1, width, length), lambda s: (s, 0, 0))
    return pl.pallas_call(
        first_back_kernel,
        grid=(nseq,),
        in_specs=[SMEM, SMEM, col, col, col, row, row, whole((1, width)), *(ANY for _ in pieces)],
        out_specs=[row, whole((8, width))],
        out_shape=[
            jax.ShapeDtypeStruct((tokens, width), F32),
            jax.ShapeDtypeStruct((8, width), F32),
        ],
        scratch_shapes=[
            ring_shape(length, width),
            pltpu.VMEM((width, 3 * width), BF),
            pltpu.SemaphoreType.DMA((len(pieces),)),
        ],
        compiler_params=params(60),
        cost_estimate=pl.CostEstimate(
            flops=2 * tokens * width * 3 * width, bytes_accessed=30 * MIB, transcendentals=0
        ),
        name="first_back",
    )(me, shift, gq, gk, gv, x, gh, gain, *pieces)


def states_kernel(mix_ref, e_ref, c_ref, part_ref, ge_ref, sum_ref):
    @pl.when(pl.program_id(0) == 0)
    def _():
        sum_ref[...] = jnp.zeros_like(sum_ref)

    cot = c_ref[...].astype(F32)
    total = None
    for j in range(e_ref.shape[0]):
        e = e_ref[j].astype(F32)
        term = mix_ref[j] * e
        total = term if total is None else total + term
        ge_ref[j] = mix_ref[j] * cot
        sum_ref[j : j + 1] += jnp.sum(e * cot, axis=0, keepdims=True)
    part_ref[...] = total


def states_call(mix, earlier, cot):
    states, tokens, width = earlier.shape
    rows = 256
    row = pl.BlockSpec((rows, width), lambda i: (i, 0))
    stack = pl.BlockSpec((states, rows, width), lambda i: (0, i, 0))
    return pl.pallas_call(
        states_kernel,
        grid=(tokens // rows,),
        in_specs=[SMEM, stack, row],
        out_specs=[row, stack, whole((8, width))],
        out_shape=[
            jax.ShapeDtypeStruct((tokens, width), F32),
            jax.ShapeDtypeStruct(earlier.shape, F32),
            jax.ShapeDtypeStruct((8, width), F32),
        ],
        compiler_params=params(32),
        cost_estimate=pl.CostEstimate(
            flops=16 * tokens * width, bytes_accessed=48 * MIB, transcendentals=0
        ),
        name="states",
    )(mix, earlier, cot)


def mix_kernel(shift_ref, mix_ref, part_ref, b_ref, out_ref, ring):
    length = b_ref.shape[0]
    ring_put(ring, 0, b_ref[...])
    rolled = ring_get(ring, length - shift_ref[pl.program_id(0)], length)
    out_ref[...] = (part_ref[...] + mix_ref[4] * rolled).astype(BF)


def mix_call(shift, mix, part, block_out):
    tokens, width = part.shape
    nseq = shift.shape[0]
    length = tokens // nseq
    row = pl.BlockSpec((length, width), lambda s: (s, 0))
    return pl.pallas_call(
        mix_kernel,
        grid=(nseq,),
        in_specs=[SMEM, SMEM, row, row],
        out_specs=row,
        out_shape=jax.ShapeDtypeStruct((tokens, width), BF),
        scratch_shapes=[ring_shape(length, width)],
        compiler_params=params(48),
        cost_estimate=pl.CostEstimate(
            flops=2 * tokens * width, bytes_accessed=16 * MIB, transcendentals=0
        ),
        name="mix",
    )(shift, mix, part, block_out)


def swap(v, axis, bits):
    size = lax.axis_size(axis)
    return lax.ppermute(v, axis, [(i, i ^ bits) for i in range(size)])


def gather_pieces(v):
    pieces = []
    for k in range(lax.axis_size("shard") // 2):
        far = v if k == 0 else swap(v, "shard", 2 * k)
        pieces += [far, swap(far, "shard", 1)]
    return pieces


def in_order(pieces, mine):
    stack = jnp.stack(pieces)
    return [lax.dynamic_index_in_dim(stack, j ^ mine, 0, keepdims=False) for j in range(len(pieces))]


def total_of(terms):
    total = terms[0].astype(F32)
    for term in terms[1:]:
        total = total + term.astype(F32)
    return total


def reduce_packed(packed):
    members, rows, width = packed.shape
    me, rep = lax.axis_index("shard"), lax.axis_index("rep")
    core, chip = me % 2, me // 2
    groups = members // 2
    pairs = packed.reshape(groups, 2, rows, width)

    def pick(v, at):
        return lax.dynamic_index_in_dim(v, at, 0, keepdims=False)

    other = lax.dynamic_index_in_dim(pairs, 1 - core, 1, keepdims=False)
    near = swap(other, "shard", 1)
    own = lax.dynamic_index_in_dim(pairs, core, 1, keepdims=False)
    terms = [pick(own, chip), pick(near, chip)]
    for k in range(1, groups):
        send = total_of([pick(own, chip ^ k), pick(near, chip ^ k)]).astype(BF)
        terms.append(swap(send, "shard", 2 * k))
    side, group = rep % 2, rep // 2
    count = lax.axis_size("rep") // 2
    terms = [t.reshape(2, rows // 2, width) for t in terms]
    send = total_of([pick(t, 1 - side) for t in terms]).astype(BF)
    terms = [pick(t, side) for t in terms] + [swap(send, "rep", 1)]
    terms = [t.reshape(count, rows // 2 // count, width) for t in terms]
    got = []
    for k in range(1, count):
        send = total_of([pick(t, group ^ k) for t in terms]).astype(BF)
        got.append(swap(send, "rep", 2 * k))
    done = total_of([pick(t, group) for t in terms] + got).astype(BF)
    pieces = [done] + [swap(done, "rep", 2 * k) for k in range(1, count)]
    half = jnp.concatenate(in_order(pieces, group), axis=0)
    return jnp.concatenate(in_order([half, swap(half, "rep", 1)], side), axis=0).astype(F32)


def reduce_small(v):
    for axis in ("shard", "rep"):
        bits = 1
        while bits < lax.axis_size(axis):
            v = v + swap(v, axis, bits)
            bits *= 2
    return v


def shards(
    inputs, earlier, segments, cotangent, mix_weights,
    ln1_gain, ln1_bias, qkv_weight, qkv_bias, out_weight, out_bias,
    ln2_gain, ln2_bias, up_weight, up_bias, down_weight, down_bias,
):
    nseq, length = segments.shape
    width = inputs.shape[1]
    blk = length // 2

    members = lax.axis_size("shard")
    me = lax.axis_index("shard").astype(jnp.int32)
    me_ref = me[None]
    vectors = [ln1_gain, ln1_bias, qkv_bias, out_bias, ln2_gain, ln2_bias, up_bias, down_bias]
    sizes = [v.shape[0] for v in vectors]
    flat = jnp.concatenate(vectors)
    flat = jnp.concatenate([flat, jnp.zeros((-flat.shape[0] % 128,), BF)]).reshape(-1, 128)
    flat = jnp.stack(in_order(gather_pieces(flat), me)).reshape(members, -1)
    full, at = [], 0
    for size in sizes:
        full.append(flat[:, at : at + size].reshape(-1))
        at += size
    g1, b1, bqkv, bo, g2, b2, bu, bd = full
    wqkv, wo, wu, wd = [gather_pieces(v) for v in (qkv_weight, out_weight, up_weight, down_weight)]

    shift = jnp.argmax(segments[:, : length - blk + 1] == segments[:, blk - 1 :], axis=1).astype(jnp.int32)
    rolled = (jnp.arange(length, dtype=jnp.int32)[None] + shift[:, None]) % length
    twice = jnp.concatenate([segments, segments], axis=1)
    others = jnp.stack([lax.dynamic_slice(twice[i], (shift[i] + blk,), (length - blk,)) for i in range(nseq)])
    segc, segr = others[:, :, None], others[:, None, :]
    inv = jnp.exp(jnp.arange(HEAD // 2, dtype=F32) * (-math.log(10000.0) / (HEAD // 2)))
    angles = rolled.astype(F32)[:, None, :] * inv[None, :, None]
    cos, sin = jnp.cos(angles), jnp.sin(angles)

    part, earlier_grad, sums3 = states_call(mix_weights, earlier, cotangent)
    xr, cr, act, q, k, v = qkv_call(
        me_ref, shift, inputs, cotangent, g1[None], b1[None], bqkv.astype(F32)[:, None], cos, sin, wqkv
    )
    o, lse = attend_call(segc, segr, q, k, v)
    values = {
        "me": me_ref, "mix": mix_weights, "x": xr, "cot": cr, "a": o, "bo": bo[None], "gain": g2[None],
        "bias": b2[None], "bu": bu[None], "bd": bd[None],
    }
    pieces = {"wo": wo, "wu": wu, "wd": wd}
    packs, dbus = [], []
    for index in range(MLP_PARTS):
        got = mlp_call(index, MLP_PARTS, values, pieces)
        packs.append(got["dw"])
        dbus.append(got["dbu"])
        values |= {"up_in": got["up"], "back_in": got.get("back"), "dwd_in": got.get("dwd")}
        values |= {name: got[name] for name in ("hid", "act") if name in got}
    block_out, gh, ga, sums2 = (got[name] for name in ("up", "gh", "ga", "sum"))
    gq, gk, gv, sums1 = attend_back_call(segc, segr, q, k, v, o, ga, lse, cos, sin)
    packs.append(qkv_grad_call(members, gq, gk, gv, act))
    output = mix_call(shift, mix_weights, part, block_out)
    input_grad, sums0 = first_back_call(me_ref, shift, gq, gk, gv, xr, gh, g1[None], wqkv)

    first, second, third = [reduce_packed(p) for p in packs]
    own = width // members
    deep = down_weight.shape[0]

    def wide(blocks):
        return jnp.concatenate([blocks[at : at + own] for at in range(0, blocks.shape[0], own)], axis=1)

    more = second.shape[0] - deep - own
    d_up = jnp.concatenate([wide(first), wide(second[:more])], axis=1)
    d_down, d_out, d_qkv = second[more : more + deep], second[more + deep :], wide(third)

    sums = [
        sums0[0], sums0[1], jnp.sum(sums1, axis=(0, 3)).reshape(-1), sums2[2], sums2[0], sums2[1],
        jnp.concatenate(dbus, axis=1)[0], sums2[3],
    ]
    tail = jnp.concatenate([jnp.sum(sums3[:4], axis=1), jnp.sum(sums2[4])[None]])
    small = jnp.concatenate([v.reshape(members, -1) for v in sums], axis=1)
    used = small.shape[1]
    tail = jnp.broadcast_to(tail[None], (members, tail.shape[0]))
    small = jnp.concatenate([small, tail, jnp.zeros((members, -(used + 5) % 128), F32)], axis=1)
    small = reduce_small(small)
    mix_grad = small[0, used : used + 5]
    small = lax.dynamic_index_in_dim(small, me, 0, keepdims=False)
    parts, at = [], 0
    for size in sizes:
        parts.append(small[at : at + size])
        at += size
    return (
        output, input_grad, earlier_grad, mix_grad,
        parts[0], parts[1], d_qkv, parts[2], d_out, parts[3], parts[4], parts[5],
        d_up, parts[6], d_down, parts[7],
    )


def solution(mesh):
    rows, shard = P(("rep", "shard"), None), P("shard")
    mat, deep = P("shard", None), P(None, ("rep", "shard"), None)
    return jax.shard_map(
        shards,
        mesh=mesh,
        in_specs=(
            rows, deep, rows, rows, P(),
            shard, shard, mat, shard, mat, shard, shard, shard, mat, shard, mat, shard,
        ),
        out_specs=(
            rows, rows, deep, P(),
            shard, shard, mat, shard, mat, shard, shard, shard, mat, shard, mat, shard,
        ),
        check_vma=False,
    )
```

time: 1190 us -> 518 us (0.44)
  the two profiles are of different devices: /device:TPU:0 before, /device:TPU:16 now
where the time goes in v1:
time: 518 us; the launch traced here: 508 us
  Pallas kernels  241 us (47%)
  waiting for transfers between devices  143 us (28%)
  local copies, waits for them, and re-layouts  54.1 us (10%)
  starting transfers between devices  45.1 us (9%)
  other arithmetic  20.6 us (4%)
    ppermute x50, waiting for transfers between devices, swap(): return lax.ppermute(v, axis, [(i, i ^ bits) for i in range(size)])  143 us
    pallas_call x2, Pallas kernels, mlp_call(): pl.pallas_call(lambda *refs: mlp_kernel(index, count, names, members, *re...  105 us
    ppermute x50, starting transfers between devices, swap(): return lax.ppermute(v, axis, [(i, i ^ bits) for i in range(size)])  45.1 us
    pallas_call x1, Pallas kernels, attend_back_call(): pl.pallas_call(attend_back_kernel, grid=(nseq, pairs), in_specs=[pl.Block...  37 us
    pallas_call x1, Pallas kernels, attend_call(): pl.pallas_call(attend_kernel, grid=(nseq, pairs), in_specs=[pl.BlockSpec(...  28.4 us
    unnamed x62, local copies, waits for them, and re-layouts  21.6 us
    pallas_call x1, Pallas kernels, first_back_call(): pl.pallas_call(first_back_kernel, grid=(nseq,), in_specs=[SMEM, SMEM, col...  20.8 us
    pallas_call x1, Pallas kernels, qkv_call(): pl.pallas_call(qkv_kernel, grid=(nseq,), in_specs=[SMEM, SMEM, row, row,...  18.6 us
  transfers between devices with their start and end apart: 50, of which 23 were waited for; matrix products, arithmetic and copies ran while one was open for 8% of the time, Pallas kernels for 27%

profile of v1, /device:TPU:16, one launch (start us, length us, event | category | flops | bytes accessed | tf_op | source)
XLA Modules:
  0.0 508.2 jit_solution(5437680044975357490)
XLA Ops:
  0.7 5.5 %concatenate.39 = bf16[2560]{0:T(1024)(128)(2,1)S(1)} concatenate(bf16[192]{0:T(256)(128)(2,1)} %param.22, bf16[192]{0:T(256)(128)(2,1)} %param.23, bf16[576]{0:T(1024)(128)(2,1)} %param.25, bf16[192]{0:T(256)(128)(2,1)} %param.27, bf16[192]{0:T(256)(128)(2,1)} %param.28, bf16[192]{0:T(256)(128)(2,1)} %param.29, bf16[768]{0:T(1024)(128)(2,1)} %param.31, bf16[192]{0:T(256)(128)(2,1)} %param.33, ...), dimensions={0} | concatenate | bytes 10240 | tf_op jit(solution)/shard_map/concatenate | solution.py:794
  6.1 1.5 collective-permute-start.1
  8.4 1.5 collective-permute-start.13
  9.9 1.5 compare_reduce_fusion
  16.0 4.6 copy-done
  20.5 1.9 copy-done.2
  23.1 10.8 %states.1 = (f32[2048,768]{1,0:T(8,128)S(1)}, f32[4,2048,768]{2,1,0:T(8,128)}, f32[8,768]{1,0:T(8,128)S(1)}) custom-call(f32[5]{0:T(128)S(1)} %copy-done.7, bf16[4,2048,768]{2,1,0:T(8,128)(2,1)S(1)} %copy-done, bf16[2048,768]{1,0:T(8,128)(2,1)S(1)} %copy-done.2), custom_call_target="tpu_custom_call" | custom-call | flops 25165824 | bytes 50331648 | tf_op jit(solution)/shard_map/states/pallas_call | solution.py:667
  33.8 2.7 copy-done.1
  37.3 1.8 multiply_sine_fusion
  41.2 2.0 reshape.361.wb_ref
  47.9 1.5 collective-permute-start.7
  49.6 18.6 %qkv.1 = (bf16[2048,768]{1,0:T(8,128)(2,1)}, bf16[2048,768]{1,0:T(8,128)(2,1)}, bf16[2048,768]{1,0:T(8,128)(2,1)}, bf16[2,768,1024]{2,1,0:T(8,128)(2,1)}, bf16[2...) custom-call(s32[1]{0:T(128)} %bitcast.me_ref.refs_0_, s32[2]{0:T(128)} %copy-done.5, bf16[2048,768]{1,0:T(8,128)(2,1)} %x_ref.1, ...), custom_call_target="tpu_custom_call" | custom-call | flops 7247757312 | bytes 20971520 | tf_op jit(solution)/shard_map/qkv/pallas_call | solution.py:160
  68.1 18.6 %collective-permute-done.7.refs_12_.refs_13_ = bf16[192,768]{1,0:T(8,128)(2,1)S(1)} collective-permute-done((bf16[192,768]{1,0:T(8,128)(2,1)S(1)}, bf16[192,768]{1,0:T(8,128)(2,1)S(1)}, u32[]{:S(2)}, u32[]{:S(2)}) %collective-permute-start.7) | collective-permute-done | bytes 294944 | tf_op jit(solution)/shard_map/ppermute | solution.py:714
  87.8 1.9 copy-done.9
  89.7 1.9 copy-done.10
  91.6 1.9 copy-done.11
  93.5 28.4 %attend.1 = (bf16[2,768,1024]{2,1,0:T(8,128)(2,1)S(1)}, f32[2,6,2,1024]{3,2,1,0:T(2,128)S(1)}) custom-call(s32[2,512,1]{2,1,0:T(8,128)S(1)} %copy.36.segc_ref, s32[2,1,512]{2,1,0:T(1,128)S(1)} %broadcast_in_dim.32.segr_ref, bf16[2,768,1024]{2,1,0:T(8,128)(2,1)S(1)} %copy-done.9, bf16[2,768,1024]{2,1,0:T(8,128)(2,1)S(1)} %copy-done.10, ...), custom_call_target="tpu_custom_call" | custom-call | flops 35999997952 | bytes 14680064 | tf_op jit(solution)/shard_map/attend/pallas_call | solution.py:238
  121.9 1.6 copy-done.12
  126.7 47.5 %mlp.2 = (bf16[4,384,768]{2,1,0:T(8,128)(2,1)}, f32[1,1536]{1,0:T(1,128)}, f32[2048,768]{1,0:T(8,128)}, f32[2048,768]{1,0:T(8,128)}, bf16[2048,768]{1,0:T(8,128)...) custom-call(s32[1]{0:T(128)} %bitcast.me_ref.refs_0_, f32[5]{0:T(128)} %mix_ref.3, ...), custom_call_target="tpu_custom_call" | custom-call | flops 32614907904 | bytes 41943040 | tf_op jit(solution)/shard_map/mlp/pallas_call | solution.py:530
  174.2 57.8 %mlp.3 = (bf16[4,1344,768]{2,1,0:T(8,128)(2,1)}, f32[1,1536]{1,0:T(1,128)}, f32[2048,768]{1,0:T(8,128)}, f32[2048,768]{1,0:T(8,128)}, bf16[2,768,1024]{2,1,0:T(8,128)(2,1)}, /*index=5*/f32[8,768]{1,0:T(8,128)}) custom-call(s32[1]{0:T(128)} %bitcast.me_ref.refs_0_, f32[5]{0:T(128)} %mix_ref.3, bf16[2048,768]{1,0:T(8,128)(2,1)} %get-tuple-element.49.refs_2_, ...), custom_call_target="tpu_custom_call" | custom-call | flops 32614907904 | bytes 41943040 | tf_op jit(solution)/shard_map/mlp/pallas_call | solution.py:530
  232.0 4.6 dynamic-slice_bitcast_fusion
  238.1 37.0 %attend_back.1 = (bf16[2,768,1024]{2,1,0:T(8,128)(2,1)}, bf16[2,768,1024]{2,1,0:T(8,128)(2,1)}, bf16[2,768,1024]{2,1,0:T(8,128)(2,1)}, f32[2,3,768,128]{3,2,1,0:T(8,128)S(1)}) custom-call(s32[2,512,1]{2,1,0:T(8,128)S(1)} %copy.36.segc_ref, s32[2,1,512]{2,1,0:T(1,128)S(1)} %broadcast_in_dim.32.segr_ref, bf16[2,768,1024]{2,1,0:T(8,128)(2,1)} %get-tuple-element.51.q_ref, ...), custom_call_target="tpu_custom_call" | custom-call | flops 60000002048 | bytes 31457280 | tf_op jit(solution)/shard_map/attend_back/pallas_call | solution.py:326
  275.1 12.7 %qkv_grad.1 = bf16[4,576,768]{2,1,0:T(8,128)(2,1)} custom-call(bf16[2,768,1024]{2,1,0:T(8,128)(2,1)} %get-tuple-element.63.gq_ref, bf16[2,768,1024]{2,1,0:T(8,128)(2,1)} %get-tuple-element.64.gk_ref, bf16[2,768,1024]{2,1,0:T(8,128)(2,1)} %get-tuple-element.65.gv_ref, bf16[2048,768]{1,0:T(8,128)(2,1)} %get-tuple-element.75.act_ref), custom_call_target="tpu_custom_call" | custom-call | flops 7247757312 | bytes 16777216 | tf_op jit(solution)/shard_map/qkv_grad/pallas_call | solution.py:567
  287.8 2.8 dynamic-slice_bitcast_fusion.1
  290.7 20.8 %first_back.1 = (f32[2048,768]{1,0:T(8,128)}, f32[8,768]{1,0:T(8,128)}) custom-call(s32[1]{0:T(128)} %bitcast.me_ref.refs_0_, s32[2]{0:T(128)} %copy-done.5, bf16[2,768,1024]{2,1,0:T(8,128)(2,1)} %get-tuple-element.63.gq_ref, bf16[2,768,1024]{2,1,0:T(8,128)(2,1)} %get-tuple-element.64.gk_ref, bf16[2,768,1024]{2,1,0:T(8,128)(2,1)} %get-tuple-element.65.gv_ref, ...), custom_call_target="tpu_custom_call" | custom-call | flops 7247757312 | bytes 31457280 | tf_op jit(solution)/shard_map/first_back/pallas_call | solution.py:624
  315.4 1.9 constant_dynamic-slice_fusion.6
  318.1 3.4 collective-permute-done.16
  321.5 1.6 collective-permute-start.17
  323.1 2.4 collective-permute-done.17
  325.5 1.6 collective-permute-start.18
  329.0 2.7 fusion
  331.8 1.5 collective-permute-start.31
  333.8 7.1 %mix.1 = bf16[2048,768]{1,0:T(8,128)(2,1)} custom-call(s32[2]{0:T(128)S(1)} %copy-done.6, f32[5]{0:T(128)S(1)} %copy-done.8, f32[2048,768]{1,0:T(8,128)} %copy-done.1, f32[2048,768]{1,0:T(8,128)} %get-tuple-element.60.b_ref), custom_call_target="tpu_custom_call" | custom-call | flops 3145728 | bytes 16777216 | tf_op jit(solution)/shard_map/mix/pallas_call | solution.py:697
  342.0 2.7 collective-permute-done.41
  344.9 1.6 collective-permute-start.42
  348.5 3.2 collective-permute-done.42
  352.7 2.6 collective-permute-start.45
  355.3 1.4 fusion.1
  357.9 4.6 collective-permute-done.45
  364.5 1.7 collective-permute-start.48
  368.5 2.3 collective-permute-done.48
  370.9 1.7 constant_dynamic-slice_fusion.3
  372.6 16.4 %collective-permute-done.31 = bf16[1344,768]{1,0:T(8,128)(2,1)S(1)} collective-permute-done((bf16[1344,768]{1,0:T(8,128)(2,1)S(1)}, bf16[1344,768]{1,0:T(8,128)(2,1)S(1)}, u32[]{:S(2)}, u32[]{:S(2)}) %collective-permute-start.31) | collective-permute-done | bytes 2064416 | tf_op jit(solution)/shard_map/ppermute | solution.py:714
  389.4 1.6 collective-permute-start.32
  391.6 12.8 %collective-permute-done.21 = bf16[576,768]{1,0:T(8,128)(2,1)S(1)} collective-permute-done((bf16[576,768]{1,0:T(8,128)(2,1)S(1)}, bf16[576,768]{1,0:T(8,128)(2,1)S(1)}, u32[]{:S(2)}, u32[]{:S(2)}) %collective-permute-start.21) | collective-permute-done | bytes 884768 | tf_op jit(solution)/shard_map/ppermute | solution.py:714
  404.6 1.6 collective-permute-start.22
  406.9 11.4 %collective-permute-done.49 = bf16[192,768]{1,0:T(8,128)(2,1)S(1)} collective-permute-done((bf16[192,768]{1,0:T(8,128)(2,1)S(1)}, bf16[192,768]{1,0:T(8,128)(2,1)S(1)}, u32[]{:S(2)}, u32[]{:S(2)}) %collective-permute-start.49) | collective-permute-done | bytes 294944 | tf_op jit(solution)/shard_map/ppermute | solution.py:714
  418.6 4.4 collective-permute-done.22
  424.1 2.7 collective-permute-start.25
  427.4 1.4 collective-permute-start.33
  429.3 1.7 collective-permute-start.35
  431.0 2.8 collective-permute-done.24
  433.8 12.2 %collective-permute-done.25 = bf16[72,768]{1,0:T(8,128)(2,1)S(1)} collective-permute-done((bf16[72,768]{1,0:T(8,128)(2,1)S(1)}, bf16[72,768]{1,0:T(8,128)(2,1)S(1)}, u32[]{:S(2)}, u32[]{:S(2)}) %collective-permute-start.25) | collective-permute-done | bytes 110624 | tf_op jit(solution)/shard_map/ppermute | solution.py:714
  447.1 2.6 collective-permute-start.28
  449.8 15.3 %collective-permute-done.35 = bf16[168,768]{1,0:T(8,128)(2,1)S(1)} collective-permute-done((bf16[168,768]{1,0:T(8,128)(2,1)S(1)}, bf16[168,768]{1,0:T(8,128)(2,1)S(1)}, u32[]{:S(2)}, u32[]{:S(2)}) %collective-permute-start.35) | collective-permute-done | bytes 258080 | tf_op jit(solution)/shard_map/ppermute | solution.py:714
  465.4 2.0 collective-permute-start.37
  467.4 1.5 collective-permute-start.38
  470.0 1.5 collective-permute-start.29
  471.7 5.8 %collective-permute-done.37 = bf16[168,768]{1,0:T(8,128)(2,1)S(1)} collective-permute-done((bf16[168,768]{1,0:T(8,128)(2,1)S(1)}, bf16[168,768]{1,0:T(8,128)(2,1)S(1)}, u32[]{:S(2)}, u32[]{:S(2)}) %collective-permute-start.37) | collective-permute-done | bytes 258080 | tf_op jit(solution)/shard_map/ppermute | solution.py:714
  477.6 4.7 collective-permute-done.38
  482.7 1.5 collective-permute-start.39
  486.2 16.6 %collective-permute-done.39 = bf16[672,768]{1,0:T(8,128)(2,1)S(1)} collective-permute-done((bf16[672,768]{1,0:T(8,128)(2,1)S(1)}, bf16[672,768]{1,0:T(8,128)(2,1)S(1)}, u32[]{:S(2)}, u32[]{:S(2)}) %collective-permute-start.39) | collective-permute-done | bytes 1032224 | tf_op jit(solution)/shard_map/ppermute | solution.py:714
  503.5 1.6 fusion.2
  506.1 1.7 pad_maximum_fusion
  (208 shorter events, 44.4 us)
Async XLA Ops:
  6.1 33.1 %collective-permute-start.1 = (bf16[20,128]{1,0:T(8,128)(2,1)S(1)}, bf16[20,128]{1,0:T(8,128)(2,1)S(1)}, u32[]{:S(2)}, u32[]{:S(2)}) collective-permute-start(bf16[20,128]{1,0:T(8,128)(2,1)S(1)} %bitcast.252), channel_id=1, source_target_pairs={{0,2},{1,3},{2,0},{3,1},{4,6},{5,7},{6,4},{7,5},{8,10},{9,11},{10,... | collective-permute-start | bytes 15368 | tf_op jit(solution)/shard_map/ppermute | solution.py:714
  7.6 32.1 %collective-permute-start = (bf16[20,128]{1,0:T(8,128)(2,1)S(1)}, bf16[20,128]{1,0:T(8,128)(2,1)S(1)}, u32[]{:S(2)}, u32[]{:S(2)}) collective-permute-start(bf16[20,128]{1,0:T(8,128)(2,1)S(1)} %bitcast.253), channel_id=1, source_target_pairs={{0,1},{1,0},{2,3},{3,2},{4,5},{5,4},{6,7},{7,6},{8,9},{9,8},{10,11... | collective-permute-start | bytes 15368 | tf_op jit(solution)/shard_map/ppermute | solution.py:714
  7.6 33.4 %collective-permute-start.4 = (bf16[192,2304]{1,0:T(8,128)(2,1)}, bf16[192,2304]{1,0:T(8,128)(2,1)}, u32[]{:S(2)}, u32[]{:S(2)}) collective-permute-start(bf16[192,2304]{1,0:T(8,128)(2,1)} %refs_0_.3), channel_id=1, source_target_pairs={{0,2},{1,3},{2,0},{3,1},{4,6},{5,7},{6,4},{7,5},{8,10},{9,11},{10,... | collective-permute-start | bytes 2654216 | tf_op jit(solution)/shard_map/ppermute | solution.py:714
  8.1 39.7 %collective-permute-start.3 = (bf16[192,2304]{1,0:T(8,128)(2,1)}, bf16[192,2304]{1,0:T(8,128)(2,1)}, u32[]{:S(2)}, u32[]{:S(2)}) collective-permute-start(bf16[192,2304]{1,0:T(8,128)(2,1)} %refs_0_.3), channel_id=1, source_target_pairs={{0,1},{1,0},{2,3},{3,2},{4,5},{5,4},{6,7},{7,6},{8,9},{9,8},{10,11... | collective-permute-start | bytes 2654216 | tf_op jit(solution)/shard_map/ppermute | solution.py:714
  8.4 79.0 %collective-permute-start.13 = (bf16[768,768]{1,0:T(8,128)(2,1)}, bf16[768,768]{1,0:T(8,128)(2,1)}, u32[]{:S(2)}, u32[]{:S(2)}) collective-permute-start(bf16[768,768]{1,0:T(8,128)(2,1)} %refs_19_.1), channel_id=1, source_target_pairs={{0,2},{1,3},{2,0},{3,1},{4,6},{5,7},{6,4},{7,5},{8,10},{9,11},{10,... | collective-permute-start | bytes 3538952 | tf_op jit(solution)/shard_map/ppermute | solution.py:714
  11.3 25.9 %copy-start.5 = (s32[2]{0:T(128)}, s32[2]{0:T(128)S(1)}, u32[]{:S(2)}) copy-start(s32[2]{0:T(128)S(1)} %get-tuple-element.47.shift_ref) | copy-start | bytes 28
  15.9 4.6 copy-start
  23.1 16.6 %copy-start.21 = (bf16[768,768]{1,0:T(8,128)(2,1)S(1)}, bf16[768,768]{1,0:T(8,128)(2,1)}, u32[]{:S(2)}) copy-start(bf16[768,768]{1,0:T(8,128)(2,1)} %refs_19_.1) | copy-start | bytes 3538948
  23.1 17.4 %copy-start.20 = (bf16[192,3072]{1,0:T(8,128)(2,1)S(1)}, bf16[192,3072]{1,0:T(8,128)(2,1)}, u32[]{:S(2)}) copy-start(bf16[192,3072]{1,0:T(8,128)(2,1)} %refs_15_.1) | copy-start | bytes 3538948
  36.5 11.3 %copy-start.25 = (bf16[192,768]{1,0:T(8,128)(2,1)S(1)}, bf16[192,768]{1,0:T(8,128)(2,1)}, u32[]{:S(2)}) copy-start(bf16[192,768]{1,0:T(8,128)(2,1)} %refs_11_.1) | copy-start | bytes 884740
  39.2 1.2 collective-permute-start.2
  39.7 83.8 %collective-permute-start.12 = (bf16[768,768]{1,0:T(8,128)(2,1)S(1)}, bf16[768,768]{1,0:T(8,128)(2,1)}, u32[]{:S(2)}, u32[]{:S(2)}) collective-permute-start(bf16[768,768]{1,0:T(8,128)(2,1)S(1)} %copy-done.21), channel_id=1, source_target_pairs={{0,1},{1,0},{2,3},{3,2},{4,5},{5,4},{6,7},{7,6},{8,9},{9,8},{10,11... | collective-permute-start | bytes 3538952 | tf_op jit(solution)/shard_map/ppermute | solution.py:714
  40.4 46.8 %collective-permute-start.10 = (bf16[192,3072]{1,0:T(8,128)(2,1)S(1)}, bf16[192,3072]{1,0:T(8,128)(2,1)}, u32[]{:S(2)}, u32[]{:S(2)}) collective-permute-start(bf16[192,3072]{1,0:T(8,128)(2,1)S(1)} %copy-done.20), channel_id=1, source_target_pairs={{0,2},{1,3},{2,0},{3,1},{4,6},{5,7},{6,4},{7,5},{8,10},{9,11},{10,... | collective-permute-start | bytes 3538952 | tf_op jit(solution)/shard_map/ppermute | solution.py:714
  41.0 8.4 %collective-permute-start.5 = (bf16[192,2304]{1,0:T(8,128)(2,1)}, bf16[192,2304]{1,0:T(8,128)(2,1)}, u32[]{:S(2)}, u32[]{:S(2)}) collective-permute-start(bf16[192,2304]{1,0:T(8,128)(2,1)} %collective-permute-done.4.refs_2_), channel_id=1, source_target_pairs={{0,1},{1,0},{2,3},{3,2},{4,5},{5,4},{6,7},{7,6},{8,9},{9,8},{10,11... | collective-permute-start | bytes 2654216 | tf_op jit(solution)/shard_map/ppermute | solution.py:714
  47.9 38.9 %collective-permute-start.7 = (bf16[192,768]{1,0:T(8,128)(2,1)S(1)}, bf16[192,768]{1,0:T(8,128)(2,1)S(1)}, u32[]{:S(2)}, u32[]{:S(2)}) collective-permute-start(bf16[192,768]{1,0:T(8,128)(2,1)S(1)} %copy-done.25), channel_id=1, source_target_pairs={{0,2},{1,3},{2,0},{3,1},{4,6},{5,7},{6,4},{7,5},{8,10},{9,11},{10,... | collective-permute-start | bytes 884744 | tf_op jit(solution)/shard_map/ppermute | solution.py:714
  49.4 37.4 %collective-permute-start.6 = (bf16[192,768]{1,0:T(8,128)(2,1)S(1)}, bf16[192,768]{1,0:T(8,128)(2,1)S(1)}, u32[]{:S(2)}, u32[]{:S(2)}) collective-permute-start(bf16[192,768]{1,0:T(8,128)(2,1)S(1)} %copy-done.25), channel_id=1, source_target_pairs={{0,1},{1,0},{2,3},{3,2},{4,5},{5,4},{6,7},{7,6},{8,9},{9,8},{10,11... | collective-permute-start | bytes 884744 | tf_op jit(solution)/shard_map/ppermute | solution.py:714
  86.8 35.1 %copy-start.26 = (bf16[192,768]{1,0:T(8,128)(2,1)}, bf16[192,768]{1,0:T(8,128)(2,1)S(1)}, u32[]{:S(2)}) copy-start(bf16[192,768]{1,0:T(8,128)(2,1)S(1)} %collective-permute-done.7.refs_12_.refs_13_) | copy-start | bytes 884740
  86.8 36.7 %collective-permute-start.9 = (bf16[192,3072]{1,0:T(8,128)(2,1)S(1)}, bf16[192,3072]{1,0:T(8,128)(2,1)S(1)}, u32[]{:S(2)}, u32[]{:S(2)}) collective-permute-start(bf16[192,3072]{1,0:T(8,128)(2,1)S(1)} %copy-done.20), channel_id=1, source_target_pairs={{0,1},{1,0},{2,3},{3,2},{4,5},{5,4},{6,7},{7,6},{8,9},{9,8},{10,11... | collective-permute-start | bytes 3538952 | tf_op jit(solution)/shard_map/ppermute | solution.py:714
  86.8 35.1 %copy-start.27 = (bf16[192,768]{1,0:T(8,128)(2,1)}, bf16[192,768]{1,0:T(8,128)(2,1)S(1)}, u32[]{:S(2)}) copy-start(bf16[192,768]{1,0:T(8,128)(2,1)S(1)} %collective-permute-done.6.refs_11_.refs_12_) | copy-start | bytes 884740
  86.8 36.7 %collective-permute-start.8 = (bf16[192,768]{1,0:T(8,128)(2,1)S(1)}, bf16[192,768]{1,0:T(8,128)(2,1)S(1)}, u32[]{:S(2)}, u32[]{:S(2)}) collective-permute-start(bf16[192,768]{1,0:T(8,128)(2,1)S(1)} %collective-permute-done.7.refs_12_.refs_13_), channel_id=1, source_target_pairs={{0,1},{1,0},{2,3},{3,2},{4,5},{5,4},{6,7},{7,6},{8,9},{9,8},{10,11... | collective-permute-start | bytes 884744 | tf_op jit(solution)/shard_map/ppermute | solution.py:714
  87.3 37.3 %collective-permute-start.11 = (bf16[192,3072]{1,0:T(8,128)(2,1)}, bf16[192,3072]{1,0:T(8,128)(2,1)S(1)}, u32[]{:S(2)}, u32[]{:S(2)}) collective-permute-start(bf16[192,3072]{1,0:T(8,128)(2,1)} %collective-permute-done.10.refs_16_.refs_17_), channel_id=1, source_target_pairs={{0,1},{1,0},{2,3},{3,2},{4,5},{5,4},{6,7},{7,6},{8,9},{9,8},{10,11... | collective-permute-start | bytes 3538952 | tf_op jit(solution)/shard_map/ppermute | solution.py:714
  87.4 38.3 %collective-permute-start.14 = (bf16[768,768]{1,0:T(8,128)(2,1)}, bf16[768,768]{1,0:T(8,128)(2,1)S(1)}, u32[]{:S(2)}, u32[]{:S(2)}) collective-permute-start(bf16[768,768]{1,0:T(8,128)(2,1)} %collective-permute-done.13.refs_20_.refs_21_), channel_id=1, source_target_pairs={{0,1},{1,0},{2,3},{3,2},{4,5},{5,4},{6,7},{7,6},{8,9},{9,8},{10,11... | collective-permute-start | bytes 3538952 | tf_op jit(solution)/shard_map/ppermute | solution.py:714
  123.5 3.2 copy-start.28
  231.9 4.7 copy-start.14
  236.5 92.5 %collective-permute-start.30 = (bf16[2,1344,768]{2,1,0:T(8,128)(2,1)}, bf16[2,1344,768]{2,1,0:T(8,128)(2,1)}, u32[]{:S(2)}, u32[]{:S(2)}) collective-permute-start(bf16[2,1344,768]{2,1,0:T(8,128)(2,1)} %dynamic-slice_bitcast_fusion), channel_id=1, source_target_pairs={{0,1},{1,0},{2,3},{3,2},{4,5},{5,4},{6,7},{7,6},{8,9},{9,8},{10,11... | collective-permute-start | bytes 12386312 | tf_op jit(solution)/shard_map/ppermute | solution.py:714
  237.7 89.5 %collective-permute-start.40 = (bf16[2,384,768]{2,1,0:T(8,128)(2,1)}, bf16[2,384,768]{2,1,0:T(8,128)(2,1)}, u32[]{:S(2)}, u32[]{:S(2)}) collective-permute-start(bf16[2,384,768]{2,1,0:T(8,128)(2,1)} %dynamic-slice_bitcast_fusion.2), channel_id=1, source_target_pairs={{0,1},{1,0},{2,3},{3,2},{4,5},{5,4},{6,7},{7,6},{8,9},{9,8},{10,11... | collective-permute-start | bytes 3538952 | tf_op jit(solution)/shard_map/ppermute | solution.py:714
  290.6 64.7 %collective-permute-start.20 = (bf16[2,576,768]{2,1,0:T(8,128)(2,1)}, bf16[2,576,768]{2,1,0:T(8,128)(2,1)}, u32[]{:S(2)}, u32[]{:S(2)}) collective-permute-start(bf16[2,576,768]{2,1,0:T(8,128)(2,1)} %dynamic-slice_bitcast_fusion.1), channel_id=1, source_target_pairs={{0,1},{1,0},{2,3},{3,2},{4,5},{5,4},{6,7},{7,6},{8,9},{9,8},{10,11... | collective-permute-start | bytes 5308424 | tf_op jit(solution)/shard_map/ppermute | solution.py:714
  290.7 20.9 %copy-start.17 = (f32[1,1536]{1,0:T(1,128)S(1)}, f32[1,1536]{1,0:T(1,128)}, u32[]{:S(2)}) copy-start(f32[1,1536]{1,0:T(1,128)} %get-tuple-element.72) | copy-start | bytes 18436
  290.7 20.9 %copy-start.18 = (f32[1,1536]{1,0:T(1,128)S(1)}, f32[1,1536]{1,0:T(1,128)}, u32[]{:S(2)}) copy-start(f32[1,1536]{1,0:T(1,128)} %get-tuple-element.73) | copy-start | bytes 18436
  314.9 2.5 collective-permute-start.15
  317.3 5.8 %copy-start.15 = (bf16[4,384,768]{2,1,0:T(8,128)(2,1)S(1)}, bf16[4,384,768]{2,1,0:T(8,128)(2,1)}, u32[]{:S(2)}) copy-start(bf16[4,384,768]{2,1,0:T(8,128)(2,1)} %get-tuple-element.77) | copy-start | bytes 7077892
  317.4 4.1 collective-permute-start.16
  321.5 4.1 collective-permute-start.17
  325.5 7.8 %collective-permute-start.18 = (f32[4,2560]{1,0:T(4,128)S(1)}, f32[4,2560]{1,0:T(4,128)S(1)}, u32[]{:S(2)}, u32[]{:S(2)}) collective-permute-start(f32[4,2560]{1,0:T(4,128)S(1)} %add.506), channel_id=1, source_target_pairs={{0,8},{4,12},{8,0},{12,4},{16,24},{20,28},{24,16},{28,20},{1,9},{5... | collective-permute-start | bytes 122888 | tf_op jit(solution)/shard_map/ppermute | solution.py:714
  328.4 5.4 %copy-start.6 = (s32[2]{0:T(128)S(1)}, s32[2]{0:T(128)}, u32[]{:S(2)}) copy-start(s32[2]{0:T(128)} %copy-done.5) | copy-start | bytes 28
  328.4 5.4 %copy-start.8 = (f32[5]{0:T(128)S(1)}, f32[5]{0:T(128)}, u32[]{:S(2)}) copy-start(f32[5]{0:T(128)} %mix_ref.3) | copy-start | bytes 64
  328.4 16.3 %collective-permute-start.41 = (bf16[384,768]{1,0:T(8,128)(2,1)S(1)}, bf16[384,768]{1,0:T(8,128)(2,1)S(1)}, u32[]{:S(2)}, u32[]{:S(2)}) collective-permute-start(bf16[384,768]{1,0:T(8,128)(2,1)S(1)} %fusion.3), channel_id=1, source_target_pairs={{0,2},{1,3},{2,0},{3,1},{4,6},{5,7},{6,4},{7,5},{8,10},{9,11},{10,... | collective-permute-start | bytes 1769480 | tf_op jit(solution)/shard_map/ppermute | solution.py:714
  331.8 57.2 %collective-permute-start.31 = (bf16[1344,768]{1,0:T(8,128)(2,1)S(1)}, bf16[1344,768]{1,0:T(8,128)(2,1)S(1)}, u32[]{:S(2)}, u32[]{:S(2)}) collective-permute-start(bf16[1344,768]{1,0:T(8,128)(2,1)S(1)} %fusion), channel_id=1, source_target_pairs={{0,2},{1,3},{2,0},{3,1},{4,6},{5,7},{6,4},{7,5},{8,10},{9,11},{10,... | collective-permute-start | bytes 6193160 | tf_op jit(solution)/shard_map/ppermute | solution.py:714
  333.4 7.5 %collective-permute-start.19 = (f32[4,2560]{1,0:T(4,128)S(1)}, f32[4,2560]{1,0:T(4,128)S(1)}, u32[]{:S(2)}, u32[]{:S(2)}) collective-permute-start(f32[4,2560]{1,0:T(4,128)S(1)} %add.507), channel_id=1, source_target_pairs={{0,16},{4,20},{8,24},{12,28},{16,0},{20,4},{24,8},{28,12},{1,17},{... | collective-permute-start | bytes 122888 | tf_op jit(solution)/shard_map/ppermute | solution.py:714
  344.9 6.8 %collective-permute-start.42 = (bf16[192,768]{1,0:T(8,128)(2,1)S(1)}, bf16[192,768]{1,0:T(8,128)(2,1)S(1)}, u32[]{:S(2)}, u32[]{:S(2)}) collective-permute-start(bf16[192,768]{1,0:T(8,128)(2,1)S(1)} %fusion.17), channel_id=1, source_target_pairs={{0,4},{4,0},{8,12},{12,8},{16,20},{20,16},{24,28},{28,24},{1,5},{5... | collective-permute-start | bytes 884744 | tf_op jit(solution)/shard_map/ppermute | solution.py:714
  351.8 5.6 %collective-permute-start.43 = (bf16[48,768]{1,0:T(8,128)(2,1)S(1)}, bf16[48,768]{1,0:T(8,128)(2,1)S(1)}, u32[]{:S(2)}, u32[]{:S(2)}) collective-permute-start(bf16[48,768]{1,0:T(8,128)(2,1)S(1)} %get-tuple-element.101), channel_id=1, source_target_pairs={{0,8},{4,12},{8,0},{12,4},{16,24},{20,28},{24,16},{28,20},{1,9},{5... | collective-permute-start | bytes 221192 | tf_op jit(solution)/shard_map/ppermute | solution.py:714
  352.3 5.6 %collective-permute-start.44 = (bf16[48,768]{1,0:T(8,128)(2,1)S(1)}, bf16[48,768]{1,0:T(8,128)(2,1)S(1)}, u32[]{:S(2)}, u32[]{:S(2)}) collective-permute-start(bf16[48,768]{1,0:T(8,128)(2,1)S(1)} %get-tuple-element.103), channel_id=1, source_target_pairs={{0,16},{4,20},{8,24},{12,28},{16,0},{20,4},{24,8},{28,12},{1,17},{... | collective-permute-start | bytes 221192 | tf_op jit(solution)/shard_map/ppermute | solution.py:714
  352.7 9.9 %collective-permute-start.45 = (bf16[48,768]{1,0:T(8,128)(2,1)S(1)}, bf16[48,768]{1,0:T(8,128)(2,1)S(1)}, u32[]{:S(2)}, u32[]{:S(2)}) collective-permute-start(bf16[48,768]{1,0:T(8,128)(2,1)S(1)} %get-tuple-element.102), channel_id=1, source_target_pairs={{0,24},{4,28},{8,16},{12,20},{16,8},{20,12},{24,0},{28,4},{1,25},{... | collective-permute-start | bytes 221192 | tf_op jit(solution)/shard_map/ppermute | solution.py:714
  356.7 47.7 %collective-permute-start.21 = (bf16[576,768]{1,0:T(8,128)(2,1)S(1)}, bf16[576,768]{1,0:T(8,128)(2,1)S(1)}, u32[]{:S(2)}, u32[]{:S(2)}) collective-permute-start(bf16[576,768]{1,0:T(8,128)(2,1)S(1)} %fusion.1), channel_id=1, source_target_pairs={{0,2},{1,3},{2,0},{3,1},{4,6},{5,7},{6,4},{7,5},{8,10},{9,11},{10,... | collective-permute-start | bytes 2654216 | tf_op jit(solution)/shard_map/ppermute | solution.py:714
  362.6 4.8 collective-permute-start.46
  363.1 5.3 %collective-permute-start.47 = (bf16[48,768]{1,0:T(8,128)(2,1)S(1)}, bf16[48,768]{1,0:T(8,128)(2,1)S(1)}, u32[]{:S(2)}, u32[]{:S(2)}) collective-permute-start(bf16[48,768]{1,0:T(8,128)(2,1)S(1)} %fusion.30), channel_id=1, source_target_pairs={{0,16},{4,20},{8,24},{12,28},{16,0},{20,4},{24,8},{28,12},{1,17},{... | collective-permute-start | bytes 221192 | tf_op jit(solution)/shard_map/ppermute | solution.py:714
  364.5 6.2 %collective-permute-start.48 = (bf16[48,768]{1,0:T(8,128)(2,1)S(1)}, bf16[48,768]{1,0:T(8,128)(2,1)S(1)}, u32[]{:S(2)}, u32[]{:S(2)}) collective-permute-start(bf16[48,768]{1,0:T(8,128)(2,1)S(1)} %fusion.30), channel_id=1, source_target_pairs={{0,24},{4,28},{8,16},{12,20},{16,8},{20,12},{24,0},{28,4},{1,25},{... | collective-permute-start | bytes 221192 | tf_op jit(solution)/shard_map/ppermute | solution.py:714
  389.4 37.5 %collective-permute-start.32 = (bf16[672,768]{1,0:T(8,128)(2,1)S(1)}, bf16[672,768]{1,0:T(8,128)(2,1)S(1)}, u32[]{:S(2)}, u32[]{:S(2)}) collective-permute-start(bf16[672,768]{1,0:T(8,128)(2,1)S(1)} %fusion.4), channel_id=1, source_target_pairs={{0,4},{4,0},{8,12},{12,8},{16,20},{20,16},{24,28},{28,24},{1,5},{5... | collective-permute-start | bytes 3096584 | tf_op jit(solution)/shard_map/ppermute | solution.py:714
  391.1 27.3 %collective-permute-start.49 = (bf16[192,768]{1,0:T(8,128)(2,1)S(1)}, bf16[192,768]{1,0:T(8,128)(2,1)S(1)}, u32[]{:S(2)}, u32[]{:S(2)}) collective-permute-start(bf16[192,768]{1,0:T(8,128)(2,1)S(1)} %get-tuple-element.120), channel_id=1, source_target_pairs={{0,4},{4,0},{8,12},{12,8},{16,20},{20,16},{24,28},{28,24},{1,5},{5... | collective-permute-start | bytes 884744 | tf_op jit(solution)/shard_map/ppermute | solution.py:714
  404.6 18.5 %collective-permute-start.22 = (bf16[288,768]{1,0:T(8,128)(2,1)S(1)}, bf16[288,768]{1,0:T(8,128)(2,1)S(1)}, u32[]{:S(2)}, u32[]{:S(2)}) collective-permute-start(bf16[288,768]{1,0:T(8,128)(2,1)S(1)} %fusion.12), channel_id=1, source_target_pairs={{0,4},{4,0},{8,12},{12,8},{16,20},{20,16},{24,28},{28,24},{1,5},{5... | collective-permute-start | bytes 1327112 | tf_op jit(solution)/shard_map/ppermute | solution.py:714
  423.2 6.1 %collective-permute-start.23 = (bf16[72,768]{1,0:T(8,128)(2,1)S(1)}, bf16[72,768]{1,0:T(8,128)(2,1)S(1)}, u32[]{:S(2)}, u32[]{:S(2)}) collective-permute-start(bf16[72,768]{1,0:T(8,128)(2,1)S(1)} %get-tuple-element.96), channel_id=1, source_target_pairs={{0,8},{4,12},{8,0},{12,4},{16,24},{20,28},{24,16},{28,20},{1,9},{5... | collective-permute-start | bytes 331784 | tf_op jit(solution)/shard_map/ppermute | solution.py:714
  423.7 10.1 %collective-permute-start.24 = (bf16[72,768]{1,0:T(8,128)(2,1)S(1)}, bf16[72,768]{1,0:T(8,128)(2,1)S(1)}, u32[]{:S(2)}, u32[]{:S(2)}) collective-permute-start(bf16[72,768]{1,0:T(8,128)(2,1)S(1)} %get-tuple-element.98), channel_id=1, source_target_pairs={{0,16},{4,20},{8,24},{12,28},{16,0},{20,4},{24,8},{28,12},{1,17},{... | collective-permute-start | bytes 331784 | tf_op jit(solution)/shard_map/ppermute | solution.py:714
  424.1 22.0 %collective-permute-start.25 = (bf16[72,768]{1,0:T(8,128)(2,1)S(1)}, bf16[72,768]{1,0:T(8,128)(2,1)S(1)}, u32[]{:S(2)}, u32[]{:S(2)}) collective-permute-start(bf16[72,768]{1,0:T(8,128)(2,1)S(1)} %get-tuple-element.97), channel_id=1, source_target_pairs={{0,24},{4,28},{8,16},{12,20},{16,8},{20,12},{24,0},{28,4},{1,25},{... | collective-permute-start | bytes 331784 | tf_op jit(solution)/shard_map/ppermute | solution.py:714
  427.4 19.7 %collective-permute-start.33 = (bf16[168,768]{1,0:T(8,128)(2,1)S(1)}, bf16[168,768]{1,0:T(8,128)(2,1)S(1)}, u32[]{:S(2)}, u32[]{:S(2)}) collective-permute-start(bf16[168,768]{1,0:T(8,128)(2,1)S(1)} %get-tuple-element.85), channel_id=1, source_target_pairs={{0,8},{4,12},{8,0},{12,4},{16,24},{20,28},{24,16},{28,20},{1,9},{5... | collective-permute-start | bytes 774152 | tf_op jit(solution)/shard_map/ppermute | solution.py:714
  428.8 21.0 %collective-permute-start.34 = (bf16[168,768]{1,0:T(8,128)(2,1)S(1)}, bf16[168,768]{1,0:T(8,128)(2,1)S(1)}, u32[]{:S(2)}, u32[]{:S(2)}) collective-permute-start(bf16[168,768]{1,0:T(8,128)(2,1)S(1)} %get-tuple-element.87), channel_id=1, source_target_pairs={{0,16},{4,20},{8,24},{12,28},{16,0},{20,4},{24,8},{28,12},{1,17},{... | collective-permute-start | bytes 774152 | tf_op jit(solution)/shard_map/ppermute | solution.py:714
  429.3 35.8 %collective-permute-start.35 = (bf16[168,768]{1,0:T(8,128)(2,1)S(1)}, bf16[168,768]{1,0:T(8,128)(2,1)S(1)}, u32[]{:S(2)}, u32[]{:S(2)}) collective-permute-start(bf16[168,768]{1,0:T(8,128)(2,1)S(1)} %get-tuple-element.86), channel_id=1, source_target_pairs={{0,24},{4,28},{8,16},{12,20},{16,8},{20,12},{24,0},{28,4},{1,25},{... | collective-permute-start | bytes 774152 | tf_op jit(solution)/shard_map/ppermute | solution.py:714
  446.2 21.2 %collective-permute-start.26 = (bf16[72,768]{1,0:T(8,128)(2,1)S(1)}, bf16[72,768]{1,0:T(8,128)(2,1)S(1)}, u32[]{:S(2)}, u32[]{:S(2)}) collective-permute-start(bf16[72,768]{1,0:T(8,128)(2,1)S(1)} %fusion.27), channel_id=1, source_target_pairs={{0,8},{4,12},{8,0},{12,4},{16,24},{20,28},{24,16},{28,20},{1,9},{5... | collective-permute-start | bytes 331784 | tf_op jit(solution)/shard_map/ppermute | solution.py:714
  446.3 22.6 %collective-permute-start.27 = (bf16[72,768]{1,0:T(8,128)(2,1)S(1)}, bf16[72,768]{1,0:T(8,128)(2,1)S(1)}, u32[]{:S(2)}, u32[]{:S(2)}) collective-permute-start(bf16[72,768]{1,0:T(8,128)(2,1)S(1)} %fusion.27), channel_id=1, source_target_pairs={{0,16},{4,20},{8,24},{12,28},{16,0},{20,4},{24,8},{28,12},{1,17},{... | collective-permute-start | bytes 331784 | tf_op jit(solution)/shard_map/ppermute | solution.py:714
  447.1 22.7 %collective-permute-start.28 = (bf16[72,768]{1,0:T(8,128)(2,1)S(1)}, bf16[72,768]{1,0:T(8,128)(2,1)S(1)}, u32[]{:S(2)}, u32[]{:S(2)}) collective-permute-start(bf16[72,768]{1,0:T(8,128)(2,1)S(1)} %fusion.27), channel_id=1, source_target_pairs={{0,24},{4,28},{8,16},{12,20},{16,8},{20,12},{24,0},{28,4},{1,25},{... | collective-permute-start | bytes 331784 | tf_op jit(solution)/shard_map/ppermute | solution.py:714
  465.3 6.4 %collective-permute-start.36 = (bf16[168,768]{1,0:T(8,128)(2,1)S(1)}, bf16[168,768]{1,0:T(8,128)(2,1)S(1)}, u32[]{:S(2)}, u32[]{:S(2)}) collective-permute-start(bf16[168,768]{1,0:T(8,128)(2,1)S(1)} %fusion.11), channel_id=1, source_target_pairs={{0,8},{4,12},{8,0},{12,4},{16,24},{20,28},{24,16},{28,20},{1,9},{5... | collective-permute-start | bytes 774152 | tf_op jit(solution)/shard_map/ppermute | solution.py:714
  465.4 12.1 %collective-permute-start.37 = (bf16[168,768]{1,0:T(8,128)(2,1)S(1)}, bf16[168,768]{1,0:T(8,128)(2,1)S(1)}, u32[]{:S(2)}, u32[]{:S(2)}) collective-permute-start(bf16[168,768]{1,0:T(8,128)(2,1)S(1)} %fusion.11), channel_id=1, source_target_pairs={{0,16},{4,20},{8,24},{12,28},{16,0},{20,4},{24,8},{28,12},{1,17},{... | collective-permute-start | bytes 774152 | tf_op jit(solution)/shard_map/ppermute | solution.py:714
  467.4 14.9 %collective-permute-start.38 = (bf16[168,768]{1,0:T(8,128)(2,1)S(1)}, bf16[168,768]{1,0:T(8,128)(2,1)S(1)}, u32[]{:S(2)}, u32[]{:S(2)}) collective-permute-start(bf16[168,768]{1,0:T(8,128)(2,1)S(1)} %fusion.11), channel_id=1, source_target_pairs={{0,24},{4,28},{8,16},{12,20},{16,8},{20,12},{24,0},{28,4},{1,25},{... | collective-permute-start | bytes 774152 | tf_op jit(solution)/shard_map/ppermute | solution.py:714
  470.0 14.3 %collective-permute-start.29 = (bf16[288,768]{1,0:T(8,128)(2,1)S(1)}, bf16[288,768]{1,0:T(8,128)(2,1)S(1)}, u32[]{:S(2)}, u32[]{:S(2)}) collective-permute-start(bf16[288,768]{1,0:T(8,128)(2,1)S(1)} %get-tuple-element.114), channel_id=1, source_target_pairs={{0,4},{4,0},{8,12},{12,8},{16,20},{20,16},{24,28},{28,24},{1,5},{5... | collective-permute-start | bytes 1327112 | tf_op jit(solution)/shard_map/ppermute | solution.py:714
  482.7 20.1 %collective-permute-start.39 = (bf16[672,768]{1,0:T(8,128)(2,1)S(1)}, bf16[672,768]{1,0:T(8,128)(2,1)S(1)}, u32[]{:S(2)}, u32[]{:S(2)}) collective-permute-start(bf16[672,768]{1,0:T(8,128)(2,1)S(1)} %get-tuple-element.104), channel_id=1, source_target_pairs={{0,4},{4,0},{8,12},{12,8},{16,20},{20,16},{24,28},{28,24},{1,5},{5... | collective-permute-start | bytes 3096584 | tf_op jit(solution)/shard_map/ppermute | solution.py:714
  (15 other events, 25.6 us)

commit v2 on v1

v2 whole, which is shorter than its diff:
```python
import math

import jax
import jax.numpy as jnp
import numpy as np
from jax import lax
from jax.experimental import pallas as pl
from jax.experimental.pallas import tpu as pltpu
from jax.sharding import PartitionSpec as P

HEADS = 12
HEAD = 64
PAIR = 2 * HEAD
EPSILON = 1e-05
LOG2E = math.log2(math.e)
NEG = -1e30
GELU_A = math.sqrt(2.0 / math.pi)
GELU_B = GELU_A * 0.044715
BF = jnp.bfloat16
F32 = jnp.float32
MIB = 1 << 20

COST_SHARE = 1.5


def cost(us):
    return pl.CostEstimate(flops=int(us * COST_SHARE * 1.15e9), bytes_accessed=1024, transcendentals=0)


def dot_nn(a, b):
    return lax.dot_general(a, b, (((1,), (0,)), ((), ())), preferred_element_type=F32)


def dot_nt(a, b):
    return lax.dot_general(a, b, (((1,), (1,)), ((), ())), preferred_element_type=F32)


def dot_tn(a, b):
    return lax.dot_general(a, b, (((0,), (0,)), ((), ())), preferred_element_type=F32)


def dot_tt(a, b):
    return lax.dot_general(a, b, (((0,), (1,)), ((), ())), preferred_element_type=F32)


def params(vmem):
    return pltpu.CompilerParams(vmem_limit_bytes=vmem * MIB)


ANY = pl.BlockSpec(memory_space=pl.ANY)


def load_pieces(me, pieces, target, sems, start, cols=None):
    copies = []
    for j, piece in enumerate(pieces):
        rows = piece.shape[0]
        at = pl.multiple_of((me ^ j) * rows, rows)
        source = piece if cols is None else piece.at[:, cols]
        copies.append(pltpu.make_async_copy(source, target.at[pl.ds(at, rows), :], sems.at[j]))
    for copy in copies:
        if start:
            copy.start()
        else:
            copy.wait()


def pack(target, source, base, own, sides, groups, at):
    rows, cols = own // groups, source.shape[-1] // sides
    for side in range(sides):
        for group in range(groups):
            for j in range(cols // 128):
                here = at + j * rows
                col = side * cols + j * 128
                target[side, group, here : here + rows, :] = source[
                    pl.ds(base + group * rows, rows), col : col + 128
                ].astype(BF)


def pack_all(targets, me, source, own, at):
    for t, target in enumerate(targets):
        count, sides, groups = target.shape[:3]
        for i in range(count):
            place = i if len(targets) == 1 else 2 * i + ((me % 2) ^ t)
            pack(target.at[i], source, pl.multiple_of(place * own, own), own, sides, groups, at)


def unpack(v, at, own, cols):
    sides, groups = v.shape[:2]
    rows, wide = own // groups, cols // sides
    count = wide // 128
    part = v[:, :, at : at + rows * count].reshape(sides, groups, count, rows, 128)
    return part.transpose(1, 3, 0, 2, 4).reshape(own, cols)


def packed_rows(own, cols, sides, groups):
    return own * cols // (128 * sides * groups)


def packed_shapes(form, members, own_cols):
    sides, groups = form
    n = sum(packed_rows(own, cols, sides, groups) for own, cols in own_cols)
    split = 1 if form == (1, 1) else 2
    shape = (members // split, sides, groups, n, 128)
    return [(whole(shape), jax.ShapeDtypeStruct(shape, BF)) for _ in range(split)]


def whole(shape):
    zeros = (0,) * len(shape)
    return pl.BlockSpec(shape, lambda *_: zeros, pipeline_mode=pl.Buffered(1))


SMEM = pl.BlockSpec(memory_space=pltpu.SMEM)


def ring_shape(length, width):
    return pltpu.VMEM((width // 128, 2 * length, 128), F32)


def ring_put(ring, at, value):
    for j in range(ring.shape[0]):
        part = value[:, j * 128 : (j + 1) * 128]
        ring[j, at : at + value.shape[0]] = part
        twin = ring.shape[1] // 2 + at
        ring[j, twin : twin + value.shape[0]] = part


def ring_get(ring, start, rows):
    return jnp.concatenate([ring[j, pl.ds(start, rows), :] for j in range(ring.shape[0])], axis=1)


def norm_parts(v):
    mean = jnp.mean(v, axis=-1, keepdims=True)
    centred = v - mean
    var = jnp.mean(centred * centred, axis=-1, keepdims=True)
    r = lax.rsqrt(var + EPSILON)
    return centred * r, r


ROWS = ("g1", "b1", "bqkv", "bo", "g2", "b2", "bu", "bd")


def vec(ref, name, base=0, share=None):
    row = ROWS.index(name)
    size = share or ref.shape[2] // DEEP_ROWS[name]
    parts = [ref[m, row : row + 1, base : base + size] for m in range(ref.shape[0])]
    return jnp.concatenate(parts, axis=1).astype(F32)


DEEP_ROWS = {"g1": 4, "b1": 4, "bo": 4, "g2": 4, "b2": 4, "bd": 4, "bu": 1}


def column(row):
    return jnp.broadcast_to(row, (128, row.shape[1])).T[:, :1]


def roll_kernel(x_ref, cot_ref, seg_ref, small_ref, tab_ref, *refs):
    shift_ref, xr_ref, cr_ref, act_ref, seg_out, cos_ref, sin_ref, ring = refs[-8:]
    length = x_ref.shape[0]
    half = length // 2
    seg = jnp.broadcast_to(seg_ref[0].astype(F32), (8, length))
    place = lax.broadcasted_iota(jnp.int32, (8, length), 1)
    same = (seg == pltpu.roll(seg, length - (half - 1), 1)) & (place <= half)
    shift = jnp.min(jnp.where(same, place.astype(F32), float(length))).astype(jnp.int32)
    shift_ref[pl.program_id(0)] = shift
    back = lax.rem(length - shift, length)
    seg_out[0] = pltpu.roll(seg, back, 1)[:, half:]
    cos_ref[0] = pltpu.roll(tab_ref[0], back, 1)
    sin_ref[0] = pltpu.roll(tab_ref[1], back, 1)
    for source, target in ((cot_ref, cr_ref), (x_ref, xr_ref)):
        ring_put(ring, 0, source[...].astype(F32))
        target[...] = ring_get(ring, shift, length).astype(BF)
    gain, bias = vec(small_ref, "g1"), vec(small_ref, "b1")
    rows = 256
    for at in range(0, length, rows):
        n, _ = norm_parts(xr_ref[at : at + rows].astype(F32))
        act_ref[at : at + rows] = (n * gain + bias).astype(BF)


def roll_call(x, cot, seg, small, tables, deps):
    tokens, width = x.shape
    nseq, length = seg.shape
    row = pl.BlockSpec((length, width), lambda s: (s, 0))
    tab = pl.BlockSpec((1, HEAD // 2, length), lambda s: (s, 0, 0))
    low = jax.ShapeDtypeStruct((tokens, width), BF)
    turn = jax.ShapeDtypeStruct((nseq, HEAD // 2, length), F32)
    return pl.pallas_call(
        roll_kernel,
        grid=(nseq,),
        in_specs=[
            row, row, pl.BlockSpec((1, 1, length), lambda s: (s, 0, 0)), whole(small.shape), whole(tables.shape),
            *(ANY for _ in deps),
        ],
        out_specs=[SMEM, row, row, row, pl.BlockSpec((1, 8, length // 2), lambda s: (s, 0, 0)), tab, tab],
        out_shape=[
            jax.ShapeDtypeStruct((nseq,), jnp.int32), low, low, low,
            jax.ShapeDtypeStruct((nseq, 8, length // 2), F32), turn, turn,
        ],
        scratch_shapes=[ring_shape(length, width)],
        compiler_params=params(62),
        cost_estimate=cost(10),
        name="roll",
    )(x, cot, seg[:, None, :], small, tables, *deps)


def qkv_kernel(me_ref, act_ref, small_ref, cos_ref, sin_ref, *refs):
    pieces, (q_ref, k_ref, v_ref, w_ref, sems) = refs[:-5], refs[-5:]
    width = act_ref.shape[1]

    @pl.when(pl.program_id(0) == 0)
    def _():
        load_pieces(me_ref[0], pieces, w_ref, sems, True)
        load_pieces(me_ref[0], pieces, w_ref, sems, False)

    half = HEAD // 2
    rows = 256
    bias = vec(small_ref, "bqkv", 0, 3 * width // small_ref.shape[0])
    cos, sin = cos_ref[0], sin_ref[0]
    for part, out in enumerate((q_ref, k_ref, v_ref)):
        scale = LOG2E * HEAD**-0.5 if part == 0 else 1.0
        for base in range(0, width, rows):
            at = part * width + base
            cols = slice(at, at + rows)
            y = dot_tt(w_ref[:, cols], act_ref[...]) + column(bias[:, cols])
            if part == 2:
                out[0, base : base + rows, :] = y.astype(BF)
                continue
            for h in range(0, rows, HEAD):
                u, w = y[h : h + half], y[h + half : h + HEAD]
                a, b = u * cos - w * sin, w * cos + u * sin
                if part == 0:
                    a, b = a * scale, b * scale
                out[0, base + h : base + h + half, :] = a.astype(BF)
                out[0, base + h + half : base + h + HEAD, :] = b.astype(BF)


def qkv_call(me, act, small, cos, sin, pieces):
    tokens, width = act.shape
    nseq, _, length = cos.shape
    col = pl.BlockSpec((1, width, length), lambda s: (s, 0, 0))
    tab = pl.BlockSpec((1, HEAD // 2, length), lambda s: (s, 0, 0))
    turned = jax.ShapeDtypeStruct((nseq, width, length), BF)
    return pl.pallas_call(
        qkv_kernel,
        grid=(nseq,),
        in_specs=[
            SMEM, pl.BlockSpec((length, width), lambda s: (s, 0)), whole(small.shape), tab, tab,
            *(ANY for _ in pieces),
        ],
        out_specs=[col, col, col],
        out_shape=[turned, turned, turned],
        scratch_shapes=[
            pltpu.VMEM((width, 3 * width), BF),
            pltpu.SemaphoreType.DMA((len(pieces),)),
        ],
        compiler_params=params(62),
        cost_estimate=cost(15),
        name="qkv",
    )(me, act, small, cos, sin, *pieces)


def fill_masks(seg_ref, mask, blk):
    row = seg_ref[0, 0:1, :]
    col = column(row)
    kk = lax.broadcasted_iota(jnp.int32, (blk, blk), 0)
    qq = lax.broadcasted_iota(jnp.int32, (blk, blk), 1)
    causal = kk <= qq
    mask[0] = jnp.where(causal, 0.0, NEG)
    for i, (kb, qb) in enumerate(((0, 0), (0, 1), (1, 1))):
        same = col[kb * blk : (kb + 1) * blk] == row[:, qb * blk : (qb + 1) * blk]
        keep = same if kb != qb else same & causal
        mask[1 + i] = jnp.where(keep, 0.0, NEG)


def scores_of(keys, query, mask, half, qb, blk):
    top = dot_nn(keys[: (qb + 1) * blk], query)
    if half == 0:
        diag = top[qb * blk :] + mask[0]
        return diag if qb == 0 else jnp.concatenate([top[:blk], diag], axis=0)
    if qb == 0:
        return top + mask[1]
    return jnp.concatenate([top[:blk] + mask[2], top[blk:] + mask[3]], axis=0)


def one_head(pair_rows, head):
    zero = jnp.zeros((HEAD, pair_rows.shape[1]), pair_rows.dtype)
    rows = pair_rows[head * HEAD : (head + 1) * HEAD]
    return jnp.concatenate([rows, zero] if head == 0 else [zero, rows], axis=0)


def attend_kernel(seg_ref, q_ref, k_ref, v_ref, o_ref, l_ref, mask):
    length = q_ref.shape[2]
    blk = length // 4

    @pl.when(pl.program_id(1) == 0)
    def _():
        fill_masks(seg_ref, mask, blk)

    for half in range(2):
        base = half * 2 * blk
        keys = k_ref[0, :, base : base + 2 * blk].T
        for head in range(2):
            hs = slice(head * HEAD, (head + 1) * HEAD)
            for qb in range(2):
                qs = slice(base + qb * blk, base + (qb + 1) * blk)
                s = scores_of(keys, one_head(q_ref[0, :, qs], head), mask, half, qb, blk)
                top = jnp.max(s, axis=0, keepdims=True)
                p = jnp.exp2(s - top)
                total = jnp.sum(p, axis=0, keepdims=True)
                o = dot_nn(v_ref[0, hs, base : base + (qb + 1) * blk], p.astype(BF))
                o_ref[0, hs, qs] = (o / total).astype(BF)
                l_ref[0, 0, head : head + 1, qs] = top + jnp.log2(total)


def attend_call(seg, q, k, v):
    nseq, width, length = q.shape
    pairs = width // PAIR
    blk = length // 4
    blockspec = pl.BlockSpec((1, PAIR, length), lambda s, h: (s, h, 0))
    return pl.pallas_call(
        attend_kernel,
        grid=(nseq, pairs),
        in_specs=[
            pl.BlockSpec((1, 8, 2 * blk), lambda s, h: (s, 0, 0)),
            blockspec, blockspec, blockspec,
        ],
        out_specs=[blockspec, pl.BlockSpec((1, 1, 2, length), lambda s, h: (s, h, 0, 0))],
        out_shape=[
            jax.ShapeDtypeStruct((nseq, width, length), BF),
            jax.ShapeDtypeStruct((nseq, pairs, 2, length), F32),
        ],
        scratch_shapes=[pltpu.VMEM((4, blk, blk), F32)],
        compiler_params=params(62),
        cost_estimate=cost(30),
        name="attend",
    )(seg, q, k, v)


def attend_back_kernel(
    seg_ref, q_ref, k_ref, v_ref, o_ref, g_ref, l_ref, cos_ref, sin_ref, *refs
):
    gq_ref, gk_ref, gv_ref, sum_ref, mask, turn = refs[-6:]
    length = q_ref.shape[2]
    blk = length // 4
    hd = HEAD // 2

    @pl.when(pl.program_id(1) == 0)
    def _():
        fill_masks(seg_ref, mask, blk)

    for half in range(2):
        base = half * 2 * blk
        ks = slice(base, base + 2 * blk)
        keys = k_ref[0, :, ks].T
        values = v_ref[0, :, ks].T
        for head in range(2):
            hs = slice(head * HEAD, (head + 1) * HEAD)
            for qb in range(2):
                qs = slice(base + qb * blk, base + (qb + 1) * blk)
                span = slice(base, base + (qb + 1) * blk)
                g = g_ref[0, hs, qs]
                delta = jnp.sum(g.astype(F32) * o_ref[0, hs, qs].astype(F32), axis=0, keepdims=True)
                s = scores_of(keys, one_head(q_ref[0, :, qs], head), mask, half, qb, blk)
                p = jnp.exp2(s - l_ref[0, 0, head : head + 1, qs])
                gp = dot_nn(values[: (qb + 1) * blk], one_head(g_ref[0, :, qs], head))
                ds = (p * (gp - delta)).astype(BF)
                dv = dot_nt(g, p.astype(BF))
                dk = dot_nt(q_ref[0, hs, qs], ds)
                turn[0, hs, qs] = dot_nn(k_ref[0, hs, span], ds)
                if qb == 0:
                    held_k, held_v = dk, dv
                else:
                    turn[1, hs, base : base + blk] = dk[:, :blk] + held_k
                    turn[1, hs, base + blk : base + 2 * blk] = dk[:, blk:]
                    turn[2, hs, base : base + blk] = dv[:, :blk] + held_v
                    turn[2, hs, base + blk : base + 2 * blk] = dv[:, blk:]
    cos, sin = cos_ref[0], sin_ref[0]

    ones = jnp.ones((8, length), BF)
    for part, (out, scale) in enumerate(((gq_ref, HEAD**-0.5), (gk_ref, 1.0 / LOG2E), (gv_ref, 1.0))):
        for head in range(2):
            at = head * HEAD
            u = turn[part, at : at + hd]
            w = turn[part, at + hd : at + HEAD]
            if part < 2:
                u, w = (u * cos + w * sin) * scale, (w * cos - u * sin) * scale
            out[0, at : at + hd, :] = u.astype(BF)
            out[0, at + hd : at + HEAD, :] = w.astype(BF)
        sum_ref[0, part] = dot_nt(ones, out[0])


def attend_back_call(seg, q, k, v, o, g, lse, cos, sin, base, pairs, deps, us=15):
    nseq, width, length = q.shape
    blk = length // 4
    source = pl.BlockSpec((1, PAIR, length), lambda s, h: (s, base + h, 0))
    target = pl.BlockSpec((1, PAIR, length), lambda s, h: (s, h, 0))
    tab = pl.BlockSpec((1, HEAD // 2, length), lambda s, h: (s, 0, 0))
    turned = jax.ShapeDtypeStruct((nseq, pairs * PAIR, length), BF)
    return pl.pallas_call(
        attend_back_kernel,
        grid=(nseq, pairs),
        in_specs=[
            pl.BlockSpec((1, 8, 2 * blk), lambda s, h: (s, 0, 0)),
            source, source, source, source, source,
            pl.BlockSpec((1, 1, 2, length), lambda s, h: (s, base + h, 0, 0)),
            tab, tab, *(ANY for _ in deps),
        ],
        out_specs=[
            target, target, target,
            pl.BlockSpec((1, 3, 8, PAIR), lambda s, h: (s, 0, 0, h)),
        ],
        out_shape=[turned, turned, turned, jax.ShapeDtypeStruct((nseq, 3, 8, pairs * PAIR), F32)],
        scratch_shapes=[pltpu.VMEM((4, blk, blk), F32), pltpu.VMEM((3, PAIR, length), F32)],
        compiler_params=params(62),
        cost_estimate=cost(us),
        name="attend_back",
    )(seg, q, k, v, o, g, lse, cos, sin, *deps)


def mlp_kernel(base, first, last, names, members, *refs):
    ref = dict(zip(names, refs))
    rows, width = ref["cot"].shape
    step = pl.program_id(0)
    final = pl.num_programs(0) - 1
    acc_u, acc_d, low = ref["acc_u"], ref["acc_d"], ref["low"]
    span = acc_u.shape[1]
    me, sems = ref["me"][0], ref["sems"]
    share = span // members
    small = ref["small"]

    def weights(start):
        copy = pltpu.make_async_copy(ref["wu_in"], ref["wu"], sems.at[members])
        if start:
            copy.start()
        else:
            copy.wait()
        load_pieces(me, [ref["wd", j] for j in range(members)], ref["wd"], sems, start)

    @pl.when(step == 0)
    def _():
        weights(True)
        acc_u[...] = jnp.zeros_like(acc_u)
        acc_d[...] = jnp.zeros_like(acc_d)
        ref["dbu"][...] = jnp.zeros_like(ref["dbu"])

    alpha = ref["mix"][4]
    cot = ref["cot"][...].astype(F32)
    g_out = cot * alpha
    low[...] = g_out.astype(BF)
    if first:
        hidden = ref["x"][...].astype(F32) + dot_tn(ref["a"][0], ref["wo"][...]) + vec(small, "bo")
        n, _ = norm_parts(hidden)
        ref["hid"][...] = hidden
        ref["act"][...] = (n * vec(small, "g2") + vec(small, "b2")).astype(BF)

    @pl.when(step == 0)
    def _():
        weights(False)

    act2 = ref["act"]
    if first:
        total_up = ref["hid"][...] + vec(small, "bd")
        total_back = None
    else:
        total_up, total_back = ref["up_in"][...], ref["back_in"][...]
    chunk = width + width // 3
    bu = vec(small, "bu", base, share)
    for at in range(0, span, chunk):
        cols = slice(at, at + chunk)
        wu, wd = ref["wu"][:, cols], ref["wd"][cols, :]
        pre = dot_nn(act2[...], wu) + bu[:, cols]
        g_act = dot_nt(low[...], wd)
        square = pre * pre
        h = 0.5 + 0.5 * jnp.tanh(pre * (GELU_A + GELU_B * square))
        act = (pre * h).astype(BF)
        slope = h + (pre * (h * (1.0 - h))) * (2.0 * GELU_A + 6.0 * GELU_B * square)
        g_pre = g_act * slope
        ref["dbu"][:, cols] += jnp.sum(g_pre, axis=0, keepdims=True)
        g_low = g_pre.astype(BF)
        total_up = total_up + dot_nn(act, wd)
        more = dot_nt(g_low, wu)
        total_back = more if total_back is None else total_back + more
        acc_d[cols, :] += dot_tn(act, low[...])
        acc_u[:, cols] += dot_tn(act2[...], g_low)
    ref["up"][...] = total_up
    if not last:
        ref["back"][...] = total_back
    else:
        e = total_back
        gain = vec(small, "g2")
        n, r = norm_parts(ref["hid"][...])
        eg = e * gain
        part = r * (
            eg - jnp.mean(eg, axis=-1, keepdims=True) - n * jnp.mean(eg * n, axis=-1, keepdims=True)
        )
        g_hidden = g_out + part
        ref["gh"][...] = g_hidden
        g_low = g_hidden.astype(BF)

        @pl.when(step == 0)
        def _():
            ref["sum"][...] = jnp.zeros_like(ref["sum"])
            ref["acc_o"][...] = jnp.zeros_like(ref["acc_o"])

        for i, term in enumerate((e * n, e, g_hidden, g_out, total_up * cot)):
            ref["sum"][i : i + 1, :] += jnp.sum(term, axis=0, keepdims=True)
        ref["acc_o"][...] += dot_nn(ref["a"][0], g_low)
        ref["ga"][0] = dot_nt(ref["wo"][...], g_low).astype(BF)

    @pl.when(step == final)
    def _():
        targets = [ref[name] for name in ("dw0", "dw1") if name in ref]
        sides, groups = targets[0].shape[1:3]
        at = 0
        for source in (acc_u, acc_d, ref["acc_o"]) if last else (acc_u, acc_d):
            own = source.shape[0] // members
            pack_all(targets, me, source, own, at)
            at += packed_rows(own, source.shape[1], sides, groups)


def mlp_call(base, share, first, last, values, form, members, deps):
    tokens, width = values["cot"].shape
    nseq, _, length = values["a"].shape
    span = share * members
    rows = length // 2
    row = pl.BlockSpec((rows, width), lambda i: (i, 0))
    col = pl.BlockSpec((1, width, rows), lambda i: (i // 2, 0, i % 2))
    f32row = jax.ShapeDtypeStruct((tokens, width), F32)
    ins = {
        "me": SMEM,
        "mix": SMEM,
        "cot": row,
        "small": whole(values["small"].shape),
        "wu_in": ANY,
    }
    parts = [(width // members, span), (span // members, width)]
    if last:
        parts.append((width // members, width))
    outs = {f"dw{i}": pair for i, pair in enumerate(packed_shapes(form, members, parts))}
    outs |= {
        "dbu": (whole((1, span)), jax.ShapeDtypeStruct((1, span), F32)),
        "up": (row, f32row),
    }
    scratch = {
        "acc_u": pltpu.VMEM((width, span), F32),
        "acc_d": pltpu.VMEM((span, width), F32),
        "low": pltpu.VMEM((rows, width), BF),
        "wu": pltpu.VMEM((width, span), BF),
        "wd": pltpu.VMEM((span, width), BF),
        "sems": pltpu.SemaphoreType.DMA((members + 1,)),
    }
    if first:
        ins |= {"x": row}
        outs |= {"hid": (row, f32row), "act": (row, jax.ShapeDtypeStruct((tokens, width), BF))}
    else:
        ins |= {"act": row, "up_in": row, "back_in": row}
    if last:
        ins |= {"hid": row}
        outs |= {
            "gh": (row, f32row),
            "ga": (col, jax.ShapeDtypeStruct(values["a"].shape, BF)),
            "sum": (whole((8, width)), jax.ShapeDtypeStruct((8, width), F32)),
        }
        scratch |= {"acc_o": pltpu.VMEM((width, width), F32)}
    else:
        outs |= {"back": (row, f32row)}
    if first or last:
        ins |= {"a": col, "wo": whole((width, width))}
    names = [*ins, *(("wd", j) for j in range(members)), *(("dep", i) for i in range(len(deps))), *outs, *scratch]
    result = pl.pallas_call(
        lambda *refs: mlp_kernel(base, first, last, names, members, *refs),
        grid=(tokens // rows,),
        in_specs=[*ins.values(), *(ANY for _ in range(members + len(deps)))],
        out_specs=[spec for spec, _ in outs.values()],
        out_shape=[shape for _, shape in outs.values()],
        scratch_shapes=list(scratch.values()),
        compiler_params=params(62),
        cost_estimate=cost(45),
        name="mlp",
    )(*(values[name] for name in ins), *values["wd"], *deps)
    return dict(zip(outs, result))


def qkv_grad_kernel(parts, deps, me_ref, act_ref, *refs):
    grads, targets, acc = refs[:parts], refs[parts + deps : -1], refs[-1]
    step = pl.program_id(0)
    last = pl.num_programs(0) - 1
    width = act_ref.shape[1]
    at = 0
    for g in grads:
        cols = slice(at, at + g.shape[1])
        at += g.shape[1]
        term = dot_tt(act_ref[...], g[0])
        acc[:, cols] = jnp.where(step == 0, term, acc[:, cols] + term)

    @pl.when(step == last)
    def _():
        split = len(targets)
        pack_all(targets, me_ref[0], acc, width // (targets[0].shape[0] * split), 0)


def turned_spec(v):
    return pl.BlockSpec((1, *v.shape[1:]), lambda s: (s, 0, 0))


def qkv_grad_call(me, grads, act, form, members, deps):
    tokens, width = act.shape
    nseq, _, length = grads[0].shape
    outs = packed_shapes(form, members, [(width // members, 3 * width)])
    return pl.pallas_call(
        lambda *refs: qkv_grad_kernel(len(grads), len(deps), *refs),
        grid=(nseq,),
        in_specs=[
            SMEM, pl.BlockSpec((length, width), lambda s: (s, 0)),
            *(turned_spec(g) for g in grads), *(ANY for _ in deps),
        ],
        out_specs=[spec for spec, _ in outs],
        out_shape=[shape for _, shape in outs],
        scratch_shapes=[pltpu.VMEM((width, 3 * width), F32)],
        compiler_params=params(62),
        cost_estimate=cost(13),
        name="qkv_grad",
    )(me, act, *grads, *deps)


def first_back_kernel(parts, deps, me_ref, shift_ref, x_ref, gh_ref, small_ref, *refs):
    smalls = refs[parts : parts + parts // 3 + 4]
    grads, pieces = refs[:parts], refs[parts + len(smalls) : -5 - deps]
    gx_ref, sum_ref, ring, w_ref, sems = refs[-5:]
    length, width = x_ref.shape
    step = pl.program_id(0)
    shift = shift_ref[step]

    @pl.when(step == 0)
    def _():
        load_pieces(me_ref[0], pieces, w_ref, sems, True)
        sum_ref[...] = jnp.zeros_like(sum_ref)
        heads, (after, up0, up1, states) = smalls[:-4], smalls[-4:]
        for part in range(3):
            row = [sum(g[s, part, 0:1] for s in range(g.shape[0])) for g in heads]
            sum_ref[2 + part : 3 + part] = jnp.concatenate(row, axis=1)
        members = small_ref.shape[0]
        cuts = [v.shape[1] // members for v in (up0, up1)]
        segments = [
            v[:, m * cut : (m + 1) * cut] for m in range(members) for v, cut in zip((up0, up1), cuts)
        ]
        per = width // sum(cuts)
        for i in range(members // per):
            sum_ref[8 + i : 9 + i] = jnp.concatenate(segments[2 * per * i : 2 * per * (i + 1)], axis=1)
        for target, source, place, count in (
            (5, after, 2, 1), (6, after, 0, 2), (12, after, 3, 1), (13, states, 0, 4), (17, after, 4, 1)
        ):
            sum_ref[target : target + count] = source[place : place + count]
        load_pieces(me_ref[0], pieces, w_ref, sems, False)

    rows = 256
    gain = vec(small_ref, "g1")
    sum_n = jnp.zeros((1, width), F32)
    sum_e = jnp.zeros((1, width), F32)
    for at in range(0, length, rows):
        rs = slice(at, at + rows)
        whole_g = jnp.concatenate([g[0, :, rs] for g in grads], axis=0)
        e = dot_tt(whole_g, w_ref[...])
        n, r = norm_parts(x_ref[rs].astype(F32))
        eg = e * gain
        part = r * (
            eg - jnp.mean(eg, axis=-1, keepdims=True) - n * jnp.mean(eg * n, axis=-1, keepdims=True)
        )
        sum_n += jnp.sum(e * n, axis=0, keepdims=True)
        sum_e += jnp.sum(e, axis=0, keepdims=True)
        ring_put(ring, at, gh_ref[rs] + part)
    sum_ref[0:1] += sum_n
    sum_ref[1:2] += sum_e
    gx_ref[...] = ring_get(ring, length - shift, length)


def first_back_call(me, shift, grads, x, gh, small, pieces, smalls, deps):
    tokens, width = x.shape
    nseq, _, length = grads[0].shape
    row = pl.BlockSpec((length, width), lambda s: (s, 0))
    return pl.pallas_call(
        lambda *refs: first_back_kernel(len(grads), len(deps), *refs),
        grid=(nseq,),
        in_specs=[
            SMEM, SMEM, row, row, whole(small.shape),
            *(turned_spec(g) for g in grads), *(whole(v.shape) for v in smalls),
            *(ANY for _ in (*pieces, *deps)),
        ],
        out_specs=[row, whole((24, width))],
        out_shape=[
            jax.ShapeDtypeStruct((tokens, width), F32),
            jax.ShapeDtypeStruct((24, width), F32),
        ],
        scratch_shapes=[
            ring_shape(length, width),
            pltpu.VMEM((width, 3 * width), BF),
            pltpu.SemaphoreType.DMA((len(pieces),)),
        ],
        compiler_params=params(62),
        cost_estimate=cost(20),
        name="first_back",
    )(me, shift, x, gh, small, *grads, *smalls, *pieces, *deps)


def states_kernel(mix_ref, e_ref, c_ref, part_ref, sum_ref):
    @pl.when(pl.program_id(0) == 0)
    def _():
        sum_ref[...] = jnp.zeros_like(sum_ref)

    cot = c_ref[...].astype(F32)
    total = None
    for j in range(e_ref.shape[0]):
        e = e_ref[j].astype(F32)
        term = mix_ref[j] * e
        total = term if total is None else total + term
        sum_ref[j : j + 1] += jnp.sum(e * cot, axis=0, keepdims=True)
    part_ref[...] = total


def states_call(mix, earlier, cot):
    states, tokens, width = earlier.shape
    rows = 256
    row = pl.BlockSpec((rows, width), lambda i: (i, 0))
    stack = pl.BlockSpec((states, rows, width), lambda i: (0, i, 0))
    return pl.pallas_call(
        states_kernel,
        grid=(tokens // rows,),
        in_specs=[SMEM, stack, row],
        out_specs=[row, whole((8, width))],
        out_shape=[
            jax.ShapeDtypeStruct((tokens, width), F32),
            jax.ShapeDtypeStruct((8, width), F32),
        ],
        compiler_params=params(62),
        cost_estimate=cost(11),
        name="states",
    )(mix, earlier, cot)


def spread_kernel(mix_ref, c_ref, *refs):
    out = refs[-1]
    cot = c_ref[...].astype(F32)
    for j in range(out.shape[0]):
        out[j] = mix_ref[j] * cot


def spread_call(states, mix, cot, deps):
    tokens, width = cot.shape
    rows = 256
    return pl.pallas_call(
        spread_kernel,
        grid=(tokens // rows,),
        in_specs=[SMEM, pl.BlockSpec((rows, width), lambda i: (i, 0)), *(ANY for _ in deps)],
        out_specs=pl.BlockSpec((states, rows, width), lambda i: (0, i, 0)),
        out_shape=jax.ShapeDtypeStruct((states, tokens, width), F32),
        compiler_params=params(62),
        cost_estimate=cost(20),
        name="spread",
    )(mix, cot, *deps)


def split_kernel(members, shares, wo_ref, wu_ref, wd_ref, *refs):
    outs = refs[-5:]
    outs[0][...] = wo_ref[...]
    deep = wu_ref.shape[1] // members
    base = 0
    for i, share in enumerate(shares):
        for m in range(members):
            outs[1 + i][:, m * share : (m + 1) * share] = wu_ref[:, m * deep + base : m * deep + base + share]
        outs[3 + i][...] = wd_ref[base : base + share]
        base += share


def split_call(members, shares, wo, wu, wd, deps):
    own = wu.shape[0]
    width = wd.shape[1]
    low = [(own, width), *((own, members * v) for v in shares), *((v, width) for v in shares)]
    full = pl.BlockSpec(memory_space=pltpu.VMEM)
    return pl.pallas_call(
        lambda *refs: split_kernel(members, shares, *refs),
        in_specs=[full, full, full, *(ANY for _ in deps)],
        out_specs=[full] * 5,
        out_shape=[jax.ShapeDtypeStruct(shape, BF) for shape in low],
        compiler_params=params(62),
        cost_estimate=cost(3),
        name="split",
    )(wo, wu, wd, *deps)


def mix_kernel(shift_ref, mix_ref, part_ref, b_ref, *refs):
    out_ref, ring = refs[-2:]
    length = b_ref.shape[0]
    ring_put(ring, 0, b_ref[...])
    rolled = ring_get(ring, length - shift_ref[pl.program_id(0)], length)
    out_ref[...] = (part_ref[...] + mix_ref[4] * rolled).astype(BF)


def mix_call(shift, mix, part, block_out, deps):
    tokens, width = part.shape
    nseq = shift.shape[0]
    length = tokens // nseq
    row = pl.BlockSpec((length, width), lambda s: (s, 0))
    return pl.pallas_call(
        mix_kernel,
        grid=(nseq,),
        in_specs=[SMEM, SMEM, row, row, *(ANY for _ in deps)],
        out_specs=row,
        out_shape=jax.ShapeDtypeStruct((tokens, width), BF),
        scratch_shapes=[ring_shape(length, width)],
        compiler_params=params(62),
        cost_estimate=cost(20),
        name="mix",
    )(shift, mix, part, block_out, *deps)


def swap(v, axis, bits):
    size = lax.axis_size(axis)
    return lax.ppermute(v, axis, [(i, i ^ bits) for i in range(size)])


def gate(arrays, deps):
    count = len(arrays)
    return pl.pallas_call(
        lambda *refs: None,
        in_specs=[ANY] * (count + len(deps)),
        out_specs=[ANY] * count,
        out_shape=[jax.ShapeDtypeStruct(v.shape, v.dtype) for v in arrays],
        input_output_aliases={i: i for i in range(count)},
        cost_estimate=cost(0.3),
        name="gate",
    )(*arrays, *deps)


def far_pieces(v):
    return [v, *(swap(v, "shard", 2 * k) for k in range(1, lax.axis_size("shard") // 2))]


def near_pieces(far, own=None):
    pieces = []
    for k, v in enumerate(far):
        pieces += [v, own if own is not None and k == 0 else swap(v, "shard", 1)]
    return pieces


def gather_pieces(v):
    return near_pieces(far_pieces(v))


def in_order(pieces, mine):
    stack = jnp.stack(pieces)
    return [lax.dynamic_index_in_dim(stack, j ^ mine, 0, keepdims=False) for j in range(len(pieces))]


def total_of(terms):
    total = terms[0].astype(F32)
    for term in terms[1:]:
        total = total + term.astype(F32)
    return total


def chain_start(pair):
    keep, send = pair
    return {"keep": keep, "near": swap(send, "shard", 1)}


def step_parts(kind, chain):
    keep, near = chain["keep"], chain["near"]
    chips, sides, groups, n, lanes = keep.shape
    half = (groups, n, lanes)

    def at(side):
        spec = pl.BlockSpec((1, 1, *half), lambda i, idx: (idx[0], side(idx), 0, 0, 0))
        deep = pl.BlockSpec((1, *half), lambda i, idx: (side(idx), 0, 0, 0))
        return [(keep, spec), (near, spec), *((far, deep) for far in chain["far"])]

    def total(refs, group):
        out = None
        for ref in refs:
            piece = ref[(0,) * (len(ref.shape) - 3) + (group,)].astype(F32)
            out = piece if out is None else out + piece
        return out

    if kind == "x":
        ins = []
        for k in range(1, chips):
            spec = pl.BlockSpec((1, sides, *half), lambda i, idx, k=k: (idx[0] ^ k, 0, 0, 0, 0))
            ins += [(keep, spec), (near, spec)]

        def body(idx, ins, outs):
            for k, out in enumerate(outs):
                out[...] = (ins[2 * k][0].astype(F32) + ins[2 * k + 1][0].astype(F32)).astype(BF)

        return ins, [(sides, *half)] * (chips - 1), body
    if kind == "y":

        def body(idx, ins, outs):
            for g in range(groups):
                outs[0][g] = total(ins, g).astype(BF)

        return at(lambda idx: 1 - idx[1]), [half], body
    if kind == "half":
        ins = [(v, whole(v.shape)) for v in (chain["done"], *chain["zg"])]

        def body(idx, ins, outs):
            for k, ref in enumerate(ins):
                outs[0][idx[2] ^ k] = ref[...]

        return ins, [half], body
    ins = [*at(lambda idx: idx[1]), (chain["yr"], whole(half))]
    if kind == "z":

        def body(idx, ins, outs):
            for k, out in enumerate(outs):
                out[...] = total(ins, idx[2] ^ (k + 1)).astype(BF)

        return ins, [(n, lanes)] * (groups - 1), body
    count = len(ins)
    ins += [(v, whole(v.shape)) for v in chain["zr"]]

    def body(idx, ins, outs):
        out = total(ins[:count], idx[2])
        for ref in ins[count:]:
            out = out + ref[...].astype(F32)
        outs[0][...] = out.astype(BF)

    return ins, [(n, lanes)], body


def step_call(idx, steps, deps):
    plans = [step_parts(kind, chain) for kind, chain in steps]
    ins = [pair for plan in plans for pair in plan[0]]
    outs = [shape for plan in plans for shape in plan[1]]

    def kernel(idx_ref, *refs):
        at, out_at = 0, len(ins) + len(deps)
        for some, shapes, body in plans:
            body(idx_ref, refs[at : at + len(some)], refs[out_at : out_at + len(shapes)])
            at += len(some)
            out_at += len(shapes)

    results = pl.pallas_call(
        kernel,
        grid_spec=pltpu.PrefetchScalarGridSpec(
            num_scalar_prefetch=1,
            grid=(1,),
            in_specs=[*(spec for _, spec in ins), *(ANY for _ in deps)],
            out_specs=[whole(shape) for shape in outs],
        ),
        out_shape=[jax.ShapeDtypeStruct(shape, BF) for shape in outs],
        compiler_params=params(62),
        cost_estimate=cost(3),
        name="_".join(["step", *(kind for kind, _ in steps)]),
    )(idx, *(v for v, _ in ins), *deps)
    at = 0
    for (kind, chain), (_, shapes, _) in zip(steps, plans):
        sends = results[at : at + len(shapes)]
        at += len(shapes)
        far = [swap(v, "shard" if kind == "x" else "rep", 2 * (k + 1)) for k, v in enumerate(sends)] if kind in "xz" else None
        if kind == "x":
            chain["far"] = far
        elif kind == "z":
            chain["zr"] = far
        elif kind == "y":
            chain["yr"] = swap(sends[0], "rep", 1)
        elif kind == "half":
            chain["half"] = sends[0]
            chain["twin"] = swap(sends[0], "rep", 1)
        else:
            chain["done"] = sends[0]
            chain["zg"] = [swap(sends[0], "rep", 2 * k) for k in range(1, lax.axis_size("rep") // 2)]
    return results[0]


def finish_call(idx, chains, plans, shapes, deps):
    ins = [v for chain in chains for v in (chain["half"], chain["twin"])]

    def kernel(idx_ref, *refs):
        outs = refs[len(ins) + len(deps) : len(ins) + len(deps) + len(shapes)]
        scratch = refs[-len(chains) :]
        for c, plan in enumerate(plans):
            both = scratch[c]
            both[idx_ref[1]] = refs[2 * c][...]
            both[1 - idx_ref[1]] = refs[2 * c + 1][...]
            sides, groups = both.shape[:2]
            at = 0
            for out, own, cols, place in plan:
                rows, wide = own // groups, cols // sides
                for j in range(wide // 128):
                    for side in range(sides):
                        for group in range(groups):
                            row, col = place(group * rows, side * wide + j * 128)
                            outs[out][row : row + rows, col : col + 128] = both[
                                side, group, at : at + rows, :
                            ].astype(F32)
                    at += rows

    return pl.pallas_call(
        kernel,
        in_specs=[SMEM, *(pl.BlockSpec(memory_space=pltpu.VMEM) for _ in ins), *(ANY for _ in deps)],
        out_specs=[pl.BlockSpec(memory_space=pltpu.VMEM) for _ in shapes],
        out_shape=[jax.ShapeDtypeStruct(shape, F32) for shape in shapes],
        scratch_shapes=[pltpu.VMEM((2, *chain["half"].shape), BF) for chain in chains],
        compiler_params=params(62),
        cost_estimate=cost(4),
        name="finish",
    )(idx, *ins, *deps)


def reduce_plain(packed):
    flat = packed.reshape(-1, 128)
    return lax.psum(lax.psum_scatter(flat, "shard", scatter_dimension=0, tiled=True), "rep")[None, None]


def reduce_small(v):
    for axis in ("shard", "rep"):
        bits = 1
        while bits < lax.axis_size(axis):
            v = v + swap(v, axis, bits)
            bits *= 2
    return v


def shards(
    inputs, earlier, segments, cotangent, mix_weights,
    ln1_gain, ln1_bias, qkv_weight, qkv_bias, out_weight, out_bias,
    ln2_gain, ln2_bias, up_weight, up_bias, down_weight, down_bias,
):
    nseq, length = segments.shape
    width = inputs.shape[1]
    blk = length // 2
    members, replicas = lax.axis_size("shard"), lax.axis_size("rep")
    me = lax.axis_index("shard").astype(jnp.int32)
    rep = lax.axis_index("rep").astype(jnp.int32)
    side = rep % 2
    me_ref = me[None]
    idx = jnp.stack([me // 2, side, rep // 2])
    own = width // members
    deep = down_weight.shape[0]
    ff = deep * members
    shares = [2 * deep // 3, deep - 2 * deep // 3]
    fits = own % (8 * replicas) == 0 and all(v % (8 * replicas) == 0 and v % 128 == 0 for v in shares)
    form = (2, replicas // 2) if fits else (1, 1)

    wqkv = far_pieces(qkv_weight)
    wqkv_near = swap(qkv_weight, "shard", 1)
    vectors = [ln1_gain, ln1_bias, qkv_bias, out_bias, ln2_gain, ln2_bias, up_bias, down_bias]
    sizes = [v.shape[0] for v in vectors]
    wide = max(sizes)
    small = jnp.stack([jnp.pad(v, (0, wide - v.shape[0])) for v in vectors])
    small = [small, *(swap(small, "shard", k) for k in range(1, members))]
    small = jnp.stack(in_order(small, me))

    part, sums3 = states_call(mix_weights, earlier, cotangent)
    inv = np.exp(np.arange(HEAD // 2) * (-math.log(10000.0) / (HEAD // 2)))
    angles = np.arange(length)[None, :] * inv[:, None]
    tables = jnp.asarray(np.stack([np.cos(angles), np.sin(angles)]), F32)
    shift, xr, cr, act, seg, cos, sin = roll_call(inputs, cotangent, segments, small, tables, [sums3])
    if any(v % 128 for v in (deep, *shares)):

        def shared(v):
            halves = jnp.split(v.reshape(v.shape[0], members, deep), [shares[0]], axis=-1)
            return [h.reshape(v.shape[0], -1) for h in halves]

        pieces = [out_weight, *shared(up_weight), down_weight[: shares[0]], down_weight[shares[0] :]]
    else:
        pieces = split_call(members, shares, out_weight, up_weight, down_weight, [act, *wqkv])
    wo, wu0, wu1 = [lax.all_gather(v, "shard", axis=0, tiled=True) for v in pieces[:3]]
    wd0 = far_pieces(pieces[3])

    wqkv = near_pieces([qkv_weight, *gate(wqkv[1:], [act])], wqkv_near)
    q, k, v = qkv_call(me_ref, act, small, cos, sin, wqkv)
    wd0 = near_pieces(gate(wd0, [q]))
    o, lse = attend_call(seg, q, k, v)
    wd1 = far_pieces(*gate(pieces[4:], [lse]))
    values = {"me": me_ref, "mix": mix_weights, "small": small, "x": xr, "cot": cr, "a": o, "wo": wo}
    got = mlp_call(0, shares[0], True, False, values | {"wu_in": wu0, "wd": wd0}, form, members, [])
    values |= {"up_in": got["up"], "back_in": got["back"], "hid": got["hid"], "act": got["act"]}
    wd1 = near_pieces(gate(wd1, [got["dbu"]]))
    first, dbu = [got[name] for name in ("dw0", "dw1") if name in got], [got["dbu"]]
    spread = [earlier.shape[0], mix_weights, cotangent]
    if fits:
        early = chain_start(first)
        earlier_grad = spread_call(*spread, [first[0]])
        deps = [step_call(idx, [("x", early)], [earlier_grad])]
    else:
        earlier_grad, deps = spread_call(*spread, []), []
    got = mlp_call(
        shares[0], shares[1], False, True, values | {"wu_in": wu1, "wd": wd1}, form, members, deps
    )
    second = [got[name] for name in ("dw0", "dw1") if name in got]
    dbu.append(got["dbu"])
    block_out, gh, ga, sums2 = (got[name] for name in ("up", "gh", "ga", "sum"))

    groups = width // PAIR // 2
    back = [seg, q, k, v, o, ga, lse, cos, sin]

    def up_place(base, share):
        def place(row, col):
            return row, col // share * deep + base + col % share

        return place

    if fits:
        late = chain_start(second)
        t = step_call(idx, [("y", early)], [late["keep"]])
        gs = [attend_back_call(*back, 0, 2, [t])]
        t = step_call(idx, [("z", early), ("x", late)], [gs[0][0]])
        gs.append(attend_back_call(*back, 2, 2, [t]))
        t = step_call(idx, [("sum", early)], [gs[1][0]])
        for i in range(2, groups):
            gs.append(attend_back_call(*back, 2 * i, 2, [t, gs[-1][0]], 0.5))
        early["zg"] = gate(early["zg"], [gs[-1][0]])
        t = step_call(idx, [("y", late)], [gs[-1][0]])
        smalls = [*(g[3] for g in gs), sums2, *dbu, sums3]
        grads = [g[i] for i in range(3) for g in gs]
        pack = qkv_grad_call(me_ref, grads, act, form, members, [t])
        tail = chain_start(pack)
        t = step_call(idx, [("half", early), ("z", late)], [pack[0]])
        output = mix_call(shift, mix_weights, part, block_out, [t])
        t = step_call(idx, [("x", tail)], [output])
        input_grad, sums = first_back_call(me_ref, shift, grads, xr, gh, small, wqkv, smalls, [t])
        t = step_call(idx, [("sum", late), ("y", tail)], [sums])
        t = step_call(idx, [("half", late), ("z", tail)], [])
        t = step_call(idx, [("sum", tail)], [])
        d_up, d_down, d_out = finish_call(
            idx,
            [early, late],
            [
                [
                    (0, own, shares[0] * members, up_place(0, shares[0])),
                    (1, shares[0], width, lambda row, col: (row, col)),
                ],
                [
                    (0, own, shares[1] * members, up_place(shares[0], shares[1])),
                    (1, shares[1], width, lambda row, col: (row + shares[0], col)),
                    (2, own, width, lambda row, col: (row, col)),
                ],
            ],
            [(own, ff), (deep, width), (own, width)],
            [t],
        )
        t = step_call(idx, [("half", tail)], [d_out])
        (d_qkv,) = finish_call(
            idx, [tail], [[(0, own, 3 * width, lambda row, col: (row, col))]], [(own, 3 * width)], []
        )
    else:
        gs = [attend_back_call(*back, 2 * i, 2, []) for i in range(groups)]
        smalls = [*(g[3] for g in gs), sums2, *dbu, sums3]
        grads = [g[i] for i in range(3) for g in gs]
        pack = qkv_grad_call(me_ref, grads, act, form, members, [])
        output = mix_call(shift, mix_weights, part, block_out, [])
        input_grad, sums = first_back_call(me_ref, shift, grads, xr, gh, small, wqkv, smalls, [])
        ups, downs = [], []
        first, second, third = [reduce_plain(p[0]) for p in (first, second, pack)]
        for v, share in ((first, shares[0]), (second, shares[1])):
            at = packed_rows(own, share * members, *v.shape[:2])
            ups.append(unpack(v, 0, own, share * members).reshape(own, members, share))
            downs.append(unpack(v, at, share, width))
            at += packed_rows(share, width, *v.shape[:2])
        d_out = unpack(second, at, own, width).astype(F32)
        d_up = jnp.concatenate(ups, axis=2).reshape(own, -1).astype(F32)
        d_down = jnp.concatenate(downs, axis=0).astype(F32)
        d_qkv = unpack(third, 0, own, 3 * width).astype(F32)

    parts, at = [], 0
    flat = reduce_small(sums).reshape(-1)
    for size in sizes:
        parts.append(lax.dynamic_slice(flat, (at + me * size,), (size,)))
        at += size * members
    mix_grad = jnp.sum(flat[at : at + 5 * width].reshape(5, width), axis=1)
    return (
        output, input_grad, earlier_grad, mix_grad,
        parts[0], parts[1], d_qkv, parts[2], d_out, parts[3], parts[4], parts[5],
        d_up, parts[6], d_down, parts[7],
    )


def solution(mesh):
    rows, shard = P(("rep", "shard"), None), P("shard")
    mat, deep = P("shard", None), P(None, ("rep", "shard"), None)
    return jax.shard_map(
        shards,
        mesh=mesh,
        in_specs=(
            rows, deep, rows, rows, P(),
            shard, shard, mat, shard, mat, shard, shard, shard, mat, shard, mat, shard,
        ),
        out_specs=(
            rows, rows, deep, P(),
            shard, shard, mat, shard, mat, shard, shard, shard, mat, shard, mat, shard,
        ),
        check_vma=False,
    )
```

time: 518 us -> 445 us (0.86)
  the two profiles are of different devices: /device:TPU:16 before, /device:TPU:0 now
where the time goes in v2:
time: 445 us; the launch traced here: 436 us
  Pallas kernels  310 us (70%)
  starting transfers between devices  52.5 us (12%)
  waiting for transfers between devices  36.6 us (8%)
  local copies, waits for them, and re-layouts  20.5 us (5%)
  between operations  14.4 us (3%)
    pallas_call x2, Pallas kernels, mlp_call(): pl.pallas_call(lambda *refs: mlp_kernel(base, first, last, names, members...  101 us
    ppermute x47, starting transfers between devices, swap(): return lax.ppermute(v, axis, [(i, i ^ bits) for i in range(size)])  52.4 us
    pallas_call x3, Pallas kernels, attend_back_call(): pl.pallas_call(attend_back_kernel, grid=(nseq, pairs), in_specs=[pl.Block...  43.8 us
    pallas_call x11, Pallas kernels, step_call(): pl.pallas_call(kernel, grid_spec=pltpu.PrefetchScalarGridSpec(num_scalar_...  38.2 us
    ppermute x47, waiting for transfers between devices, swap(): return lax.ppermute(v, axis, [(i, i ^ bits) for i in range(size)])  35.8 us
    pallas_call x1, Pallas kernels, attend_call(): pl.pallas_call(attend_kernel, grid=(nseq, pairs), in_specs=[pl.BlockSpec(...  30.6 us
    pallas_call x1, Pallas kernels, first_back_call(): pl.pallas_call(lambda *refs: first_back_kernel(len(grads), len(deps), *re...  20.6 us
    pallas_call x1, Pallas kernels, qkv_call(): pl.pallas_call(qkv_kernel, grid=(nseq,), in_specs=[SMEM, pl.BlockSpec((le...  14.8 us
  transfers between devices with their start and end apart: 50, of which 12 were waited for; matrix products, arithmetic and copies ran while one was open for 1% of the time, Pallas kernels for 67%

profile of v2, /device:TPU:0, one launch (start us, length us, event | category | flops | bytes accessed | tf_op | source)
XLA Modules:
  0.0 436.3 jit_solution(15786507305644241779)
XLA Ops:
  12.7 2.4 collective-permute-start.2
  15.8 1.7 collective-permute-start.3
  17.5 10.7 %states.1 = (f32[2048,768]{1,0:T(8,128)}, f32[8,768]{1,0:T(8,128)}) custom-call(f32[5]{0:T(128)} %mix_ref.5, bf16[4,2048,768]{2,1,0:T(8,128)(2,1)} %e_ref.1, bf16[2048,768]{1,0:T(8,128)(2,1)} %c_ref.3), custom_call_target="tpu_custom_call" | custom-call | flops 18975000576 | bytes 1024 | tf_op jit(solution)/shard_map/states/pallas_call | solution.py:724
  29.6 9.6 %roll.1 = (s32[2]{0:T(128)}, bf16[2048,768]{1,0:T(8,128)(2,1)}, bf16[2048,768]{1,0:T(8,128)(2,1)}, bf16[2048,768]{1,0:T(8,128)(2,1)}, f32[2,8,512]{2,1,0:T(8,128...) custom-call(bf16[2048,768]{1,0:T(8,128)(2,1)} %x_ref.1, bf16[2048,768]{1,0:T(8,128)(2,1)} %c_ref.3, ...), custom_call_target="tpu_custom_call" | custom-call | flops 17250000896 | bytes 1024 | tf_op jit(solution)/shard_map/roll/pallas_call | solution.py:186
  40.1 3.3 split.1
  45.7 1.3 collective-permute-done.4.refs_1_.refs_22_
  47.0 1.3 collective-permute-done.5.refs_3_.refs_24_
  48.3 14.8 %qkv.1 = (bf16[2,768,1024]{2,1,0:T(8,128)(2,1)}, bf16[2,768,1024]{2,1,0:T(8,128)(2,1)}, bf16[2,768,1024]{2,1,0:T(8,128)(2,1)}) custom-call(s32[1]{0:T(128)} %bitcast.4.me_ref.refs_0_, bf16[2048,768]{1,0:T(8,128)(2,1)} %get-tuple-element.93.refs_3_.refs_1_.act_ref, bf16[4,8,768]{2,1,0:T(8,128)(2,1)} %pad_maximum_fusion.1.small_ref.refs_3_.refs_4_, ...), custom_call_target="tpu_custom_call" | custom-call | flops 25874999296 | bytes 1024 | tf_op jit(solution)/shard_map/qkv/pallas_call | solution.py:242
  63.1 8.2 %collective-permute-done.6.refs_1_ = bf16[512,768]{1,0:T(8,128)(2,1)S(1)} collective-permute-done((bf16[512,768]{1,0:T(8,128)(2,1)S(1)}, bf16[512,768]{1,0:T(8,128)(2,1)S(1)}, u32[]{:S(2)}, u32[]{:S(2)}) %collective-permute-start.6) | collective-permute-done | bytes 786464 | tf_op jit(solution)/shard_map/ppermute | solution.py:817
  72.7 30.6 %attend.1 = (bf16[2,768,1024]{2,1,0:T(8,128)(2,1)}, f32[2,6,2,1024]{3,2,1,0:T(2,128)}) custom-call(f32[2,8,512]{2,1,0:T(8,128)} %get-tuple-element.97.seg_ref, bf16[2,768,1024]{2,1,0:T(8,128)(2,1)} %get-tuple-element.100.q_ref.refs_2_, bf16[2,768,1024]{2,1,0:T(8,128)(2,1)} %get-tuple-element.101.k_ref, bf16[2,768,1024]{2,1,0:T(8,128)(2,1)} %get-tuple-element.102.v_ref), custom_call_target="tpu_custom_call" | custom-call | flops 51749998592 | bytes 1024 | tf_op jit(solution)/shard_map/attend/pallas_call | solution.py:319
  104.9 59.1 %mlp.2 = (bf16[2,2,4,768,128]{4,3,2,1,0:T(8,128)(2,1)}, bf16[2,2,4,768,128]{4,3,2,1,0:T(8,128)(2,1)}, f32[1,2048]{1,0:T(1,128)}, f32[2048,768]{1,0:T(8,128)}, f3...) custom-call(s32[1]{0:T(128)} %bitcast.4.me_ref.refs_0_, f32[5]{0:T(128)} %mix_ref.5, ...), custom_call_target="tpu_custom_call" | custom-call | flops 77624999936 | bytes 1024 | tf_op jit(solution)/shard_map/mlp/pallas_call | solution.py:569
  165.2 10.4 %spread.1.refs_2_ = f32[4,2048,768]{2,1,0:T(8,128)} custom-call(f32[5]{0:T(128)} %mix_ref.5, bf16[2048,768]{1,0:T(8,128)(2,1)} %c_ref.3, bf16[2,2,4,768,128]{4,3,2,1,0:T(8,128)(2,1)} %get-tuple-element.117.refs_0_), custom_call_target="tpu_custom_call" | custom-call | flops 34500001792 | bytes 1024 | tf_op jit(solution)/shard_map/spread/pallas_call | solution.py:749
  175.6 4.0 step_x.2.refs_15_
  179.6 1.6 collective-permute-start.13
  182.0 42.4 %mlp.3 = (bf16[2,2,4,528,128]{4,3,2,1,0:T(8,128)(2,1)}, bf16[2,2,4,528,128]{4,3,2,1,0:T(8,128)(2,1)}, f32[1,1024]{1,0:T(1,128)}, f32[2048,768]{1,0:T(8,128)}, f3...) custom-call(s32[1]{0:T(128)} %bitcast.4.me_ref.refs_0_, f32[5]{0:T(128)} %mix_ref.5, ...), custom_call_target="tpu_custom_call" | custom-call | flops 77624999936 | bytes 1024 | tf_op jit(solution)/shard_map/mlp/pallas_call | solution.py:569
  224.7 1.1 copy-done.6
  225.9 3.4 step_y.2.refs_0_
  229.3 1.5 collective-permute-start.14
  230.8 14.9 %attend_back.3 = (bf16[2,256,1024]{2,1,0:T(8,128)(2,1)}, bf16[2,256,1024]{2,1,0:T(8,128)(2,1)}, bf16[2,256,1024]{2,1,0:T(8,128)(2,1)}, f32[2,3,8,256]{3,2,1,0:T(8,128)}) custom-call(f32[2,8,512]{2,1,0:T(8,128)} %get-tuple-element.97.seg_ref, bf16[2,768,1024]{2,1,0:T(8,128)(2,1)} %get-tuple-element.100.q_ref.refs_2_, ...), custom_call_target="tpu_custom_call" | custom-call | flops 25874999296 | bytes 1024 | tf_op jit(solution)/shard_map/attend_back/pallas_call | solution.py:398
  245.7 3.5 collective-permute-done.14.refs_3_
  250.1 4.7 %step_z_x.1 = (bf16[768,128]{1,0:T(8,128)(2,1)}, bf16[768,128]{1,0:T(8,128)(2,1)}, bf16[768,128]{1,0:T(8,128)(2,1)}, bf16[2,4,528,128]{3,2,1,0:T(8,128)(2,1)}) custom-call(s32[3]{0:T(128)} %pad_add_fusion.idx_ref, bf16[2,2,4,768,128]{4,3,2,1,0:T(8,128)(2,1)} %get-tuple-element.117.refs_0_, bf16[2,2,4,768,128]{4,3,2,1,0:T(8,128)(2,1)} %collective-permute-done.12.refs_1_, ...), custom_call_target="tpu_custom_call" | custom-call | flops 5175000064 | bytes 1024 | tf_op jit(solution)/shard_map/step_z_x/pallas_call | solution.py:940
  254.8 1.6 collective-permute-start.16
  256.4 2.7 collective-permute-start.17
  259.6 14.5 %attend_back.4 = (bf16[2,256,1024]{2,1,0:T(8,128)(2,1)}, bf16[2,256,1024]{2,1,0:T(8,128)(2,1)}, bf16[2,256,1024]{2,1,0:T(8,128)(2,1)}, f32[2,3,8,256]{3,2,1,0:T(8,128)}) custom-call(f32[2,8,512]{2,1,0:T(8,128)} %get-tuple-element.97.seg_ref, bf16[2,768,1024]{2,1,0:T(8,128)(2,1)} %get-tuple-element.100.q_ref.refs_2_, ...), custom_call_target="tpu_custom_call" | custom-call | flops 25874999296 | bytes 1024 | tf_op jit(solution)/shard_map/attend_back/pallas_call | solution.py:398
  274.9 3.5 step_sum.2.refs_0_
  278.4 2.6 collective-permute-start.19
  281.0 1.8 collective-permute-start.20
  283.5 14.5 %attend_back.5 = (bf16[2,256,1024]{2,1,0:T(8,128)(2,1)}, bf16[2,256,1024]{2,1,0:T(8,128)(2,1)}, bf16[2,256,1024]{2,1,0:T(8,128)(2,1)}, f32[2,3,8,256]{3,2,1,0:T(8,128)}) custom-call(f32[2,8,512]{2,1,0:T(8,128)} %get-tuple-element.97.seg_ref, bf16[2,768,1024]{2,1,0:T(8,128)(2,1)} %get-tuple-element.100.q_ref.refs_2_, ...), custom_call_target="tpu_custom_call" | custom-call | flops 862499968 | bytes 1024 | tf_op jit(solution)/shard_map/attend_back/pallas_call | solution.py:398
  298.8 1.0 copy-done.7
  299.8 3.0 step_y.3.refs_11_
  302.8 1.5 collective-permute-start.23
  304.3 12.9 %qkv_grad.1 = (bf16[2,2,4,432,128]{4,3,2,1,0:T(8,128)(2,1)}, bf16[2,2,4,432,128]{4,3,2,1,0:T(8,128)(2,1)}) custom-call(s32[1]{0:T(128)} %bitcast.4.me_ref.refs_0_, bf16[2048,768]{1,0:T(8,128)(2,1)} %get-tuple-element.93.refs_3_.refs_1_.act_ref, bf16[2,256,1024]{2,1,0:T(8,128)(2,1)} %get-tuple-element.123.refs_6_.refs_2_.refs_5_, ...), custom_call_target="tpu_custom_call" | custom-call | flops 22424999936 | bytes 1024 | tf_op jit(solution)/shard_map/qkv_grad/pallas_call | solution.py:609
  317.2 3.6 step_half_z.2
  320.8 2.1 collective-permute-start.31
  323.0 1.6 collective-permute-start.32
  324.5 1.1 collective-permute-start.33
  325.6 7.1 %mix.1.refs_2_ = bf16[2048,768]{1,0:T(8,128)(2,1)} custom-call(s32[2]{0:T(128)} %get-tuple-element.90.shift_ref.refs_1_, f32[5]{0:T(128)} %mix_ref.5, f32[2048,768]{1,0:T(8,128)} %get-tuple-element.91.part_ref, f32[2048,768]{1,0:T(8,128)} %get-tuple-element.119.b_ref, bf16[4,768,128]{2,1,0:T(8,128)(2,1)} %get-tuple-element.140.refs_0_), custom_call_target="tpu_custom_call" | custom-call | flops 34500001792 | bytes 1024 | tf_op jit(solution)/shard_map/mix/pallas_call | solution.py:802
  332.6 1.2 copy-done.5
  333.8 3.2 step_x.3.refs_25_
  337.7 20.6 %first_back.1 = (f32[2048,768]{1,0:T(8,128)}, f32[24,768]{1,0:T(8,128)}) custom-call(s32[1]{0:T(128)} %bitcast.4.me_ref.refs_0_, s32[2]{0:T(128)} %get-tuple-element.90.shift_ref.refs_1_, bf16[2048,768]{1,0:T(8,128)(2,1)} %get-tuple-element.96.refs_5_.refs_2_, f32[2048,768]{1,0:T(8,128)} %get-tuple-element.141.refs_3_, ...), custom_call_target="tpu_custom_call" | custom-call | flops 34500001792 | bytes 1024 | tf_op jit(solution)/shard_map/first_back/pallas_call | solution.py:680
  359.7 3.9 step_sum_y.1
  364.7 3.2 collective-permute-start.36
  368.6 1.3 collective-permute-done.25
  369.8 1.4 collective-permute-start.44
  371.3 1.1 collective-permute-start.26
  372.4 5.7 %collective-permute-done.36.refs_2_ = bf16[528,128]{1,0:T(8,128)(2,1)} collective-permute-done((bf16[528,128]{1,0:T(8,128)(2,1)}, bf16[528,128]{1,0:T(8,128)(2,1)}, u32[]{:S(2)}, u32[]{:S(2)}) %collective-permute-start.36) | collective-permute-done | bytes 135200 | tf_op jit(solution)/shard_map/ppermute | solution.py:817
  378.1 3.3 step_half_z.3
  381.4 2.0 collective-permute-start.38
  384.3 1.4 collective-permute-start.40
  385.8 1.4 collective-permute-start.45
  387.2 1.4 collective-permute-start.27
  388.7 5.1 %collective-permute-done.39.refs_5_ = bf16[432,128]{1,0:T(8,128)(2,1)} collective-permute-done((bf16[432,128]{1,0:T(8,128)(2,1)}, bf16[432,128]{1,0:T(8,128)(2,1)}, u32[]{:S(2)}, u32[]{:S(2)}) %collective-permute-start.39) | collective-permute-done | bytes 110624 | tf_op jit(solution)/shard_map/ppermute | solution.py:817
  393.7 2.9 step_sum.3.refs_4_.refs_0_
  396.7 1.8 collective-permute-start.41
  399.2 1.8 collective-permute-start.43
  401.0 3.3 collective-permute-done.45.refs_3_
  404.4 4.4 %finish.2 = (f32[192,3072]{1,0:T(8,128)}, f32[768,768]{1,0:T(8,128)}, f32[192,768]{1,0:T(8,128)}) custom-call(s32[3]{0:T(128)} %pad_add_fusion.idx_ref, bf16[4,768,128]{2,1,0:T(8,128)(2,1)} %get-tuple-element.140.refs_0_, bf16[4,768,128]{2,1,0:T(8,128)(2,1)} %copy-done.10, bf16[4,528,128]{2,1,0:T(8,128)(2,1)} %get-tuple-element.158.refs_2_, ...), custom_call_target="tpu_custom_call" | custom-call | flops 6899999744 | bytes 1024 | tf_op jit(solution)/shard_map/finish/pallas_call | solution.py:996
  409.9 2.5 step_half.1.refs_0_
  412.4 1.4 collective-permute-start.46
  413.9 1.7 collective-permute-start.28
  415.6 2.7 collective-permute-done.28
  418.3 2.9 collective-permute-start.29
  421.2 2.4 collective-permute-done.29
  427.0 2.5 finish.3
  (158 shorter events, 29.7 us)
Async XLA Ops:
  7.2 96.5 %all-gather.8.cloned.1.call-start = ((), (), s32[]{:S(2)}) async-start(), calls=%async_computation.2 | async-start | bytes 1474560 | tf_op jit(solution)/shard_map/all_gather | solution.py:1066
  12.7 15.6 %copy-start.4 = (s32[2,1024]{1,0:T(2,128)S(1)}, s32[2,1024]{1,0:T(2,128)}, u32[]{:S(2)}) copy-start(s32[2,1024]{1,0:T(2,128)} %param.20) | copy-start | bytes 24580
  12.7 16.2 %collective-permute-start.2 = (bf16[8,768]{1,0:T(8,128)(2,1)S(1)}, bf16[8,768]{1,0:T(8,128)(2,1)S(1)}, u32[]{:S(2)}, u32[]{:S(2)}) collective-permute-start(bf16[8,768]{1,0:T(8,128)(2,1)S(1)} %stack.69), channel_id=1, source_target_pairs={{0,3},{1,2},{2,1},{3,0},{4,7},{5,6},{6,5},{7,4},{8,11},{9,10},{10,... | collective-permute-start | bytes 36872 | tf_op jit(solution)/shard_map/ppermute | solution.py:817
  15.1 13.8 %collective-permute-start.1 = (bf16[8,768]{1,0:T(8,128)(2,1)S(1)}, bf16[8,768]{1,0:T(8,128)(2,1)S(1)}, u32[]{:S(2)}, u32[]{:S(2)}) collective-permute-start(bf16[8,768]{1,0:T(8,128)(2,1)S(1)} %stack.69), channel_id=1, source_target_pairs={{0,2},{1,3},{2,0},{3,1},{4,6},{5,7},{6,4},{7,5},{8,10},{9,11},{10,... | collective-permute-start | bytes 36872 | tf_op jit(solution)/shard_map/ppermute | solution.py:817
  15.8 13.1 %collective-permute-start = (bf16[8,768]{1,0:T(8,128)(2,1)S(1)}, bf16[8,768]{1,0:T(8,128)(2,1)S(1)}, u32[]{:S(2)}, u32[]{:S(2)}) collective-permute-start(bf16[8,768]{1,0:T(8,128)(2,1)S(1)} %stack.69), channel_id=1, source_target_pairs={{0,1},{1,0},{2,3},{3,2},{4,5},{5,4},{6,7},{7,6},{8,9},{9,8},{10,11... | collective-permute-start | bytes 36872 | tf_op jit(solution)/shard_map/ppermute | solution.py:817
  15.8 23.4 %collective-permute-start.3 = (bf16[192,2304]{1,0:T(8,128)(2,1)}, bf16[192,2304]{1,0:T(8,128)(2,1)S(1)}, u32[]{:S(2)}, u32[]{:S(2)}) collective-permute-start(bf16[192,2304]{1,0:T(8,128)(2,1)} %refs_21_.1), channel_id=1, source_target_pairs={{0,2},{1,3},{2,0},{3,1},{4,6},{5,7},{6,4},{7,5},{8,10},{9,11},{10,... | collective-permute-start | bytes 2654216 | tf_op jit(solution)/shard_map/ppermute | solution.py:817
  39.2 0.9 copy-start
  43.4 2.1 copy-start.1
  43.4 60.3 %all-gather.6.cloned.1.call-start = ((), (), s32[]{:S(2)}) async-start(), calls=%async_computation.1 | async-start | bytes 3932160 | tf_op jit(solution)/shard_map/all_gather | solution.py:1066
  44.1 137.2 %all-gather.4.cloned.1.call-start = ((), (), s32[]{:S(2)}) async-start(), calls=%async_computation | async-start | bytes 1966080 | tf_op jit(solution)/shard_map/all_gather | solution.py:1066
  44.2 2.8 collective-permute-start.4
  44.3 4.0 collective-permute-start.5
  45.4 25.9 %collective-permute-start.6 = (bf16[512,768]{1,0:T(8,128)(2,1)S(1)}, bf16[512,768]{1,0:T(8,128)(2,1)S(1)}, u32[]{:S(2)}, u32[]{:S(2)}) collective-permute-start(bf16[512,768]{1,0:T(8,128)(2,1)S(1)} %copy-done.1), channel_id=1, source_target_pairs={{0,2},{1,3},{2,0},{3,1},{4,6},{5,7},{6,4},{7,5},{8,10},{9,11},{10,... | collective-permute-start | bytes 2359304 | tf_op jit(solution)/shard_map/ppermute | solution.py:817
  72.1 31.5 %collective-permute-start.7 = (bf16[512,768]{1,0:T(8,128)(2,1)}, bf16[512,768]{1,0:T(8,128)(2,1)S(1)}, u32[]{:S(2)}, u32[]{:S(2)}) collective-permute-start(bf16[512,768]{1,0:T(8,128)(2,1)} %get-tuple-element.106.refs_8_), channel_id=1, source_target_pairs={{0,1},{1,0},{2,3},{3,2},{4,5},{5,4},{6,7},{7,6},{8,9},{9,8},{10,11... | collective-permute-start | bytes 2359304 | tf_op jit(solution)/shard_map/ppermute | solution.py:817
  72.2 31.5 %collective-permute-start.8 = (bf16[512,768]{1,0:T(8,128)(2,1)}, bf16[512,768]{1,0:T(8,128)(2,1)S(1)}, u32[]{:S(2)}, u32[]{:S(2)}) collective-permute-start(bf16[512,768]{1,0:T(8,128)(2,1)} %get-tuple-element.107.refs_10_), channel_id=1, source_target_pairs={{0,1},{1,0},{2,3},{3,2},{4,5},{5,4},{6,7},{7,6},{8,9},{9,8},{10,11... | collective-permute-start | bytes 2359304 | tf_op jit(solution)/shard_map/ppermute | solution.py:817
  103.3 60.7 %collective-permute-start.9 = (bf16[256,768]{1,0:T(8,128)(2,1)}, bf16[256,768]{1,0:T(8,128)(2,1)S(1)}, u32[]{:S(2)}, u32[]{:S(2)}) collective-permute-start(bf16[256,768]{1,0:T(8,128)(2,1)} %gate.7.refs_0_), channel_id=1, source_target_pairs={{0,2},{1,3},{2,0},{3,1},{4,6},{5,7},{6,4},{7,5},{8,10},{9,11},{10,... | collective-permute-start | bytes 1179656 | tf_op jit(solution)/shard_map/ppermute | solution.py:817
  103.7 0.9 copy-start.12
  103.7 1.2 copy-start.13
  164.7 16.6 %collective-permute-start.10 = (bf16[256,768]{1,0:T(8,128)(2,1)}, bf16[256,768]{1,0:T(8,128)(2,1)S(1)}, u32[]{:S(2)}, u32[]{:S(2)}) collective-permute-start(bf16[256,768]{1,0:T(8,128)(2,1)} %get-tuple-element.115.refs_11_), channel_id=1, source_target_pairs={{0,1},{1,0},{2,3},{3,2},{4,5},{5,4},{6,7},{7,6},{8,9},{9,8},{10,11... | collective-permute-start | bytes 1179656 | tf_op jit(solution)/shard_map/ppermute | solution.py:817
  164.7 16.6 %collective-permute-start.11 = (bf16[256,768]{1,0:T(8,128)(2,1)}, bf16[256,768]{1,0:T(8,128)(2,1)}, u32[]{:S(2)}, u32[]{:S(2)}) collective-permute-start(bf16[256,768]{1,0:T(8,128)(2,1)} %get-tuple-element.116.refs_13_), channel_id=1, source_target_pairs={{0,1},{1,0},{2,3},{3,2},{4,5},{5,4},{6,7},{7,6},{8,9},{9,8},{10,11... | collective-permute-start | bytes 1179656 | tf_op jit(solution)/shard_map/ppermute | solution.py:817
  165.2 10.4 %collective-permute-start.12 = (bf16[2,2,4,768,128]{4,3,2,1,0:T(8,128)(2,1)}, bf16[2,2,4,768,128]{4,3,2,1,0:T(8,128)(2,1)}, u32[]{:S(2)}, u32[]{:S(2)}) collective-permute-start(bf16[2,2,4,768,128]{4,3,2,1,0:T(8,128)(2,1)} %get-tuple-element.118), channel_id=1, source_target_pairs={{0,1},{1,0},{2,3},{3,2},{4,5},{5,4},{6,7},{7,6},{8,9},{9,8},{10,11... | collective-permute-start | bytes 9437192 | tf_op jit(solution)/shard_map/ppermute | solution.py:817
  179.6 45.1 %collective-permute-start.13 = (bf16[2,4,768,128]{3,2,1,0:T(8,128)(2,1)}, bf16[2,4,768,128]{3,2,1,0:T(8,128)(2,1)S(1)}, u32[]{:S(2)}, u32[]{:S(2)}) collective-permute-start(bf16[2,4,768,128]{3,2,1,0:T(8,128)(2,1)} %step_x.2.refs_15_), channel_id=1, source_target_pairs={{0,2},{1,3},{2,0},{3,1},{4,6},{5,7},{6,4},{7,5},{8,10},{9,11},{10,... | collective-permute-start | bytes 4718600 | tf_op jit(solution)/shard_map/ppermute | solution.py:817
  224.4 21.3 %collective-permute-start.15 = (bf16[2,2,4,528,128]{4,3,2,1,0:T(8,128)(2,1)}, bf16[2,2,4,528,128]{4,3,2,1,0:T(8,128)(2,1)}, u32[]{:S(2)}, u32[]{:S(2)}) collective-permute-start(bf16[2,2,4,528,128]{4,3,2,1,0:T(8,128)(2,1)} %get-tuple-element.121), channel_id=1, source_target_pairs={{0,1},{1,0},{2,3},{3,2},{4,5},{5,4},{6,7},{7,6},{8,9},{9,8},{10,11... | collective-permute-start | bytes 6488072 | tf_op jit(solution)/shard_map/ppermute | solution.py:817
  224.7 1.1 copy-start.6
  229.3 19.9 %collective-permute-start.14 = (bf16[4,768,128]{2,1,0:T(8,128)(2,1)}, bf16[4,768,128]{2,1,0:T(8,128)(2,1)S(1)}, u32[]{:S(2)}, u32[]{:S(2)}) collective-permute-start(bf16[4,768,128]{2,1,0:T(8,128)(2,1)} %step_y.2.refs_0_), channel_id=1, source_target_pairs={{0,4},{4,0},{8,12},{12,8},{16,20},{20,16},{24,28},{28,24},{1,5},{5... | collective-permute-start | bytes 2359304 | tf_op jit(solution)/shard_map/ppermute | solution.py:817
  254.8 19.2 %collective-permute-start.16 = (bf16[768,128]{1,0:T(8,128)(2,1)}, bf16[768,128]{1,0:T(8,128)(2,1)S(1)}, u32[]{:S(2)}, u32[]{:S(2)}) collective-permute-start(bf16[768,128]{1,0:T(8,128)(2,1)} %get-tuple-element.124.refs_0_), channel_id=1, source_target_pairs={{0,8},{4,12},{8,0},{12,4},{16,24},{20,28},{24,16},{28,20},{1,9},{5... | collective-permute-start | bytes 589832 | tf_op jit(solution)/shard_map/ppermute | solution.py:817
  256.4 17.7 %collective-permute-start.17 = (bf16[768,128]{1,0:T(8,128)(2,1)}, bf16[768,128]{1,0:T(8,128)(2,1)S(1)}, u32[]{:S(2)}, u32[]{:S(2)}) collective-permute-start(bf16[768,128]{1,0:T(8,128)(2,1)} %get-tuple-element.125), channel_id=1, source_target_pairs={{0,16},{4,20},{8,24},{12,28},{16,0},{20,4},{24,8},{28,12},{1,17},{... | collective-permute-start | bytes 589832 | tf_op jit(solution)/shard_map/ppermute | solution.py:817
  259.1 15.0 %collective-permute-start.18 = (bf16[768,128]{1,0:T(8,128)(2,1)}, bf16[768,128]{1,0:T(8,128)(2,1)S(1)}, u32[]{:S(2)}, u32[]{:S(2)}) collective-permute-start(bf16[768,128]{1,0:T(8,128)(2,1)} %get-tuple-element.126), channel_id=1, source_target_pairs={{0,24},{4,28},{8,16},{12,20},{16,8},{20,12},{24,0},{28,4},{1,25},{... | collective-permute-start | bytes 589832 | tf_op jit(solution)/shard_map/ppermute | solution.py:817
  259.2 39.6 %collective-permute-start.22 = (bf16[2,4,528,128]{3,2,1,0:T(8,128)(2,1)}, bf16[2,4,528,128]{3,2,1,0:T(8,128)(2,1)S(1)}, u32[]{:S(2)}, u32[]{:S(2)}) collective-permute-start(bf16[2,4,528,128]{3,2,1,0:T(8,128)(2,1)} %get-tuple-element.132), channel_id=1, source_target_pairs={{0,2},{1,3},{2,0},{3,1},{4,6},{5,7},{6,4},{7,5},{8,10},{9,11},{10,... | collective-permute-start | bytes 3244040 | tf_op jit(solution)/shard_map/ppermute | solution.py:817
  278.4 19.6 %collective-permute-start.19 = (bf16[768,128]{1,0:T(8,128)(2,1)}, bf16[768,128]{1,0:T(8,128)(2,1)S(1)}, u32[]{:S(2)}, u32[]{:S(2)}) collective-permute-start(bf16[768,128]{1,0:T(8,128)(2,1)} %step_sum.2.refs_0_), channel_id=1, source_target_pairs={{0,8},{4,12},{8,0},{12,4},{16,24},{20,28},{24,16},{28,20},{1,9},{5... | collective-permute-start | bytes 589832 | tf_op jit(solution)/shard_map/ppermute | solution.py:817
  281.0 17.0 %collective-permute-start.20 = (bf16[768,128]{1,0:T(8,128)(2,1)}, bf16[768,128]{1,0:T(8,128)(2,1)S(1)}, u32[]{:S(2)}, u32[]{:S(2)}) collective-permute-start(bf16[768,128]{1,0:T(8,128)(2,1)} %step_sum.2.refs_0_), channel_id=1, source_target_pairs={{0,16},{4,20},{8,24},{12,28},{16,0},{20,4},{24,8},{28,12},{1,17},{... | collective-permute-start | bytes 589832 | tf_op jit(solution)/shard_map/ppermute | solution.py:817
  282.8 15.3 %collective-permute-start.21 = (bf16[768,128]{1,0:T(8,128)(2,1)}, bf16[768,128]{1,0:T(8,128)(2,1)S(1)}, u32[]{:S(2)}, u32[]{:S(2)}) collective-permute-start(bf16[768,128]{1,0:T(8,128)(2,1)} %step_sum.2.refs_0_), channel_id=1, source_target_pairs={{0,24},{4,28},{8,16},{12,20},{16,8},{20,12},{24,0},{28,4},{1,25},{... | collective-permute-start | bytes 589832 | tf_op jit(solution)/shard_map/ppermute | solution.py:817
  298.8 1.0 copy-start.7
  302.8 14.4 %collective-permute-start.23 = (bf16[4,528,128]{2,1,0:T(8,128)(2,1)}, bf16[4,528,128]{2,1,0:T(8,128)(2,1)}, u32[]{:S(2)}, u32[]{:S(2)}) collective-permute-start(bf16[4,528,128]{2,1,0:T(8,128)(2,1)} %step_y.3.refs_11_), channel_id=1, source_target_pairs={{0,4},{4,0},{8,12},{12,8},{16,20},{20,16},{24,28},{28,24},{1,5},{5... | collective-permute-start | bytes 1622024 | tf_op jit(solution)/shard_map/ppermute | solution.py:817
  317.2 15.5 %collective-permute-start.24 = (bf16[2,2,4,432,128]{4,3,2,1,0:T(8,128)(2,1)}, bf16[2,2,4,432,128]{4,3,2,1,0:T(8,128)(2,1)S(1)}, u32[]{:S(2)}, u32[]{:S(2)}) collective-permute-start(bf16[2,2,4,432,128]{4,3,2,1,0:T(8,128)(2,1)} %get-tuple-element.147), channel_id=1, source_target_pairs={{0,1},{1,0},{2,3},{3,2},{4,5},{5,4},{6,7},{7,6},{8,9},{9,8},{10,11... | collective-permute-start | bytes 5308424 | tf_op jit(solution)/shard_map/ppermute | solution.py:817
  320.8 37.4 %collective-permute-start.31 = (bf16[528,128]{1,0:T(8,128)(2,1)}, bf16[528,128]{1,0:T(8,128)(2,1)S(1)}, u32[]{:S(2)}, u32[]{:S(2)}) collective-permute-start(bf16[528,128]{1,0:T(8,128)(2,1)} %get-tuple-element.150), channel_id=1, source_target_pairs={{0,8},{4,12},{8,0},{12,4},{16,24},{20,28},{24,16},{28,20},{1,9},{5... | collective-permute-start | bytes 405512 | tf_op jit(solution)/shard_map/ppermute | solution.py:817
  323.0 35.3 %collective-permute-start.32 = (bf16[528,128]{1,0:T(8,128)(2,1)}, bf16[528,128]{1,0:T(8,128)(2,1)}, u32[]{:S(2)}, u32[]{:S(2)}) collective-permute-start(bf16[528,128]{1,0:T(8,128)(2,1)} %get-tuple-element.151), channel_id=1, source_target_pairs={{0,16},{4,20},{8,24},{12,28},{16,0},{20,4},{24,8},{28,12},{1,17},{... | collective-permute-start | bytes 405512 | tf_op jit(solution)/shard_map/ppermute | solution.py:817
  324.5 33.8 %collective-permute-start.33 = (bf16[528,128]{1,0:T(8,128)(2,1)}, bf16[528,128]{1,0:T(8,128)(2,1)}, u32[]{:S(2)}, u32[]{:S(2)}) collective-permute-start(bf16[528,128]{1,0:T(8,128)(2,1)} %get-tuple-element.152), channel_id=1, source_target_pairs={{0,24},{4,28},{8,16},{12,20},{16,8},{20,12},{24,0},{28,4},{1,25},{... | collective-permute-start | bytes 405512 | tf_op jit(solution)/shard_map/ppermute | solution.py:817
  332.6 1.2 copy-start.5
  337.1 21.7 %collective-permute-start.30 = (bf16[2,4,432,128]{3,2,1,0:T(8,128)(2,1)}, bf16[2,4,432,128]{3,2,1,0:T(8,128)(2,1)S(1)}, u32[]{:S(2)}, u32[]{:S(2)}) collective-permute-start(bf16[2,4,432,128]{3,2,1,0:T(8,128)(2,1)} %step_x.3.refs_25_), channel_id=1, source_target_pairs={{0,2},{1,3},{2,0},{3,1},{4,6},{5,7},{6,4},{7,5},{8,10},{9,11},{10,... | collective-permute-start | bytes 2654216 | tf_op jit(solution)/shard_map/ppermute | solution.py:817
  358.8 0.9 copy-start.8
  359.7 8.9 %copy-start.3 = (f32[24,768]{1,0:T(8,128)S(1)}, f32[24,768]{1,0:T(8,128)}, u32[]{:S(2)}) copy-start(f32[24,768]{1,0:T(8,128)} %get-tuple-element.149.refs_10_) | copy-start | bytes 221188
  359.7 10.1 %copy-start.9 = (bf16[4,768,128]{2,1,0:T(8,128)(2,1)S(1)}, bf16[4,768,128]{2,1,0:T(8,128)(2,1)}, u32[]{:S(2)}) copy-start(bf16[4,768,128]{2,1,0:T(8,128)(2,1)} %get-tuple-element.140.refs_0_) | copy-start | bytes 2359300
  363.6 14.5 %collective-permute-start.34 = (bf16[4,432,128]{2,1,0:T(8,128)(2,1)}, bf16[4,432,128]{2,1,0:T(8,128)(2,1)}, u32[]{:S(2)}, u32[]{:S(2)}) collective-permute-start(bf16[4,432,128]{2,1,0:T(8,128)(2,1)} %get-tuple-element.153), channel_id=1, source_target_pairs={{0,4},{4,0},{8,12},{12,8},{16,20},{20,16},{24,28},{28,24},{1,5},{5... | collective-permute-start | bytes 1327112 | tf_op jit(solution)/shard_map/ppermute | solution.py:817
  364.2 7.1 %collective-permute-start.35 = (bf16[528,128]{1,0:T(8,128)(2,1)}, bf16[528,128]{1,0:T(8,128)(2,1)S(1)}, u32[]{:S(2)}, u32[]{:S(2)}) collective-permute-start(bf16[528,128]{1,0:T(8,128)(2,1)} %get-tuple-element.154.refs_0_), channel_id=1, source_target_pairs={{0,8},{4,12},{8,0},{12,4},{16,24},{20,28},{24,16},{28,20},{1,9},{5... | collective-permute-start | bytes 405512 | tf_op jit(solution)/shard_map/ppermute | solution.py:817
  364.7 13.3 %collective-permute-start.36 = (bf16[528,128]{1,0:T(8,128)(2,1)}, bf16[528,128]{1,0:T(8,128)(2,1)}, u32[]{:S(2)}, u32[]{:S(2)}) collective-permute-start(bf16[528,128]{1,0:T(8,128)(2,1)} %get-tuple-element.154.refs_0_), channel_id=1, source_target_pairs={{0,16},{4,20},{8,24},{12,28},{16,0},{20,4},{24,8},{28,12},{1,17},{... | collective-permute-start | bytes 405512 | tf_op jit(solution)/shard_map/ppermute | solution.py:817
  367.9 10.2 %collective-permute-start.37 = (bf16[528,128]{1,0:T(8,128)(2,1)}, bf16[528,128]{1,0:T(8,128)(2,1)}, u32[]{:S(2)}, u32[]{:S(2)}) collective-permute-start(bf16[528,128]{1,0:T(8,128)(2,1)} %get-tuple-element.154.refs_0_), channel_id=1, source_target_pairs={{0,24},{4,28},{8,16},{12,20},{16,8},{20,12},{24,0},{28,4},{1,25},{... | collective-permute-start | bytes 405512 | tf_op jit(solution)/shard_map/ppermute | solution.py:817
  368.6 1.3 collective-permute-start.25
  369.8 29.4 %collective-permute-start.44 = (bf16[4,768,128]{2,1,0:T(8,128)(2,1)S(1)}, bf16[4,768,128]{2,1,0:T(8,128)(2,1)S(1)}, u32[]{:S(2)}, u32[]{:S(2)}) collective-permute-start(bf16[4,768,128]{2,1,0:T(8,128)(2,1)S(1)} %copy-done.9), channel_id=1, source_target_pairs={{0,4},{4,0},{8,12},{12,8},{16,20},{20,16},{24,28},{28,24},{1,5},{5... | collective-permute-start | bytes 2359304 | tf_op jit(solution)/shard_map/ppermute | solution.py:817
  371.3 6.8 %copy-start.24 = (bf16[528,128]{1,0:T(8,128)(2,1)}, bf16[528,128]{1,0:T(8,128)(2,1)S(1)}, u32[]{:S(2)}) copy-start(bf16[528,128]{1,0:T(8,128)(2,1)S(1)} %collective-permute-done.35.refs_1_) | copy-start | bytes 405508
  371.3 14.5 %collective-permute-start.26 = (f32[24,768]{1,0:T(8,128)S(1)}, f32[24,768]{1,0:T(8,128)S(1)}, u32[]{:S(2)}, u32[]{:S(2)}) collective-permute-start(f32[24,768]{1,0:T(8,128)S(1)} %add.94), channel_id=1, source_target_pairs={{0,2},{1,3},{2,0},{3,1},{4,6},{5,7},{6,4},{7,5},{8,10},{9,11},{10,... | collective-permute-start | bytes 221192 | tf_op jit(solution)/shard_map/ppermute | solution.py:817
  381.4 5.9 %collective-permute-start.38 = (bf16[432,128]{1,0:T(8,128)(2,1)}, bf16[432,128]{1,0:T(8,128)(2,1)S(1)}, u32[]{:S(2)}, u32[]{:S(2)}) collective-permute-start(bf16[432,128]{1,0:T(8,128)(2,1)} %get-tuple-element.155), channel_id=1, source_target_pairs={{0,8},{4,12},{8,0},{12,4},{16,24},{20,28},{24,16},{28,20},{1,9},{5... | collective-permute-start | bytes 331784 | tf_op jit(solution)/shard_map/ppermute | solution.py:817
  383.4 10.4 %collective-permute-start.39 = (bf16[432,128]{1,0:T(8,128)(2,1)}, bf16[432,128]{1,0:T(8,128)(2,1)}, u32[]{:S(2)}, u32[]{:S(2)}) collective-permute-start(bf16[432,128]{1,0:T(8,128)(2,1)} %get-tuple-element.156), channel_id=1, source_target_pairs={{0,16},{4,20},{8,24},{12,28},{16,0},{20,4},{24,8},{28,12},{1,17},{... | collective-permute-start | bytes 331784 | tf_op jit(solution)/shard_map/ppermute | solution.py:817
  384.3 9.4 %collective-permute-start.40 = (bf16[432,128]{1,0:T(8,128)(2,1)}, bf16[432,128]{1,0:T(8,128)(2,1)}, u32[]{:S(2)}, u32[]{:S(2)}) collective-permute-start(bf16[432,128]{1,0:T(8,128)(2,1)} %get-tuple-element.157), channel_id=1, source_target_pairs={{0,24},{4,28},{8,16},{12,20},{16,8},{20,12},{24,0},{28,4},{1,25},{... | collective-permute-start | bytes 331784 | tf_op jit(solution)/shard_map/ppermute | solution.py:817
  385.8 18.6 %collective-permute-start.45 = (bf16[4,528,128]{2,1,0:T(8,128)(2,1)}, bf16[4,528,128]{2,1,0:T(8,128)(2,1)}, u32[]{:S(2)}, u32[]{:S(2)}) collective-permute-start(bf16[4,528,128]{2,1,0:T(8,128)(2,1)} %get-tuple-element.158.refs_2_), channel_id=1, source_target_pairs={{0,4},{4,0},{8,12},{12,8},{16,20},{20,16},{24,28},{28,24},{1,5},{5... | collective-permute-start | bytes 1622024 | tf_op jit(solution)/shard_map/ppermute | solution.py:817
  387.2 6.5 %copy-start.25 = (bf16[432,128]{1,0:T(8,128)(2,1)}, bf16[432,128]{1,0:T(8,128)(2,1)S(1)}, u32[]{:S(2)}) copy-start(bf16[432,128]{1,0:T(8,128)(2,1)S(1)} %collective-permute-done.38.refs_4_) | copy-start | bytes 331780
  387.2 26.6 %collective-permute-start.27 = (f32[24,768]{1,0:T(8,128)S(1)}, f32[24,768]{1,0:T(8,128)S(1)}, u32[]{:S(2)}, u32[]{:S(2)}) collective-permute-start(f32[24,768]{1,0:T(8,128)S(1)} %add.95), channel_id=1, source_target_pairs={{0,4},{4,0},{8,12},{12,8},{16,20},{20,16},{24,28},{28,24},{1,5},{5... | collective-permute-start | bytes 221192 | tf_op jit(solution)/shard_map/ppermute | solution.py:817
  396.7 12.1 %collective-permute-start.41 = (bf16[432,128]{1,0:T(8,128)(2,1)}, bf16[432,128]{1,0:T(8,128)(2,1)S(1)}, u32[]{:S(2)}, u32[]{:S(2)}) collective-permute-start(bf16[432,128]{1,0:T(8,128)(2,1)} %step_sum.3.refs_4_.refs_0_), channel_id=1, source_target_pairs={{0,8},{4,12},{8,0},{12,4},{16,24},{20,28},{24,16},{28,20},{1,9},{5... | collective-permute-start | bytes 331784 | tf_op jit(solution)/shard_map/ppermute | solution.py:817
  398.4 10.8 %collective-permute-start.42 = (bf16[432,128]{1,0:T(8,128)(2,1)}, bf16[432,128]{1,0:T(8,128)(2,1)}, u32[]{:S(2)}, u32[]{:S(2)}) collective-permute-start(bf16[432,128]{1,0:T(8,128)(2,1)} %step_sum.3.refs_4_.refs_0_), channel_id=1, source_target_pairs={{0,16},{4,20},{8,24},{12,28},{16,0},{20,4},{24,8},{28,12},{1,17},{... | collective-permute-start | bytes 331784 | tf_op jit(solution)/shard_map/ppermute | solution.py:817
  399.2 5.1 %copy-start.10 = (bf16[4,768,128]{2,1,0:T(8,128)(2,1)}, bf16[4,768,128]{2,1,0:T(8,128)(2,1)S(1)}, u32[]{:S(2)}) copy-start(bf16[4,768,128]{2,1,0:T(8,128)(2,1)S(1)} %collective-permute-done.44.refs_1_) | copy-start | bytes 2359300
  399.2 10.0 %collective-permute-start.43 = (bf16[432,128]{1,0:T(8,128)(2,1)}, bf16[432,128]{1,0:T(8,128)(2,1)S(1)}, u32[]{:S(2)}, u32[]{:S(2)}) collective-permute-start(bf16[432,128]{1,0:T(8,128)(2,1)} %step_sum.3.refs_4_.refs_0_), channel_id=1, source_target_pairs={{0,24},{4,28},{8,16},{12,20},{16,8},{20,12},{24,0},{28,4},{1,25},{... | collective-permute-start | bytes 331784 | tf_op jit(solution)/shard_map/ppermute | solution.py:817
  412.4 13.9 %collective-permute-start.46 = (bf16[4,432,128]{2,1,0:T(8,128)(2,1)}, bf16[4,432,128]{2,1,0:T(8,128)(2,1)S(1)}, u32[]{:S(2)}, u32[]{:S(2)}) collective-permute-start(bf16[4,432,128]{2,1,0:T(8,128)(2,1)} %step_half.1.refs_0_), channel_id=1, source_target_pairs={{0,4},{4,0},{8,12},{12,8},{16,20},{20,16},{24,28},{28,24},{1,5},{5... | collective-permute-start | bytes 1327112 | tf_op jit(solution)/shard_map/ppermute | solution.py:817
  413.9 4.4 %collective-permute-start.28 = (f32[24,768]{1,0:T(8,128)S(1)}, f32[24,768]{1,0:T(8,128)S(1)}, u32[]{:S(2)}, u32[]{:S(2)}) collective-permute-start(f32[24,768]{1,0:T(8,128)S(1)} %add.96), channel_id=1, source_target_pairs={{0,8},{4,12},{8,0},{12,4},{16,24},{20,28},{24,16},{28,20},{1,9},{5... | collective-permute-start | bytes 221192 | tf_op jit(solution)/shard_map/ppermute | solution.py:817
  418.3 5.3 %collective-permute-start.29 = (f32[24,768]{1,0:T(8,128)S(1)}, f32[24,768]{1,0:T(8,128)S(1)}, u32[]{:S(2)}, u32[]{:S(2)}) collective-permute-start(f32[24,768]{1,0:T(8,128)S(1)} %add.97), channel_id=1, source_target_pairs={{0,16},{4,20},{8,24},{12,28},{16,0},{20,4},{24,8},{28,12},{1,17},{... | collective-permute-start | bytes 221192 | tf_op jit(solution)/shard_map/ppermute | solution.py:817
  (14 other events, 10.3 us)
Sparse Core Ops, SparseCore 0:
  43.5 24.2 all-gather.7
  69.9 28.5 all-gather.5
  100.6 23.7 all-gather.3

commit v3 on v2

--- a/solution.py
+++ b/solution.py
@@ -119,9 +119,8 @@
 def ring_put(ring, at, value):
     for j in range(ring.shape[0]):
         part = value[:, j * 128 : (j + 1) * 128]
-        ring[j, at : at + value.shape[0]] = part
-        twin = ring.shape[1] // 2 + at
-        ring[j, twin : twin + value.shape[0]] = part
+        ring[j, pl.ds(at, value.shape[0]), :] = part
+        ring[j, pl.ds(ring.shape[1] // 2 + at, value.shape[0]), :] = part
 
 
 def ring_get(ring, start, rows):
@@ -203,59 +202,74 @@
 
 
 def qkv_kernel(me_ref, act_ref, small_ref, cos_ref, sin_ref, *refs):
-    pieces, (q_ref, k_ref, v_ref, w_ref, sems) = refs[:-5], refs[-5:]
+    pieces, (out_ref, w_ref, sems) = refs[:-3], refs[-3:]
     width = act_ref.shape[1]
-
-    @pl.when(pl.program_id(0) == 0)
-    def _():
-        load_pieces(me_ref[0], pieces, w_ref, sems, True)
-        load_pieces(me_ref[0], pieces, w_ref, sems, False)
-
     half = HEAD // 2
     rows = 256
     bias = vec(small_ref, "bqkv", 0, 3 * width // small_ref.shape[0])
-    cos, sin = cos_ref[0], sin_ref[0]
-    for part, out in enumerate((q_ref, k_ref, v_ref)):
-        scale = LOG2E * HEAD**-0.5 if part == 0 else 1.0
+
+    def load(part, start):
+        cols = slice(part * width, (part + 1) * width)
+        load_pieces(me_ref[0], pieces, w_ref.at[part], sems.at[part], start, cols)
+
+    @pl.when((pl.program_id(0) == 0) & (pl.program_id(1) == 0))
+    def _():
+        for part in range(3):
+            load(part, True)
+
+    def project(part):
+        @pl.when(pl.program_id(0) == 0)
+        def _():
+            load(part, False)
+
+        cos, sin = cos_ref[0], sin_ref[0]
         for base in range(0, width, rows):
+            cols = slice(base, base + rows)
             at = part * width + base
-            cols = slice(at, at + rows)
-            y = dot_tt(w_ref[:, cols], act_ref[...]) + column(bias[:, cols])
+            y = dot_tt(w_ref[part, :, cols], act_ref[...]) + column(bias[:, at : at + rows])
             if part == 2:
-                out[0, base : base + rows, :] = y.astype(BF)
+                out_ref[0, base : base + rows, :] = y.astype(BF)
                 continue
             for h in range(0, rows, HEAD):
                 u, w = y[h : h + half], y[h + half : h + HEAD]
                 a, b = u * cos - w * sin, w * cos + u * sin
                 if part == 0:
-                    a, b = a * scale, b * scale
-                out[0, base + h : base + h + half, :] = a.astype(BF)
-                out[0, base + h + half : base + h + HEAD, :] = b.astype(BF)
+                    a, b = a * (LOG2E * HEAD**-0.5), b * (LOG2E * HEAD**-0.5)
+                out_ref[0, base + h : base + h + half, :] = a.astype(BF)
+                out_ref[0, base + h + half : base + h + HEAD, :] = b.astype(BF)
+
+    for part in range(3):
+        pl.when(pl.program_id(1) == part)(lambda part=part: project(part))
 
 
 def qkv_call(me, act, small, cos, sin, pieces):
     tokens, width = act.shape
     nseq, _, length = cos.shape
-    col = pl.BlockSpec((1, width, length), lambda s: (s, 0, 0))
-    tab = pl.BlockSpec((1, HEAD // 2, length), lambda s: (s, 0, 0))
-    turned = jax.ShapeDtypeStruct((nseq, width, length), BF)
+    tab = pl.BlockSpec((1, HEAD // 2, length), lambda s, p: (s, 0, 0))
     return pl.pallas_call(
         qkv_kernel,
-        grid=(nseq,),
+        grid=(nseq, 3),
         in_specs=[
-            SMEM, pl.BlockSpec((length, width), lambda s: (s, 0)), whole(small.shape), tab, tab,
+            SMEM, pl.BlockSpec((length, width), lambda s, p: (s, 0)), whole(small.shape), tab, tab,
             *(ANY for _ in pieces),
         ],
-        out_specs=[col, col, col],
-        out_shape=[turned, turned, turned],
+        out_specs=pl.BlockSpec((1, None, width, length), lambda s, p: (s, p, 0, 0)),
+        out_shape=jax.ShapeDtypeStruct((nseq, 3, width, length), BF),
         scratch_shapes=[
-            pltpu.VMEM((width, 3 * width), BF),
-            pltpu.SemaphoreType.DMA((len(pieces),)),
+            pltpu.VMEM((3, width, width), BF),
+            pltpu.SemaphoreType.DMA((3, len(pieces))),
         ],
         compiler_params=params(62),
         cost_estimate=cost(15),
         name="qkv",
     )(me, act, small, cos, sin, *pieces)
+
+
+def head_specs(base):
+    return [
+        lambda length, part=part: pl.BlockSpec((1, None, PAIR, length), lambda s, h: (s, part, base + h, 0))
+        for part in range(3)
+    ]
 
 
 def fill_masks(seg_ref, mask, blk):
@@ -295,24 +309,31 @@
     def _():
         fill_masks(seg_ref, mask, blk)
 
-    for half in range(2):
+    units = [(half, head, qb) for qb in range(2) for half in range(2) for head in range(2)]
+    keys = [k_ref[0, :, half * 2 * blk : (half + 1) * 2 * blk].T for half in range(2)]
+
+    def place(half, head, qb):
         base = half * 2 * blk
-        keys = k_ref[0, :, base : base + 2 * blk].T
-        for head in range(2):
-            hs = slice(head * HEAD, (head + 1) * HEAD)
-            for qb in range(2):
-                qs = slice(base + qb * blk, base + (qb + 1) * blk)
-                s = scores_of(keys, one_head(q_ref[0, :, qs], head), mask, half, qb, blk)
-                top = jnp.max(s, axis=0, keepdims=True)
-                p = jnp.exp2(s - top)
-                total = jnp.sum(p, axis=0, keepdims=True)
-                o = dot_nn(v_ref[0, hs, base : base + (qb + 1) * blk], p.astype(BF))
-                o_ref[0, hs, qs] = (o / total).astype(BF)
-                l_ref[0, 0, head : head + 1, qs] = top + jnp.log2(total)
-
-
-def attend_call(seg, q, k, v):
-    nseq, width, length = q.shape
+        qs = slice(base + qb * blk, base + (qb + 1) * blk)
+        return base, qs, slice(head * HEAD, (head + 1) * HEAD)
+
+    scores = []
+    for half, head, qb in units:
+        _, qs, _ = place(half, head, qb)
+        scores.append(scores_of(keys[half], one_head(q_ref[0, :, qs], head), mask, half, qb, blk))
+    tops = [jnp.max(s, axis=0, keepdims=True) for s in scores]
+    probs = [jnp.exp2(s - top) for s, top in zip(scores, tops)]
+    totals = [jnp.sum(p, axis=0, keepdims=True) for p in probs]
+    lows = [p.astype(BF) for p in probs]
+    for (half, head, qb), p, top, total in zip(units, lows, tops, totals):
+        base, qs, hs = place(half, head, qb)
+        o = dot_nn(v_ref[0, hs, base : base + (qb + 1) * blk], p)
+        o_ref[0, hs, qs] = (o / total).astype(BF)
+        l_ref[0, 0, head : head + 1, qs] = top + jnp.log2(total)
+
+
+def attend_call(seg, qkv):
+    nseq, _, width, length = qkv.shape
     pairs = width // PAIR
     blk = length // 4
     blockspec = pl.BlockSpec((1, PAIR, length), lambda s, h: (s, h, 0))
@@ -321,7 +342,7 @@
         grid=(nseq, pairs),
         in_specs=[
             pl.BlockSpec((1, 8, 2 * blk), lambda s, h: (s, 0, 0)),
-            blockspec, blockspec, blockspec,
+            *(spec(length) for spec in head_specs(0)),
         ],
         out_specs=[blockspec, pl.BlockSpec((1, 1, 2, length), lambda s, h: (s, h, 0, 0))],
         out_shape=[
@@ -332,7 +353,7 @@
         compiler_params=params(62),
         cost_estimate=cost(30),
         name="attend",
-    )(seg, q, k, v)
+    )(seg, qkv, qkv, qkv)
 
 
 def attend_back_kernel(
@@ -347,32 +368,50 @@
     def _():
         fill_masks(seg_ref, mask, blk)
 
-    for half in range(2):
+    units = [(half, head, qb) for qb in range(2) for half in range(2) for head in range(2)]
+    keys = [k_ref[0, :, half * 2 * blk : (half + 1) * 2 * blk].T for half in range(2)]
+    values = [v_ref[0, :, half * 2 * blk : (half + 1) * 2 * blk].T for half in range(2)]
+
+    def place(half, head, qb):
         base = half * 2 * blk
-        ks = slice(base, base + 2 * blk)
-        keys = k_ref[0, :, ks].T
-        values = v_ref[0, :, ks].T
-        for head in range(2):
-            hs = slice(head * HEAD, (head + 1) * HEAD)
-            for qb in range(2):
-                qs = slice(base + qb * blk, base + (qb + 1) * blk)
-                span = slice(base, base + (qb + 1) * blk)
-                g = g_ref[0, hs, qs]
-                delta = jnp.sum(g.astype(F32) * o_ref[0, hs, qs].astype(F32), axis=0, keepdims=True)
-                s = scores_of(keys, one_head(q_ref[0, :, qs], head), mask, half, qb, blk)
-                p = jnp.exp2(s - l_ref[0, 0, head : head + 1, qs])
-                gp = dot_nn(values[: (qb + 1) * blk], one_head(g_ref[0, :, qs], head))
-                ds = (p * (gp - delta)).astype(BF)
-                dv = dot_nt(g, p.astype(BF))
-                dk = dot_nt(q_ref[0, hs, qs], ds)
-                turn[0, hs, qs] = dot_nn(k_ref[0, hs, span], ds)
-                if qb == 0:
-                    held_k, held_v = dk, dv
-                else:
-                    turn[1, hs, base : base + blk] = dk[:, :blk] + held_k
-                    turn[1, hs, base + blk : base + 2 * blk] = dk[:, blk:]
-                    turn[2, hs, base : base + blk] = dv[:, :blk] + held_v
-                    turn[2, hs, base + blk : base + 2 * blk] = dv[:, blk:]
+        qs = slice(base + qb * blk, base + (qb + 1) * blk)
+        return base, qs, slice(head * HEAD, (head + 1) * HEAD)
+
+    def products(unit):
+        half, head, qb = unit
+        _, qs, hs = place(*unit)
+        s = scores_of(keys[half], one_head(q_ref[0, :, qs], head), mask, half, qb, blk)
+        gp = dot_nn(values[half][: (qb + 1) * blk], one_head(g_ref[0, :, qs], head))
+        g = g_ref[0, hs, qs].astype(F32) * o_ref[0, hs, qs].astype(F32)
+        return s, gp, jnp.sum(g, axis=0, keepdims=True)
+
+    def softmax(unit, held):
+        s, gp, delta = held
+        _, qs, _ = place(*unit)
+        p = jnp.exp2(s - l_ref[0, 0, unit[1] : unit[1] + 1, qs])
+        return p.astype(BF), (p * (gp - delta)).astype(BF)
+
+    def finish(unit, pair):
+        half, head, qb = unit
+        p, ds = pair
+        base, qs, hs = place(*unit)
+        dv = dot_nt(g_ref[0, hs, qs], p)
+        dk = dot_nt(q_ref[0, hs, qs], ds)
+        turn[0, hs, qs] = dot_nn(k_ref[0, hs, base : base + (qb + 1) * blk], ds)
+        first_half, second_half = slice(base, base + blk), slice(base + blk, base + 2 * blk)
+        if qb == 0:
+            turn[1, hs, first_half], turn[2, hs, first_half] = dk, dv
+        else:
+            turn[1, hs, first_half] += dk[:, :blk]
+            turn[2, hs, first_half] += dv[:, :blk]
+            turn[1, hs, second_half], turn[2, hs, second_half] = dk[:, blk:], dv[:, blk:]
+
+    before = None
+    for unit in (*units, None):
+        held = products(unit) if unit else None
+        if before:
+            finish(before[0], softmax(*before))
+        before = (unit, held)
     cos, sin = cos_ref[0], sin_ref[0]
 
     ones = jnp.ones((8, length), BF)
@@ -388,8 +427,8 @@
         sum_ref[0, part] = dot_nt(ones, out[0])
 
 
-def attend_back_call(seg, q, k, v, o, g, lse, cos, sin, base, pairs, deps, us=15):
-    nseq, width, length = q.shape
+def attend_back_call(seg, qkv, o, g, lse, cos, sin, base, pairs, deps, us=15):
+    nseq, _, _, length = qkv.shape
     blk = length // 4
     source = pl.BlockSpec((1, PAIR, length), lambda s, h: (s, base + h, 0))
     target = pl.BlockSpec((1, PAIR, length), lambda s, h: (s, h, 0))
@@ -400,7 +439,7 @@
         grid=(nseq, pairs),
         in_specs=[
             pl.BlockSpec((1, 8, 2 * blk), lambda s, h: (s, 0, 0)),
-            source, source, source, source, source,
+            *(spec(length) for spec in head_specs(base)), source, source,
             pl.BlockSpec((1, 1, 2, length), lambda s, h: (s, base + h, 0, 0)),
             tab, tab, *(ANY for _ in deps),
         ],
@@ -413,7 +452,7 @@
         compiler_params=params(62),
         cost_estimate=cost(us),
         name="attend_back",
-    )(seg, q, k, v, o, g, lse, cos, sin, *deps)
+    )(seg, qkv, qkv, qkv, o, g, lse, cos, sin, *deps)
 
 
 def mlp_kernel(base, first, last, names, members, *refs):
@@ -428,12 +467,9 @@
     small = ref["small"]
 
     def weights(start):
-        copy = pltpu.make_async_copy(ref["wu_in"], ref["wu"], sems.at[members])
-        if start:
-            copy.start()
-        else:
-            copy.wait()
-        load_pieces(me, [ref["wd", j] for j in range(members)], ref["wd"], sems, start)
+        for i, name in enumerate(("wu", "wd")):
+            pieces = [ref[key] for key in ref if key[0] == name]
+            load_pieces(me if len(pieces) > 1 else 0, pieces, ref[name], sems.at[i], start)
 
     @pl.when(step == 0)
     def _():
@@ -530,7 +566,6 @@
         "mix": SMEM,
         "cot": row,
         "small": whole(values["small"].shape),
-        "wu_in": ANY,
     }
     parts = [(width // members, span), (span // members, width)]
     if last:
@@ -546,7 +581,7 @@
         "low": pltpu.VMEM((rows, width), BF),
         "wu": pltpu.VMEM((width, span), BF),
         "wd": pltpu.VMEM((span, width), BF),
-        "sems": pltpu.SemaphoreType.DMA((members + 1,)),
+        "sems": pltpu.SemaphoreType.DMA((2, members)),
     }
     if first:
         ins |= {"x": row}
@@ -565,18 +600,19 @@
         outs |= {"back": (row, f32row)}
     if first or last:
         ins |= {"a": col, "wo": whole((width, width))}
-    names = [*ins, *(("wd", j) for j in range(members)), *(("dep", i) for i in range(len(deps))), *outs, *scratch]
+    pieces = {(name, j): piece for name in ("wu", "wd") for j, piece in enumerate(values[name])}
+    names = [*ins, *pieces, *(("dep", i) for i in range(len(deps))), *outs, *scratch]
     result = pl.pallas_call(
         lambda *refs: mlp_kernel(base, first, last, names, members, *refs),
         grid=(tokens // rows,),
-        in_specs=[*ins.values(), *(ANY for _ in range(members + len(deps)))],
+        in_specs=[*ins.values(), *(ANY for _ in (*pieces, *deps))],
         out_specs=[spec for spec, _ in outs.values()],
         out_shape=[shape for _, shape in outs.values()],
         scratch_shapes=list(scratch.values()),
         compiler_params=params(62),
         cost_estimate=cost(45),
         name="mlp",
-    )(*(values[name] for name in ins), *values["wd"], *deps)
+    )(*(values[name] for name in ins), *pieces.values(), *deps)
     return dict(zip(outs, result))
 
 
@@ -626,11 +662,11 @@
     smalls = refs[parts : parts + parts // 3 + 4]
     grads, pieces = refs[:parts], refs[parts + len(smalls) : -5 - deps]
     gx_ref, sum_ref, ring, w_ref, sems = refs[-5:]
-    length, width = x_ref.shape
-    step = pl.program_id(0)
-    shift = shift_ref[step]
-
-    @pl.when(step == 0)
+    rows, width = x_ref.shape
+    length = gx_ref.shape[0]
+    seq, step = pl.program_id(0), pl.program_id(1)
+
+    @pl.when((seq == 0) & (step == 0))
     def _():
         load_pieces(me_ref[0], pieces, w_ref, sems, True)
         sum_ref[...] = jnp.zeros_like(sum_ref)
@@ -652,40 +688,37 @@
             sum_ref[target : target + count] = source[place : place + count]
         load_pieces(me_ref[0], pieces, w_ref, sems, False)
 
-    rows = 256
     gain = vec(small_ref, "g1")
-    sum_n = jnp.zeros((1, width), F32)
-    sum_e = jnp.zeros((1, width), F32)
-    for at in range(0, length, rows):
-        rs = slice(at, at + rows)
-        whole_g = jnp.concatenate([g[0, :, rs] for g in grads], axis=0)
-        e = dot_tt(whole_g, w_ref[...])
-        n, r = norm_parts(x_ref[rs].astype(F32))
-        eg = e * gain
-        part = r * (
-            eg - jnp.mean(eg, axis=-1, keepdims=True) - n * jnp.mean(eg * n, axis=-1, keepdims=True)
-        )
-        sum_n += jnp.sum(e * n, axis=0, keepdims=True)
-        sum_e += jnp.sum(e, axis=0, keepdims=True)
-        ring_put(ring, at, gh_ref[rs] + part)
-    sum_ref[0:1] += sum_n
-    sum_ref[1:2] += sum_e
-    gx_ref[...] = ring_get(ring, length - shift, length)
+    e = dot_tt(jnp.concatenate([g[0] for g in grads], axis=0), w_ref[...])
+    n, r = norm_parts(x_ref[...].astype(F32))
+    eg = e * gain
+    part = r * (
+        eg - jnp.mean(eg, axis=-1, keepdims=True) - n * jnp.mean(eg * n, axis=-1, keepdims=True)
+    )
+    sum_ref[0:1] += jnp.sum(e * n, axis=0, keepdims=True)
+    sum_ref[1:2] += jnp.sum(e, axis=0, keepdims=True)
+    ring_put(ring, pl.multiple_of(step * rows, rows), gh_ref[...] + part)
+
+    @pl.when(step == pl.num_programs(1) - 1)
+    def _():
+        gx_ref[...] = ring_get(ring, length - shift_ref[seq], length)
 
 
 def first_back_call(me, shift, grads, x, gh, small, pieces, smalls, deps):
     tokens, width = x.shape
     nseq, _, length = grads[0].shape
-    row = pl.BlockSpec((length, width), lambda s: (s, 0))
+    steps = 4
+    rows = length // steps
+    row = pl.BlockSpec((rows, width), lambda s, i: (s * steps + i, 0))
     return pl.pallas_call(
         lambda *refs: first_back_kernel(len(grads), len(deps), *refs),
-        grid=(nseq,),
+        grid=(nseq, steps),
         in_specs=[
             SMEM, SMEM, row, row, whole(small.shape),
-            *(turned_spec(g) for g in grads), *(whole(v.shape) for v in smalls),
+            *(pl.BlockSpec((1, g.shape[1], rows), lambda s, i: (s, 0, i)) for g in grads), *(whole(v.shape) for v in smalls),
             *(ANY for _ in (*pieces, *deps)),
         ],
-        out_specs=[row, whole((24, width))],
+        out_specs=[pl.BlockSpec((length, width), lambda s, i: (s, 0)), whole((24, width))],
         out_shape=[
             jax.ShapeDtypeStruct((tokens, width), F32),
             jax.ShapeDtypeStruct((24, width), F32),
@@ -863,6 +896,12 @@
 
 
 def step_parts(kind, chain):
+    if kind == "small":
+
+        def body(idx, ins, outs):
+            outs[0][...] = ins[0][...] + ins[1][...]
+
+        return [(v, whole(v.shape)) for v in (chain["sum"], chain["got"])], [(*chain["sum"].shape, F32)], body
     keep, near = chain["keep"], chain["near"]
     chips, sides, groups, n, lanes = keep.shape
     half = (groups, n, lanes)
@@ -905,30 +944,29 @@
                 outs[0][idx[2] ^ k] = ref[...]
 
         return ins, [half], body
-    ins = [*at(lambda idx: idx[1]), (chain["yr"], whole(half))]
     if kind == "z":
 
         def body(idx, ins, outs):
-            for k, out in enumerate(outs):
-                out[...] = total(ins, idx[2] ^ (k + 1)).astype(BF)
-
-        return ins, [(n, lanes)] * (groups - 1), body
-    count = len(ins)
-    ins += [(v, whole(v.shape)) for v in chain["zr"]]
+            for k in range(groups):
+                outs[k][...] = total(ins, idx[2] ^ k).astype(outs[k].dtype)
+
+        return [*at(lambda idx: idx[1]), (chain["yr"], whole(half))], [(n, lanes, F32), *[(n, lanes)] * (groups - 1)], body
 
     def body(idx, ins, outs):
-        out = total(ins[:count], idx[2])
-        for ref in ins[count:]:
+        out = ins[0][...]
+        for ref in ins[1:]:
             out = out + ref[...].astype(F32)
         outs[0][...] = out.astype(BF)
 
-    return ins, [(n, lanes)], body
+    return [(v, whole(v.shape)) for v in (chain["mine"], *chain["zr"])], [(n, lanes)], body
 
 
 def step_call(idx, steps, deps):
     plans = [step_parts(kind, chain) for kind, chain in steps]
     ins = [pair for plan in plans for pair in plan[0]]
     outs = [shape for plan in plans for shape in plan[1]]
+    types = [F32 if shape[-1] == F32 else BF for shape in outs]
+    outs = [shape[:-1] if shape[-1] == F32 else shape for shape in outs]
 
     def kernel(idx_ref, *refs):
         at, out_at = 0, len(ins) + len(deps)
@@ -945,29 +983,46 @@
             in_specs=[*(spec for _, spec in ins), *(ANY for _ in deps)],
             out_specs=[whole(shape) for shape in outs],
         ),
-        out_shape=[jax.ShapeDtypeStruct(shape, BF) for shape in outs],
+        out_shape=[jax.ShapeDtypeStruct(shape, dtype) for shape, dtype in zip(outs, types)],
         compiler_params=params(62),
         cost_estimate=cost(3),
         name="_".join(["step", *(kind for kind, _ in steps)]),
     )(idx, *(v for v, _ in ins), *deps)
     at = 0
+    others = range(1, lax.axis_size("rep") // 2)
     for (kind, chain), (_, shapes, _) in zip(steps, plans):
         sends = results[at : at + len(shapes)]
         at += len(shapes)
-        far = [swap(v, "shard" if kind == "x" else "rep", 2 * (k + 1)) for k, v in enumerate(sends)] if kind in "xz" else None
         if kind == "x":
-            chain["far"] = far
-        elif kind == "z":
-            chain["zr"] = far
+            chain["far"] = [swap(v, "shard", 2 * (k + 1)) for k, v in enumerate(sends)]
         elif kind == "y":
             chain["yr"] = swap(sends[0], "rep", 1)
+        elif kind == "z":
+            chain["mine"] = sends[0]
+            chain["zr"] = [swap(sends[k], "rep", 2 * k) for k in others]
+        elif kind == "sum":
+            chain["done"] = sends[0]
+            chain["zg"] = [swap(sends[0], "rep", 2 * k) for k in others]
         elif kind == "half":
             chain["half"] = sends[0]
             chain["twin"] = swap(sends[0], "rep", 1)
         else:
-            chain["done"] = sends[0]
-            chain["zg"] = [swap(sends[0], "rep", 2 * k) for k in range(1, lax.axis_size("rep") // 2)]
+            small_next(chain, sends[0])
     return results[0]
+
+
+def small_next(chain, sums):
+    chain["sum"] = sums
+    count = chain["steps"] = chain.get("steps", -1) + 1
+    bits = [("shard", 1 << b) for b in range(lax.axis_size("shard").bit_length() - 1)] + [("rep", 1)]
+    if count < len(bits):
+        chain["got"] = swap(sums, *bits[count])
+    else:
+        chain["got"] = [swap(sums, "rep", 2 * k) for k in range(1, lax.axis_size("rep") // 2)]
+
+
+def small_end(chain, group):
+    return total_of(in_order([chain["sum"], *chain["got"]], group))
 
 
 def finish_call(idx, chains, plans, shapes, deps):
@@ -1063,16 +1118,21 @@
         pieces = [out_weight, *shared(up_weight), down_weight[: shares[0]], down_weight[shares[0] :]]
     else:
         pieces = split_call(members, shares, out_weight, up_weight, down_weight, [act, *wqkv])
-    wo, wu0, wu1 = [lax.all_gather(v, "shard", axis=0, tiled=True) for v in pieces[:3]]
+    wo = lax.all_gather(pieces[0], "shard", axis=0, tiled=True)
     wd0 = far_pieces(pieces[3])
 
     wqkv = near_pieces([qkv_weight, *gate(wqkv[1:], [act])], wqkv_near)
-    q, k, v = qkv_call(me_ref, act, small, cos, sin, wqkv)
-    wd0 = near_pieces(gate(wd0, [q]))
-    o, lse = attend_call(seg, q, k, v)
-    wd1 = far_pieces(*gate(pieces[4:], [lse]))
+    qkv = qkv_call(me_ref, act, small, cos, sin, wqkv)
+    *wd0, wu0 = gate([*wd0, pieces[1]], [qkv])
+    wd0 = near_pieces(wd0)
+    wu0, wu0_near = far_pieces(wu0), swap(wu0, "shard", 1)
+    o, lse = attend_call(seg, qkv)
+    wd0[1::2], (*wu0, wu1, wd1) = gate(wd0[1::2], [lse]), gate([*wu0, pieces[2], pieces[4]], [lse])
+    wu0 = near_pieces(wu0, wu0_near)
+    wu1 = lax.all_gather(wu1, "shard", axis=0, tiled=True)
+    wd1 = far_pieces(wd1)
     values = {"me": me_ref, "mix": mix_weights, "small": small, "x": xr, "cot": cr, "a": o, "wo": wo}
-    got = mlp_call(0, shares[0], True, False, values | {"wu_in": wu0, "wd": wd0}, form, members, [])
+    got = mlp_call(0, shares[0], True, False, values | {"wu": wu0, "wd": wd0}, form, members, [])
     values |= {"up_in": got["up"], "back_in": got["back"], "hid": got["hid"], "act": got["act"]}
     wd1 = near_pieces(gate(wd1, [got["dbu"]]))
     first, dbu = [got[name] for name in ("dw0", "dw1") if name in got], [got["dbu"]]
@@ -1084,14 +1144,14 @@
     else:
         earlier_grad, deps = spread_call(*spread, []), []
     got = mlp_call(
-        shares[0], shares[1], False, True, values | {"wu_in": wu1, "wd": wd1}, form, members, deps
+        shares[0], shares[1], False, True, values | {"wu": [wu1], "wd": wd1}, form, members, deps
     )
     second = [got[name] for name in ("dw0", "dw1") if name in got]
     dbu.append(got["dbu"])
     block_out, gh, ga, sums2 = (got[name] for name in ("up", "gh", "ga", "sum"))
 
     groups = width // PAIR // 2
-    back = [seg, q, k, v, o, ga, lse, cos, sin]
+    back = [seg, qkv, o, ga, lse, cos, sin]
 
     def up_place(base, share):
         def place(row, col):
@@ -1118,9 +1178,12 @@
         output = mix_call(shift, mix_weights, part, block_out, [t])
         t = step_call(idx, [("x", tail)], [output])
         input_grad, sums = first_back_call(me_ref, shift, grads, xr, gh, small, wqkv, smalls, [t])
+        (early["twin"],) = gate([early["twin"]], [sums])
+        sums_chain = {}
+        small_next(sums_chain, sums)
         t = step_call(idx, [("sum", late), ("y", tail)], [sums])
-        t = step_call(idx, [("half", late), ("z", tail)], [])
-        t = step_call(idx, [("sum", tail)], [])
+        t = step_call(idx, [("half", late), ("z", tail), ("small", sums_chain)], [])
+        t = step_call(idx, [("sum", tail), ("small", sums_chain)], [])
         d_up, d_down, d_out = finish_call(
             idx,
             [early, late],
@@ -1138,7 +1201,8 @@
             [(own, ff), (deep, width), (own, width)],
             [t],
         )
-        t = step_call(idx, [("half", tail)], [d_out])
+        t = step_call(idx, [("half", tail), ("small", sums_chain)], [d_out])
+        flat = small_end(sums_chain, rep // 2).reshape(-1)
         (d_qkv,) = finish_call(
             idx, [tail], [[(0, own, 3 * width, lambda row, col: (row, col))]], [(own, 3 * width)], []
         )
@@ -1160,9 +1224,9 @@
         d_up = jnp.concatenate(ups, axis=2).reshape(own, -1).astype(F32)
         d_down = jnp.concatenate(downs, axis=0).astype(F32)
         d_qkv = unpack(third, 0, own, 3 * width).astype(F32)
+        flat = reduce_small(sums).reshape(-1)
 
     parts, at = [], 0
-    flat = reduce_small(sums).reshape(-1)
     for size in sizes:
         parts.append(lax.dynamic_slice(flat, (at + me * size,), (size,)))
         at += size * members

time: 445 us -> 438 us (0.984)
  Pallas kernels: 310 us -> 284 us
  waiting for transfers between devices: 36.6 us -> 54.6 us
    ppermute x47 -> x51, waiting for transfers between devices: 35.8 us -> 54.5 us  [swap(): return lax.ppermute(v, axis, [(i, i ^ bits) for i in range(size)])]
    pallas_call x1, Pallas kernels: 30.6 us -> 17.3 us  [attend_call(): pl.pallas_call(attend_kernel, grid=(nseq, pairs), in_specs=[pl.BlockSpec(...]
    pallas_call x3, Pallas kernels: 43.8 us -> 33.3 us  [attend_back_call(): pl.pallas_call(attend_back_kernel, grid=(nseq, pairs), in_specs=[pl.Block...]
    unnamed x56 -> x74, local copies, waits for them, and re-layouts: 12.5 us -> 15.2 us
    ppermute x47 -> x51, starting transfers between devices: 52.4 us -> 50.4 us  [swap(): return lax.ppermute(v, axis, [(i, i ^ bits) for i in range(size)])]
  transfers between devices with their start and end apart: 50 -> 53, of which waited for: 12 -> 17; matrix products, arithmetic and copies ran while one was open for 1% -> 1% of each run, Pallas kernels for 67% -> 62%
where the time goes in v3:
time: 438 us; the launch traced here: 430 us
  Pallas kernels  284 us (65%)
  waiting for transfers between devices  54.6 us (12%)
  starting transfers between devices  50.4 us (12%)
  local copies, waits for them, and re-layouts  23.2 us (5%)
  between operations  14.9 us (3%)
    pallas_call x2, Pallas kernels, mlp_call(): pl.pallas_call(lambda *refs: mlp_kernel(base, first, last, names, members...  101 us
    ppermute x51, waiting for transfers between devices, swap(): return lax.ppermute(v, axis, [(i, i ^ bits) for i in range(size)])  54.5 us
    ppermute x51, starting transfers between devices, swap(): return lax.ppermute(v, axis, [(i, i ^ bits) for i in range(size)])  50.4 us
    pallas_call x11, Pallas kernels, step_call(): pl.pallas_call(kernel, grid_spec=pltpu.PrefetchScalarGridSpec(num_scalar_...  36.9 us
    pallas_call x3, Pallas kernels, attend_back_call(): pl.pallas_call(attend_back_kernel, grid=(nseq, pairs), in_specs=[pl.Block...  33.3 us
    pallas_call x1, Pallas kernels, first_back_call(): pl.pallas_call(lambda *refs: first_back_kernel(len(grads), len(deps), *re...  19.5 us
    pallas_call x1, Pallas kernels, attend_call(): pl.pallas_call(attend_kernel, grid=(nseq, pairs), in_specs=[pl.BlockSpec(...  17.3 us
    unnamed x74, local copies, waits for them, and re-layouts  15.2 us
  transfers between devices with their start and end apart: 53, of which 17 were waited for; matrix products, arithmetic and copies ran while one was open for 1% of the time, Pallas kernels for 62%

profile of v3, /device:TPU:0, one launch (start us, length us, event | category | flops | bytes accessed | tf_op | source)
XLA Modules:
  0.0 429.7 jit_solution(18219606029897061617)
XLA Ops:
  12.7 2.4 collective-permute-start.2
  15.8 1.7 collective-permute-start.4
  17.5 10.8 %states.1 = (f32[2048,768]{1,0:T(8,128)}, f32[8,768]{1,0:T(8,128)}) custom-call(f32[5]{0:T(128)} %mix_ref.5, bf16[4,2048,768]{2,1,0:T(8,128)(2,1)} %e_ref.1, bf16[2048,768]{1,0:T(8,128)(2,1)} %c_ref.3), custom_call_target="tpu_custom_call" | custom-call | flops 18975000576 | bytes 1024 | tf_op jit(solution)/shard_map/states/pallas_call | solution.py:757
  29.6 9.6 %roll.1 = (s32[2]{0:T(128)}, bf16[2048,768]{1,0:T(8,128)(2,1)}, bf16[2048,768]{1,0:T(8,128)(2,1)}, bf16[2048,768]{1,0:T(8,128)(2,1)}, f32[2,8,512]{2,1,0:T(8,128...) custom-call(bf16[2048,768]{1,0:T(8,128)(2,1)} %x_ref.1, bf16[2048,768]{1,0:T(8,128)(2,1)} %c_ref.3, ...), custom_call_target="tpu_custom_call" | custom-call | flops 17250000896 | bytes 1024 | tf_op jit(solution)/shard_map/roll/pallas_call | solution.py:185
  40.1 3.3 split.1
  45.0 1.3 collective-permute-done.5.refs_3_.refs_24_
  46.3 14.4 %qkv.1.q_ref.k_ref.v_ref.refs_3_ = bf16[2,3,768,1024]{3,2,1,0:T(8,128)(2,1)} custom-call(s32[1]{0:T(128)} %bitcast.4.me_ref.refs_0_, bf16[2048,768]{1,0:T(8,128)(2,1)} %get-tuple-element.107.refs_1_.act_ref.refs_3_, bf16[4,8,768]{2,1,0:T(8,128)(2,1)} %pad_maximum_fusion.2.small_ref.refs_3_.refs_4_, f32[2,32,1024]{2,1,0:T(8,128)} %get-tuple-element.108.cos_ref, ...), custom_call_target="tpu_custom_call" | custom-call | flops 25874999296 | bytes 1024 | tf_op jit(solution)/shard_map/qkv/pallas_call | solution.py:249
  60.7 10.1 %collective-permute-done.6.refs_1_ = bf16[512,768]{1,0:T(8,128)(2,1)S(1)} collective-permute-done((bf16[512,768]{1,0:T(8,128)(2,1)S(1)}, bf16[512,768]{1,0:T(8,128)(2,1)S(1)}, u32[]{:S(2)}, u32[]{:S(2)}) %collective-permute-start.6) | collective-permute-done | bytes 786464 | tf_op jit(solution)/shard_map/ppermute | solution.py:850
  72.0 17.3 %attend.1 = (bf16[2,768,1024]{2,1,0:T(8,128)(2,1)}, f32[2,6,2,1024]{3,2,1,0:T(2,128)}) custom-call(f32[2,8,512]{2,1,0:T(8,128)} %get-tuple-element.106.seg_ref, bf16[2,3,768,1024]{3,2,1,0:T(8,128)(2,1)} %qkv.1.q_ref.k_ref.v_ref.refs_3_, bf16[2,3,768,1024]{3,2,1,0:T(8,128)(2,1)} %qkv.1.q_ref.k_ref.v_ref.refs_3_, ...), custom_call_target="tpu_custom_call" | custom-call | flops 51749998592 | bytes 1024 | tf_op jit(solution)/shard_map/attend/pallas_call | solution.py:340
  89.8 2.1 collective-permute-done.7.refs_1_
  94.6 59.0 %mlp.2 = (bf16[2,2,4,768,128]{4,3,2,1,0:T(8,128)(2,1)}, bf16[2,2,4,768,128]{4,3,2,1,0:T(8,128)(2,1)}, f32[1,2048]{1,0:T(1,128)}, f32[2048,768]{1,0:T(8,128)}, f3...) custom-call(s32[1]{0:T(128)} %bitcast.4.me_ref.refs_0_, f32[5]{0:T(128)} %mix_ref.5, ...), custom_call_target="tpu_custom_call" | custom-call | flops 77624999936 | bytes 1024 | tf_op jit(solution)/shard_map/mlp/pallas_call | solution.py:605
  155.0 10.4 %spread.1.refs_2_ = f32[4,2048,768]{2,1,0:T(8,128)} custom-call(f32[5]{0:T(128)} %mix_ref.5, bf16[2048,768]{1,0:T(8,128)(2,1)} %c_ref.3, bf16[2,2,4,768,128]{4,3,2,1,0:T(8,128)(2,1)} %get-tuple-element.133.refs_0_), custom_call_target="tpu_custom_call" | custom-call | flops 34500001792 | bytes 1024 | tf_op jit(solution)/shard_map/spread/pallas_call | solution.py:782
  165.4 4.0 step_x.2.refs_15_
  169.4 1.5 collective-permute-start.16
  171.6 42.4 %mlp.3 = (bf16[2,2,4,528,128]{4,3,2,1,0:T(8,128)(2,1)}, bf16[2,2,4,528,128]{4,3,2,1,0:T(8,128)(2,1)}, f32[1,1024]{1,0:T(1,128)}, f32[2048,768]{1,0:T(8,128)}, f3...) custom-call(s32[1]{0:T(128)} %bitcast.4.me_ref.refs_0_, f32[5]{0:T(128)} %mix_ref.5, ...), custom_call_target="tpu_custom_call" | custom-call | flops 77624999936 | bytes 1024 | tf_op jit(solution)/shard_map/mlp/pallas_call | solution.py:605
  215.3 3.4 step_y.2.refs_0_
  218.7 1.5 collective-permute-start.17
  220.3 11.2 %attend_back.3 = (bf16[2,256,1024]{2,1,0:T(8,128)(2,1)}, bf16[2,256,1024]{2,1,0:T(8,128)(2,1)}, bf16[2,256,1024]{2,1,0:T(8,128)(2,1)}, f32[2,3,8,256]{3,2,1,0:T(8,128)}) custom-call(f32[2,8,512]{2,1,0:T(8,128)} %get-tuple-element.106.seg_ref, bf16[2,3,768,1024]{3,2,1,0:T(8,128)(2,1)} %qkv.1.q_ref.k_ref.v_ref.refs_3_, ...), custom_call_target="tpu_custom_call" | custom-call | flops 25874999296 | bytes 1024 | tf_op jit(solution)/shard_map/attend_back/pallas_call | solution.py:437
  231.5 7.4 %collective-permute-done.17.refs_3_ = bf16[4,768,128]{2,1,0:T(8,128)(2,1)S(1)} collective-permute-done((bf16[4,768,128]{2,1,0:T(8,128)(2,1)}, bf16[4,768,128]{2,1,0:T(8,128)(2,1)S(1)}, u32[]{:S(2)}, u32[]{:S(2)}) %collective-permute-start.17) | collective-permute-done | bytes 786464 | tf_op jit(solution)/shard_map/ppermute | solution.py:850
  239.8 4.8 %step_z_x.1 = (f32[768,128]{1,0:T(8,128)}, bf16[768,128]{1,0:T(8,128)(2,1)}, bf16[768,128]{1,0:T(8,128)(2,1)}, bf16[768,128]{1,0:T(8,128)(2,1)}, bf16[2,4,528,128]{3,2,1,0:T(8,128)(2,1)}) custom-call(s32[3]{0:T(128)} %pad_add_fusion.idx_ref, bf16[2,2,4,768,128]{4,3,2,1,0:T(8,128)(2,1)} %get-tuple-element.133.refs_0_, ...), custom_call_target="tpu_custom_call" | custom-call | flops 5175000064 | bytes 1024 | tf_op jit(solution)/shard_map/step_z_x/pallas_call | solution.py:978
  244.5 1.6 collective-permute-start.19
  246.1 2.6 collective-permute-start.20
  249.5 11.1 %attend_back.4 = (bf16[2,256,1024]{2,1,0:T(8,128)(2,1)}, bf16[2,256,1024]{2,1,0:T(8,128)(2,1)}, bf16[2,256,1024]{2,1,0:T(8,128)(2,1)}, f32[2,3,8,256]{3,2,1,0:T(8,128)}) custom-call(f32[2,8,512]{2,1,0:T(8,128)} %get-tuple-element.106.seg_ref, bf16[2,3,768,1024]{3,2,1,0:T(8,128)(2,1)} %qkv.1.q_ref.k_ref.v_ref.refs_3_, ...), custom_call_target="tpu_custom_call" | custom-call | flops 25874999296 | bytes 1024 | tf_op jit(solution)/shard_map/attend_back/pallas_call | solution.py:437
  260.6 2.9 collective-permute-done.20.refs_2_
  264.2 2.6 step_sum.1.refs_0_
  266.9 3.1 collective-permute-start.22
  271.0 1.5 collective-permute-start.24
  272.5 11.0 %attend_back.5 = (bf16[2,256,1024]{2,1,0:T(8,128)(2,1)}, bf16[2,256,1024]{2,1,0:T(8,128)(2,1)}, bf16[2,256,1024]{2,1,0:T(8,128)(2,1)}, f32[2,3,8,256]{3,2,1,0:T(8,128)}) custom-call(f32[2,8,512]{2,1,0:T(8,128)} %get-tuple-element.106.seg_ref, bf16[2,3,768,1024]{3,2,1,0:T(8,128)(2,1)} %qkv.1.q_ref.k_ref.v_ref.refs_3_, ...), custom_call_target="tpu_custom_call" | custom-call | flops 862499968 | bytes 1024 | tf_op jit(solution)/shard_map/attend_back/pallas_call | solution.py:437
  283.6 3.2 collective-permute-done.23.refs_1_
  288.5 3.0 step_y.3.refs_11_
  291.5 1.5 collective-permute-start.26
  293.1 12.9 %qkv_grad.1 = (bf16[2,2,4,432,128]{4,3,2,1,0:T(8,128)(2,1)}, bf16[2,2,4,432,128]{4,3,2,1,0:T(8,128)(2,1)}) custom-call(s32[1]{0:T(128)} %bitcast.4.me_ref.refs_0_, bf16[2048,768]{1,0:T(8,128)(2,1)} %get-tuple-element.107.refs_1_.act_ref.refs_3_, bf16[2,256,1024]{2,1,0:T(8,128)(2,1)} %get-tuple-element.139.refs_6_.refs_2_.refs_5_, ...), custom_call_target="tpu_custom_call" | custom-call | flops 22424999936 | bytes 1024 | tf_op jit(solution)/shard_map/qkv_grad/pallas_call | solution.py:645
  306.1 3.8 step_half_z.1
  309.9 2.6 collective-permute-start.28
  313.5 1.4 collective-permute-start.30
  314.9 7.1 %mix.1.refs_2_ = bf16[2048,768]{1,0:T(8,128)(2,1)} custom-call(s32[2]{0:T(128)} %get-tuple-element.102.shift_ref.refs_1_, f32[5]{0:T(128)} %mix_ref.5, f32[2048,768]{1,0:T(8,128)} %get-tuple-element.103.part_ref, f32[2048,768]{1,0:T(8,128)} %get-tuple-element.135.b_ref, bf16[4,768,128]{2,1,0:T(8,128)(2,1)} %get-tuple-element.157.refs_0_), custom_call_target="tpu_custom_call" | custom-call | flops 34500001792 | bytes 1024 | tf_op jit(solution)/shard_map/mix/pallas_call | solution.py:835
  322.0 1.2 copy-done.6
  323.2 3.2 step_x.3.refs_25_
  326.9 19.5 %first_back.1 = (f32[2048,768]{1,0:T(8,128)}, f32[24,768]{1,0:T(8,128)}) custom-call(s32[1]{0:T(128)} %bitcast.4.me_ref.refs_0_, s32[2]{0:T(128)} %get-tuple-element.102.shift_ref.refs_1_, bf16[2048,768]{1,0:T(8,128)(2,1)} %get-tuple-element.105.refs_4_.refs_2_, f32[2048,768]{1,0:T(8,128)} %get-tuple-element.158.refs_3_, ...), custom_call_target="tpu_custom_call" | custom-call | flops 34500001792 | bytes 1024 | tf_op jit(solution)/shard_map/first_back/pallas_call | solution.py:713
  346.5 1.6 collective-permute-done.31.refs_6_
  349.0 3.3 step_sum_y.1
  352.8 1.5 collective-permute-start.45
  355.1 2.2 collective-permute-start.33
  357.3 1.4 collective-permute-start.34
  358.8 4.3 collective-permute-done.32.refs_1_
  363.0 5.5 %collective-permute-done.33.refs_2_ = bf16[528,128]{1,0:T(8,128)(2,1)S(1)} collective-permute-done((bf16[528,128]{1,0:T(8,128)(2,1)}, bf16[528,128]{1,0:T(8,128)(2,1)S(1)}, u32[]{:S(2)}, u32[]{:S(2)}) %collective-permute-start.33) | collective-permute-done | bytes 135200 | tf_op jit(solution)/shard_map/ppermute | solution.py:850
  369.2 3.4 step_half_z_small.1
  372.5 2.2 collective-permute-start.37
  375.8 1.4 collective-permute-start.39
  377.7 2.8 collective-permute-done.45.refs_0_
  381.8 4.1 collective-permute-done.38.refs_2_
  386.6 2.6 step_sum_small.1
  389.2 1.7 collective-permute-start.41
  391.8 1.8 collective-permute-start.43
  394.9 4.4 %finish.2 = (f32[192,3072]{1,0:T(8,128)}, f32[768,768]{1,0:T(8,128)}, f32[192,768]{1,0:T(8,128)}) custom-call(s32[3]{0:T(128)} %pad_add_fusion.idx_ref, bf16[4,768,128]{2,1,0:T(8,128)(2,1)} %get-tuple-element.157.refs_0_, bf16[4,768,128]{2,1,0:T(8,128)(2,1)} %gate.13.refs_1_, bf16[4,528,128]{2,1,0:T(8,128)(2,1)} %get-tuple-element.180.refs_2_, ...), custom_call_target="tpu_custom_call" | custom-call | flops 6899999744 | bytes 1024 | tf_op jit(solution)/shard_map/finish/pallas_call | solution.py:1051
  399.3 2.3 collective-permute-done.42.refs_2_
  402.3 2.7 step_half_small.1
  405.0 2.0 collective-permute-start.49
  406.9 1.2 collective-permute-start.48
  408.1 1.2 collective-permute-start.47
  409.9 2.3 collective-permute-done.49
  412.2 1.7 collective-permute-done.48
  417.4 1.7 collective-permute-done.50.refs_1_
  419.9 2.5 finish.3
  (180 shorter events, 38.4 us)
Async XLA Ops:
  7.2 86.6 %all-gather.3.cloned.1.call-start = ((), (), s32[]{:S(2)}) async-start(), calls=%async_computation | async-start | bytes 1474560 | tf_op jit(solution)/shard_map/all_gather | solution.py:1121
  12.7 15.6 %copy-start.5 = (s32[2,1024]{1,0:T(2,128)S(1)}, s32[2,1024]{1,0:T(2,128)}, u32[]{:S(2)}) copy-start(s32[2,1024]{1,0:T(2,128)} %param.20) | copy-start | bytes 24580
  12.7 16.2 %collective-permute-start.2 = (bf16[8,768]{1,0:T(8,128)(2,1)S(1)}, bf16[8,768]{1,0:T(8,128)(2,1)S(1)}, u32[]{:S(2)}, u32[]{:S(2)}) collective-permute-start(bf16[8,768]{1,0:T(8,128)(2,1)S(1)} %stack.84), channel_id=1, source_target_pairs={{0,3},{1,2},{2,1},{3,0},{4,7},{5,6},{6,5},{7,4},{8,11},{9,10},{10,... | collective-permute-start | bytes 36872 | tf_op jit(solution)/shard_map/ppermute | solution.py:850
  15.1 13.8 %collective-permute-start.1 = (bf16[8,768]{1,0:T(8,128)(2,1)S(1)}, bf16[8,768]{1,0:T(8,128)(2,1)S(1)}, u32[]{:S(2)}, u32[]{:S(2)}) collective-permute-start(bf16[8,768]{1,0:T(8,128)(2,1)S(1)} %stack.84), channel_id=1, source_target_pairs={{0,2},{1,3},{2,0},{3,1},{4,6},{5,7},{6,4},{7,5},{8,10},{9,11},{10,... | collective-permute-start | bytes 36872 | tf_op jit(solution)/shard_map/ppermute | solution.py:850
  15.8 13.2 %collective-permute-start = (bf16[8,768]{1,0:T(8,128)(2,1)S(1)}, bf16[8,768]{1,0:T(8,128)(2,1)S(1)}, u32[]{:S(2)}, u32[]{:S(2)}) collective-permute-start(bf16[8,768]{1,0:T(8,128)(2,1)S(1)} %stack.84), channel_id=1, source_target_pairs={{0,1},{1,0},{2,3},{3,2},{4,5},{5,4},{6,7},{7,6},{8,9},{9,8},{10,11... | collective-permute-start | bytes 36872 | tf_op jit(solution)/shard_map/ppermute | solution.py:850
  15.8 23.4 %collective-permute-start.4 = (bf16[192,2304]{1,0:T(8,128)(2,1)}, bf16[192,2304]{1,0:T(8,128)(2,1)S(1)}, u32[]{:S(2)}, u32[]{:S(2)}) collective-permute-start(bf16[192,2304]{1,0:T(8,128)(2,1)} %refs_21_.1), channel_id=1, source_target_pairs={{0,2},{1,3},{2,0},{3,1},{4,6},{5,7},{6,4},{7,5},{8,10},{9,11},{10,... | collective-permute-start | bytes 2654216 | tf_op jit(solution)/shard_map/ppermute | solution.py:850
  17.5 27.4 %collective-permute-start.3 = (bf16[192,2304]{1,0:T(8,128)(2,1)}, bf16[192,2304]{1,0:T(8,128)(2,1)}, u32[]{:S(2)}, u32[]{:S(2)}) collective-permute-start(bf16[192,2304]{1,0:T(8,128)(2,1)} %refs_21_.1), channel_id=1, source_target_pairs={{0,1},{1,0},{2,3},{3,2},{4,5},{5,4},{6,7},{7,6},{8,9},{9,8},{10,11... | collective-permute-start | bytes 2654216 | tf_op jit(solution)/shard_map/ppermute | solution.py:850
  43.4 2.9 collective-permute-start.5
  43.9 127.0 %all-gather.5.cloned.1.call-start = ((), (), s32[]{:S(2)}) async-start(), calls=%async_computation.1 | async-start | bytes 1966080 | tf_op jit(solution)/shard_map/all_gather | solution.py:1132
  44.5 26.3 %collective-permute-start.6 = (bf16[512,768]{1,0:T(8,128)(2,1)S(1)}, bf16[512,768]{1,0:T(8,128)(2,1)S(1)}, u32[]{:S(2)}, u32[]{:S(2)}) collective-permute-start(bf16[512,768]{1,0:T(8,128)(2,1)S(1)} %copy-done.1), channel_id=1, source_target_pairs={{0,2},{1,3},{2,0},{3,1},{4,6},{5,7},{6,4},{7,5},{8,10},{9,11},{10,... | collective-permute-start | bytes 2359304 | tf_op jit(solution)/shard_map/ppermute | solution.py:850
  71.7 18.2 %collective-permute-start.8 = (bf16[192,2048]{1,0:T(8,128)(2,1)}, bf16[192,2048]{1,0:T(8,128)(2,1)}, u32[]{:S(2)}, u32[]{:S(2)}) collective-permute-start(bf16[192,2048]{1,0:T(8,128)(2,1)} %get-tuple-element.114.refs_0_), channel_id=1, source_target_pairs={{0,1},{1,0},{2,3},{3,2},{4,5},{5,4},{6,7},{7,6},{8,9},{9,8},{10,11... | collective-permute-start | bytes 2359304 | tf_op jit(solution)/shard_map/ppermute | solution.py:850
  71.7 20.3 %collective-permute-start.7 = (bf16[192,2048]{1,0:T(8,128)(2,1)}, bf16[192,2048]{1,0:T(8,128)(2,1)}, u32[]{:S(2)}, u32[]{:S(2)}) collective-permute-start(bf16[192,2048]{1,0:T(8,128)(2,1)} %get-tuple-element.114.refs_0_), channel_id=1, source_target_pairs={{0,2},{1,3},{2,0},{3,1},{4,6},{5,7},{6,4},{7,5},{8,10},{9,11},{10,... | collective-permute-start | bytes 2359304 | tf_op jit(solution)/shard_map/ppermute | solution.py:850
  72.0 17.3 %copy-start.2 = (bf16[512,768]{1,0:T(8,128)(2,1)S(1)}, bf16[512,768]{1,0:T(8,128)(2,1)}, u32[]{:S(2)}) copy-start(bf16[512,768]{1,0:T(8,128)(2,1)} %get-tuple-element.120.refs_11_) | copy-start | bytes 2359300
  72.0 17.6 %copy-start.4 = (bf16[512,768]{1,0:T(8,128)(2,1)S(1)}, bf16[512,768]{1,0:T(8,128)(2,1)}, u32[]{:S(2)}) copy-start(bf16[512,768]{1,0:T(8,128)(2,1)} %get-tuple-element.121.refs_13_) | copy-start | bytes 2359300
  89.3 3.6 collective-permute-start.10
  89.6 3.4 collective-permute-start.11
  91.9 2.6 collective-permute-start.9
  92.6 61.0 %collective-permute-start.12 = (bf16[256,768]{1,0:T(8,128)(2,1)}, bf16[256,768]{1,0:T(8,128)(2,1)S(1)}, u32[]{:S(2)}, u32[]{:S(2)}) collective-permute-start(bf16[256,768]{1,0:T(8,128)(2,1)} %get-tuple-element.129.refs_0_), channel_id=1, source_target_pairs={{0,2},{1,3},{2,0},{3,1},{4,6},{5,7},{6,4},{7,5},{8,10},{9,11},{10,... | collective-permute-start | bytes 1179656 | tf_op jit(solution)/shard_map/ppermute | solution.py:850
  154.3 16.6 %collective-permute-start.13 = (bf16[256,768]{1,0:T(8,128)(2,1)}, bf16[256,768]{1,0:T(8,128)(2,1)S(1)}, u32[]{:S(2)}, u32[]{:S(2)}) collective-permute-start(bf16[256,768]{1,0:T(8,128)(2,1)} %get-tuple-element.131.refs_11_), channel_id=1, source_target_pairs={{0,1},{1,0},{2,3},{3,2},{4,5},{5,4},{6,7},{7,6},{8,9},{9,8},{10,11... | collective-permute-start | bytes 1179656 | tf_op jit(solution)/shard_map/ppermute | solution.py:850
  154.4 16.5 %collective-permute-start.14 = (bf16[256,768]{1,0:T(8,128)(2,1)}, bf16[256,768]{1,0:T(8,128)(2,1)}, u32[]{:S(2)}, u32[]{:S(2)}) collective-permute-start(bf16[256,768]{1,0:T(8,128)(2,1)} %get-tuple-element.132.refs_13_), channel_id=1, source_target_pairs={{0,1},{1,0},{2,3},{3,2},{4,5},{5,4},{6,7},{7,6},{8,9},{9,8},{10,11... | collective-permute-start | bytes 1179656 | tf_op jit(solution)/shard_map/ppermute | solution.py:850
  154.8 10.5 %collective-permute-start.15 = (bf16[2,2,4,768,128]{4,3,2,1,0:T(8,128)(2,1)}, bf16[2,2,4,768,128]{4,3,2,1,0:T(8,128)(2,1)}, u32[]{:S(2)}, u32[]{:S(2)}) collective-permute-start(bf16[2,2,4,768,128]{4,3,2,1,0:T(8,128)(2,1)} %get-tuple-element.134), channel_id=1, source_target_pairs={{0,1},{1,0},{2,3},{3,2},{4,5},{5,4},{6,7},{7,6},{8,9},{9,8},{10,11... | collective-permute-start | bytes 9437192 | tf_op jit(solution)/shard_map/ppermute | solution.py:850
  169.4 44.8 %collective-permute-start.16 = (bf16[2,4,768,128]{3,2,1,0:T(8,128)(2,1)}, bf16[2,4,768,128]{3,2,1,0:T(8,128)(2,1)S(1)}, u32[]{:S(2)}, u32[]{:S(2)}) collective-permute-start(bf16[2,4,768,128]{3,2,1,0:T(8,128)(2,1)} %step_x.2.refs_15_), channel_id=1, source_target_pairs={{0,2},{1,3},{2,0},{3,1},{4,6},{5,7},{6,4},{7,5},{8,10},{9,11},{10,... | collective-permute-start | bytes 4718600 | tf_op jit(solution)/shard_map/ppermute | solution.py:850
  214.1 17.4 %collective-permute-start.18 = (bf16[2,2,4,528,128]{4,3,2,1,0:T(8,128)(2,1)}, bf16[2,2,4,528,128]{4,3,2,1,0:T(8,128)(2,1)}, u32[]{:S(2)}, u32[]{:S(2)}) collective-permute-start(bf16[2,2,4,528,128]{4,3,2,1,0:T(8,128)(2,1)} %get-tuple-element.137), channel_id=1, source_target_pairs={{0,1},{1,0},{2,3},{3,2},{4,5},{5,4},{6,7},{7,6},{8,9},{9,8},{10,11... | collective-permute-start | bytes 6488072 | tf_op jit(solution)/shard_map/ppermute | solution.py:850
  218.7 20.1 %collective-permute-start.17 = (bf16[4,768,128]{2,1,0:T(8,128)(2,1)}, bf16[4,768,128]{2,1,0:T(8,128)(2,1)S(1)}, u32[]{:S(2)}, u32[]{:S(2)}) collective-permute-start(bf16[4,768,128]{2,1,0:T(8,128)(2,1)} %step_y.2.refs_0_), channel_id=1, source_target_pairs={{0,4},{4,0},{8,12},{12,8},{16,20},{20,16},{24,28},{28,24},{1,5},{5... | collective-permute-start | bytes 2359304 | tf_op jit(solution)/shard_map/ppermute | solution.py:850
  244.5 16.0 %collective-permute-start.19 = (bf16[768,128]{1,0:T(8,128)(2,1)}, bf16[768,128]{1,0:T(8,128)(2,1)S(1)}, u32[]{:S(2)}, u32[]{:S(2)}) collective-permute-start(bf16[768,128]{1,0:T(8,128)(2,1)} %get-tuple-element.141), channel_id=1, source_target_pairs={{0,8},{4,12},{8,0},{12,4},{16,24},{20,28},{24,16},{28,20},{1,9},{5... | collective-permute-start | bytes 589832 | tf_op jit(solution)/shard_map/ppermute | solution.py:850
  246.1 17.4 %collective-permute-start.20 = (bf16[768,128]{1,0:T(8,128)(2,1)}, bf16[768,128]{1,0:T(8,128)(2,1)S(1)}, u32[]{:S(2)}, u32[]{:S(2)}) collective-permute-start(bf16[768,128]{1,0:T(8,128)(2,1)} %get-tuple-element.142), channel_id=1, source_target_pairs={{0,16},{4,20},{8,24},{12,28},{16,0},{20,4},{24,8},{28,12},{1,17},{... | collective-permute-start | bytes 589832 | tf_op jit(solution)/shard_map/ppermute | solution.py:850
  248.7 14.8 %collective-permute-start.21 = (bf16[768,128]{1,0:T(8,128)(2,1)}, bf16[768,128]{1,0:T(8,128)(2,1)S(1)}, u32[]{:S(2)}, u32[]{:S(2)}) collective-permute-start(bf16[768,128]{1,0:T(8,128)(2,1)} %get-tuple-element.143), channel_id=1, source_target_pairs={{0,24},{4,28},{8,16},{12,20},{16,8},{20,12},{24,0},{28,4},{1,25},{... | collective-permute-start | bytes 589832 | tf_op jit(solution)/shard_map/ppermute | solution.py:850
  248.9 38.6 %collective-permute-start.25 = (bf16[2,4,528,128]{3,2,1,0:T(8,128)(2,1)}, bf16[2,4,528,128]{3,2,1,0:T(8,128)(2,1)S(1)}, u32[]{:S(2)}, u32[]{:S(2)}) collective-permute-start(bf16[2,4,528,128]{3,2,1,0:T(8,128)(2,1)} %get-tuple-element.149), channel_id=1, source_target_pairs={{0,2},{1,3},{2,0},{3,1},{4,6},{5,7},{6,4},{7,5},{8,10},{9,11},{10,... | collective-permute-start | bytes 3244040 | tf_op jit(solution)/shard_map/ppermute | solution.py:850
  260.6 2.9 copy-start.19
  266.9 16.7 %collective-permute-start.22 = (bf16[768,128]{1,0:T(8,128)(2,1)}, bf16[768,128]{1,0:T(8,128)(2,1)S(1)}, u32[]{:S(2)}, u32[]{:S(2)}) collective-permute-start(bf16[768,128]{1,0:T(8,128)(2,1)} %step_sum.1.refs_0_), channel_id=1, source_target_pairs={{0,8},{4,12},{8,0},{12,4},{16,24},{20,28},{24,16},{28,20},{1,9},{5... | collective-permute-start | bytes 589832 | tf_op jit(solution)/shard_map/ppermute | solution.py:850
  270.0 16.8 %collective-permute-start.23 = (bf16[768,128]{1,0:T(8,128)(2,1)}, bf16[768,128]{1,0:T(8,128)(2,1)S(1)}, u32[]{:S(2)}, u32[]{:S(2)}) collective-permute-start(bf16[768,128]{1,0:T(8,128)(2,1)} %step_sum.1.refs_0_), channel_id=1, source_target_pairs={{0,16},{4,20},{8,24},{12,28},{16,0},{20,4},{24,8},{28,12},{1,17},{... | collective-permute-start | bytes 589832 | tf_op jit(solution)/shard_map/ppermute | solution.py:850
  271.0 15.7 %collective-permute-start.24 = (bf16[768,128]{1,0:T(8,128)(2,1)}, bf16[768,128]{1,0:T(8,128)(2,1)S(1)}, u32[]{:S(2)}, u32[]{:S(2)}) collective-permute-start(bf16[768,128]{1,0:T(8,128)(2,1)} %step_sum.1.refs_0_), channel_id=1, source_target_pairs={{0,24},{4,28},{8,16},{12,20},{16,8},{20,12},{24,0},{28,4},{1,25},{... | collective-permute-start | bytes 589832 | tf_op jit(solution)/shard_map/ppermute | solution.py:850
  283.5 3.2 copy-start.18
  291.5 14.5 %collective-permute-start.26 = (bf16[4,528,128]{2,1,0:T(8,128)(2,1)}, bf16[4,528,128]{2,1,0:T(8,128)(2,1)}, u32[]{:S(2)}, u32[]{:S(2)}) collective-permute-start(bf16[4,528,128]{2,1,0:T(8,128)(2,1)} %step_y.3.refs_11_), channel_id=1, source_target_pairs={{0,4},{4,0},{8,12},{12,8},{16,20},{20,16},{24,28},{28,24},{1,5},{5... | collective-permute-start | bytes 1622024 | tf_op jit(solution)/shard_map/ppermute | solution.py:850
  306.0 16.0 %collective-permute-start.27 = (bf16[2,2,4,432,128]{4,3,2,1,0:T(8,128)(2,1)}, bf16[2,2,4,432,128]{4,3,2,1,0:T(8,128)(2,1)S(1)}, u32[]{:S(2)}, u32[]{:S(2)}) collective-permute-start(bf16[2,2,4,432,128]{4,3,2,1,0:T(8,128)(2,1)} %get-tuple-element.164), channel_id=1, source_target_pairs={{0,1},{1,0},{2,3},{3,2},{4,5},{5,4},{6,7},{7,6},{8,9},{9,8},{10,11... | collective-permute-start | bytes 5308424 | tf_op jit(solution)/shard_map/ppermute | solution.py:850
  309.9 36.5 %collective-permute-start.28 = (bf16[528,128]{1,0:T(8,128)(2,1)}, bf16[528,128]{1,0:T(8,128)(2,1)S(1)}, u32[]{:S(2)}, u32[]{:S(2)}) collective-permute-start(bf16[528,128]{1,0:T(8,128)(2,1)} %get-tuple-element.167), channel_id=1, source_target_pairs={{0,8},{4,12},{8,0},{12,4},{16,24},{20,28},{24,16},{28,20},{1,9},{5... | collective-permute-start | bytes 405512 | tf_op jit(solution)/shard_map/ppermute | solution.py:850
  312.5 34.0 %collective-permute-start.29 = (bf16[528,128]{1,0:T(8,128)(2,1)}, bf16[528,128]{1,0:T(8,128)(2,1)}, u32[]{:S(2)}, u32[]{:S(2)}) collective-permute-start(bf16[528,128]{1,0:T(8,128)(2,1)} %get-tuple-element.168), channel_id=1, source_target_pairs={{0,16},{4,20},{8,24},{12,28},{16,0},{20,4},{24,8},{28,12},{1,17},{... | collective-permute-start | bytes 405512 | tf_op jit(solution)/shard_map/ppermute | solution.py:850
  313.5 32.9 %collective-permute-start.30 = (bf16[528,128]{1,0:T(8,128)(2,1)}, bf16[528,128]{1,0:T(8,128)(2,1)}, u32[]{:S(2)}, u32[]{:S(2)}) collective-permute-start(bf16[528,128]{1,0:T(8,128)(2,1)} %get-tuple-element.169), channel_id=1, source_target_pairs={{0,24},{4,28},{8,16},{12,20},{16,8},{20,12},{24,0},{28,4},{1,25},{... | collective-permute-start | bytes 405512 | tf_op jit(solution)/shard_map/ppermute | solution.py:850
  326.4 21.7 %collective-permute-start.31 = (bf16[2,4,432,128]{3,2,1,0:T(8,128)(2,1)}, bf16[2,4,432,128]{3,2,1,0:T(8,128)(2,1)S(1)}, u32[]{:S(2)}, u32[]{:S(2)}) collective-permute-start(bf16[2,4,432,128]{3,2,1,0:T(8,128)(2,1)} %step_x.3.refs_25_), channel_id=1, source_target_pairs={{0,2},{1,3},{2,0},{3,1},{4,6},{5,7},{6,4},{7,5},{8,10},{9,11},{10,... | collective-permute-start | bytes 2654216 | tf_op jit(solution)/shard_map/ppermute | solution.py:850
  349.0 3.8 copy-start.10
  349.0 5.3 %copy-start.33 = (f32[24,768]{1,0:T(8,128)S(1)}, f32[24,768]{1,0:T(8,128)}, u32[]{:S(2)}) copy-start(f32[24,768]{1,0:T(8,128)} %get-tuple-element.170.refs_7_.refs_8_.refs_1_) | copy-start | bytes 221188
  352.3 16.2 %collective-permute-start.35 = (bf16[4,432,128]{2,1,0:T(8,128)(2,1)}, bf16[4,432,128]{2,1,0:T(8,128)(2,1)}, u32[]{:S(2)}, u32[]{:S(2)}) collective-permute-start(bf16[4,432,128]{2,1,0:T(8,128)(2,1)} %get-tuple-element.172), channel_id=1, source_target_pairs={{0,4},{4,0},{8,12},{12,8},{16,20},{20,16},{24,28},{28,24},{1,5},{5... | collective-permute-start | bytes 1327112 | tf_op jit(solution)/shard_map/ppermute | solution.py:850
  352.8 27.7 %collective-permute-start.45 = (bf16[4,768,128]{2,1,0:T(8,128)(2,1)S(1)}, bf16[4,768,128]{2,1,0:T(8,128)(2,1)S(1)}, u32[]{:S(2)}, u32[]{:S(2)}) collective-permute-start(bf16[4,768,128]{2,1,0:T(8,128)(2,1)S(1)} %copy-done.10), channel_id=1, source_target_pairs={{0,4},{4,0},{8,12},{12,8},{16,20},{20,16},{24,28},{28,24},{1,5},{5... | collective-permute-start | bytes 2359304 | tf_op jit(solution)/shard_map/ppermute | solution.py:850
  354.4 3.0 collective-permute-start.36
  354.4 8.7 %collective-permute-start.32 = (bf16[528,128]{1,0:T(8,128)(2,1)}, bf16[528,128]{1,0:T(8,128)(2,1)S(1)}, u32[]{:S(2)}, u32[]{:S(2)}) collective-permute-start(bf16[528,128]{1,0:T(8,128)(2,1)} %get-tuple-element.171.refs_0_), channel_id=1, source_target_pairs={{0,8},{4,12},{8,0},{12,4},{16,24},{20,28},{24,16},{28,20},{1,9},{5... | collective-permute-start | bytes 405512 | tf_op jit(solution)/shard_map/ppermute | solution.py:850
  355.1 13.4 %collective-permute-start.33 = (bf16[528,128]{1,0:T(8,128)(2,1)}, bf16[528,128]{1,0:T(8,128)(2,1)S(1)}, u32[]{:S(2)}, u32[]{:S(2)}) collective-permute-start(bf16[528,128]{1,0:T(8,128)(2,1)} %get-tuple-element.171.refs_0_), channel_id=1, source_target_pairs={{0,16},{4,20},{8,24},{12,28},{16,0},{20,4},{24,8},{28,12},{1,17},{... | collective-permute-start | bytes 405512 | tf_op jit(solution)/shard_map/ppermute | solution.py:850
  357.3 11.2 %copy-start.34 = (f32[24,768]{1,0:T(8,128)}, f32[24,768]{1,0:T(8,128)S(1)}, u32[]{:S(2)}) copy-start(f32[24,768]{1,0:T(8,128)S(1)} %collective-permute-done.36.refs_9_) | copy-start | bytes 221188
  357.3 11.2 %collective-permute-start.34 = (bf16[528,128]{1,0:T(8,128)(2,1)}, bf16[528,128]{1,0:T(8,128)(2,1)}, u32[]{:S(2)}, u32[]{:S(2)}) collective-permute-start(bf16[528,128]{1,0:T(8,128)(2,1)} %get-tuple-element.171.refs_0_), channel_id=1, source_target_pairs={{0,24},{4,28},{8,16},{12,20},{16,8},{20,12},{24,0},{28,4},{1,25},{... | collective-permute-start | bytes 405512 | tf_op jit(solution)/shard_map/ppermute | solution.py:850
  363.0 5.5 %copy-start.25 = (bf16[528,128]{1,0:T(8,128)(2,1)}, bf16[528,128]{1,0:T(8,128)(2,1)S(1)}, u32[]{:S(2)}) copy-start(bf16[528,128]{1,0:T(8,128)(2,1)S(1)} %collective-permute-done.32.refs_1_) | copy-start | bytes 405508
  372.5 9.3 %collective-permute-start.37 = (bf16[432,128]{1,0:T(8,128)(2,1)}, bf16[432,128]{1,0:T(8,128)(2,1)S(1)}, u32[]{:S(2)}, u32[]{:S(2)}) collective-permute-start(bf16[432,128]{1,0:T(8,128)(2,1)} %get-tuple-element.174), channel_id=1, source_target_pairs={{0,8},{4,12},{8,0},{12,4},{16,24},{20,28},{24,16},{28,20},{1,9},{5... | collective-permute-start | bytes 331784 | tf_op jit(solution)/shard_map/ppermute | solution.py:850
  374.8 11.1 %collective-permute-start.38 = (bf16[432,128]{1,0:T(8,128)(2,1)}, bf16[432,128]{1,0:T(8,128)(2,1)S(1)}, u32[]{:S(2)}, u32[]{:S(2)}) collective-permute-start(bf16[432,128]{1,0:T(8,128)(2,1)} %get-tuple-element.175), channel_id=1, source_target_pairs={{0,16},{4,20},{8,24},{12,28},{16,0},{20,4},{24,8},{28,12},{1,17},{... | collective-permute-start | bytes 331784 | tf_op jit(solution)/shard_map/ppermute | solution.py:850
  375.8 10.1 %collective-permute-start.39 = (bf16[432,128]{1,0:T(8,128)(2,1)}, bf16[432,128]{1,0:T(8,128)(2,1)S(1)}, u32[]{:S(2)}, u32[]{:S(2)}) collective-permute-start(bf16[432,128]{1,0:T(8,128)(2,1)} %get-tuple-element.176), channel_id=1, source_target_pairs={{0,24},{4,28},{8,16},{12,20},{16,8},{20,12},{24,0},{28,4},{1,25},{... | collective-permute-start | bytes 331784 | tf_op jit(solution)/shard_map/ppermute | solution.py:850
  377.2 4.6 %collective-permute-start.40 = (f32[24,768]{1,0:T(8,128)}, f32[24,768]{1,0:T(8,128)S(1)}, u32[]{:S(2)}, u32[]{:S(2)}) collective-permute-start(f32[24,768]{1,0:T(8,128)} %get-tuple-element.177.refs_4_), channel_id=1, source_target_pairs={{0,2},{1,3},{2,0},{3,1},{4,6},{5,7},{6,4},{7,5},{8,10},{9,11},{10,... | collective-permute-start | bytes 221192 | tf_op jit(solution)/shard_map/ppermute | solution.py:850
  380.5 13.5 %collective-permute-start.46 = (bf16[4,528,128]{2,1,0:T(8,128)(2,1)}, bf16[4,528,128]{2,1,0:T(8,128)(2,1)S(1)}, u32[]{:S(2)}, u32[]{:S(2)}) collective-permute-start(bf16[4,528,128]{2,1,0:T(8,128)(2,1)} %get-tuple-element.180.refs_2_), channel_id=1, source_target_pairs={{0,4},{4,0},{8,12},{12,8},{16,20},{20,16},{24,28},{28,24},{1,5},{5... | collective-permute-start | bytes 1622024 | tf_op jit(solution)/shard_map/ppermute | solution.py:850
  381.8 4.1 copy-start.35
  381.8 4.2 copy-start.27
  389.2 10.1 %collective-permute-start.41 = (bf16[432,128]{1,0:T(8,128)(2,1)}, bf16[432,128]{1,0:T(8,128)(2,1)S(1)}, u32[]{:S(2)}, u32[]{:S(2)}) collective-permute-start(bf16[432,128]{1,0:T(8,128)(2,1)} %get-tuple-element.178.refs_4_.refs_0_), channel_id=1, source_target_pairs={{0,8},{4,12},{8,0},{12,4},{16,24},{20,28},{24,16},{28,20},{1,9},{5... | collective-permute-start | bytes 331784 | tf_op jit(solution)/shard_map/ppermute | solution.py:850
  390.9 10.7 %collective-permute-start.42 = (bf16[432,128]{1,0:T(8,128)(2,1)}, bf16[432,128]{1,0:T(8,128)(2,1)S(1)}, u32[]{:S(2)}, u32[]{:S(2)}) collective-permute-start(bf16[432,128]{1,0:T(8,128)(2,1)} %get-tuple-element.178.refs_4_.refs_0_), channel_id=1, source_target_pairs={{0,16},{4,20},{8,24},{12,28},{16,0},{20,4},{24,8},{28,12},{1,17},{... | collective-permute-start | bytes 331784 | tf_op jit(solution)/shard_map/ppermute | solution.py:850
  391.8 9.8 %collective-permute-start.43 = (bf16[432,128]{1,0:T(8,128)(2,1)}, bf16[432,128]{1,0:T(8,128)(2,1)S(1)}, u32[]{:S(2)}, u32[]{:S(2)}) collective-permute-start(bf16[432,128]{1,0:T(8,128)(2,1)} %get-tuple-element.178.refs_4_.refs_0_), channel_id=1, source_target_pairs={{0,24},{4,28},{8,16},{12,20},{16,8},{20,12},{24,0},{28,4},{1,25},{... | collective-permute-start | bytes 331784 | tf_op jit(solution)/shard_map/ppermute | solution.py:850
  393.6 5.7 %collective-permute-start.44 = (f32[24,768]{1,0:T(8,128)}, f32[24,768]{1,0:T(8,128)S(1)}, u32[]{:S(2)}, u32[]{:S(2)}) collective-permute-start(f32[24,768]{1,0:T(8,128)} %get-tuple-element.179.refs_4_), channel_id=1, source_target_pairs={{0,4},{4,0},{8,12},{12,8},{16,20},{20,16},{24,28},{28,24},{1,5},{5... | collective-permute-start | bytes 221192 | tf_op jit(solution)/shard_map/ppermute | solution.py:850
  405.0 7.2 %collective-permute-start.49 = (f32[24,768]{1,0:T(8,128)}, f32[24,768]{1,0:T(8,128)S(1)}, u32[]{:S(2)}, u32[]{:S(2)}) collective-permute-start(f32[24,768]{1,0:T(8,128)} %get-tuple-element.182), channel_id=1, source_target_pairs={{0,24},{4,28},{8,16},{12,20},{16,8},{20,12},{24,0},{28,4},{1,25},{... | collective-permute-start | bytes 221192 | tf_op jit(solution)/shard_map/ppermute | solution.py:850
  406.9 6.9 %collective-permute-start.48 = (f32[24,768]{1,0:T(8,128)}, f32[24,768]{1,0:T(8,128)S(1)}, u32[]{:S(2)}, u32[]{:S(2)}) collective-permute-start(f32[24,768]{1,0:T(8,128)} %get-tuple-element.182), channel_id=1, source_target_pairs={{0,16},{4,20},{8,24},{12,28},{16,0},{20,4},{24,8},{28,12},{1,17},{... | collective-permute-start | bytes 221192 | tf_op jit(solution)/shard_map/ppermute | solution.py:850
  408.1 5.7 %collective-permute-start.47 = (f32[24,768]{1,0:T(8,128)}, f32[24,768]{1,0:T(8,128)S(1)}, u32[]{:S(2)}, u32[]{:S(2)}) collective-permute-start(f32[24,768]{1,0:T(8,128)} %get-tuple-element.182), channel_id=1, source_target_pairs={{0,8},{4,12},{8,0},{12,4},{16,24},{20,28},{24,16},{28,20},{1,9},{5... | collective-permute-start | bytes 221192 | tf_op jit(solution)/shard_map/ppermute | solution.py:850
  409.4 9.8 %collective-permute-start.50 = (bf16[4,432,128]{2,1,0:T(8,128)(2,1)}, bf16[4,432,128]{2,1,0:T(8,128)(2,1)S(1)}, u32[]{:S(2)}, u32[]{:S(2)}) collective-permute-start(bf16[4,432,128]{2,1,0:T(8,128)(2,1)} %get-tuple-element.183.refs_0_), channel_id=1, source_target_pairs={{0,4},{4,0},{8,12},{12,8},{16,20},{20,16},{24,28},{28,24},{1,5},{5... | collective-permute-start | bytes 1327112 | tf_op jit(solution)/shard_map/ppermute | solution.py:850
  (26 other events, 25.4 us)
Sparse Core Ops, SparseCore 0:
  44.0 24.1 all-gather.2
  93.0 21.1 all-gather.4
